TPU v7x, 32 devices: a whole 2x2x4 slice. The times are simulated.
32 devices in a mesh: dp: 2 (over y), seq: 16 (over z, x, core).
Axes of the slice: x: 2, y: 2, z: 4, core: 2. Of those that a mesh axis runs over, the one named last changes fastest.
Arguments:
- tokens: bfloat16 [2, 2, 1024, 1024], P(None, 'dp', 'seq'), may hold values from -6 to 6
- cotangent: bfloat16 [2, 2, 1024, 1024], P(None, 'dp', 'seq'), may hold values from -6 to 6
- w_query: bfloat16 [1024, 2048], replicated, may hold values from -0.1875 to 0.1875
- w_key: bfloat16 [1024, 1024], replicated, may hold values from -0.1875 to 0.1875
- w_value: bfloat16 [1024, 1024], replicated, may hold values from -0.1875 to 0.1875
- w_out: bfloat16 [2048, 1024], replicated, may hold values from -0.125 to 0.125
- q_gain: float32 [2048], replicated, may hold values from 0.25 to 1.75
- k_gain: float32 [1024], replicated, may hold values from 0.25 to 1.75
- attn_gain: float32 [1024], replicated, may hold values from 0.25 to 1.75
- w_gate: bfloat16 [1024, 3072], replicated, may hold values from -0.1875 to 0.1875
- w_up: bfloat16 [1024, 3072], replicated, may hold values from -0.1875 to 0.1875
- w_down: bfloat16 [3072, 1024], replicated, may hold values from -0.109375 to 0.109375
- mlp_gain: float32 [1024], replicated, may hold values from 0.25 to 1.75
- doc_lengths: int32 [2, 2, 2], P(None, 'dp'), may hold values from 0 to 1024, as said below
- block_order: int32 [16], replicated, may hold values from 0 to 15, each once
Outputs:
- layer_out: bfloat16 [2, 2, 1024, 1024], P(None, 'dp', 'seq')
- input_grad: float32 [2, 2, 1024, 1024], P(None, 'dp', 'seq')
- grad_w_query: float32 [1024, 2048], P(('dp', 'seq'))
- grad_w_key: float32 [1024, 1024], P(('dp', 'seq'))
- grad_w_value: float32 [1024, 1024], P(('dp', 'seq'))
- grad_w_out: float32 [2048, 1024], P(('dp', 'seq'))
- grad_q_gain: float32 [2048], P(('dp', 'seq'))
- grad_k_gain: float32 [1024], P(('dp', 'seq'))
- grad_attn_gain: float32 [1024], P(('dp', 'seq'))
- grad_w_gate: float32 [1024, 3072], P(('dp', 'seq'))
- grad_w_up: float32 [1024, 3072], P(('dp', 'seq'))
- grad_w_down: float32 [3072, 1024], P(('dp', 'seq'))
- grad_mlp_gain: float32 [1024], P(('dp', 'seq'))
Inputs may be any that keep to these rules, and one draw needn't show every extreme that they name: Row r of micro-batch b holds two documents in order: positions 0 to doc_lengths[b, r, 0] - 1 and the rest; the two lengths sum to 1024. For every r exactly one micro-batch holds a single document of 1024 positions (second length 0); in the others the first length lies between 256 and 768. Layout positions j * 64 to (j + 1) * 64 - 1 of every row hold the positions block_order[j] * 64 onward, in order; each block appears once.
All inputs are finite; a program needn't handle non-finite values.
Results may differ from a plain program's by a relative error of at most 0.015.
Values may be sent and summed in bfloat16 or wider, within the bound.
A program may use at most 256 MiB of HBM per device.

v0:
```python
import jax
import jax.numpy as jnp
from jax import lax
from jax.sharding import PartitionSpec as P

HD = 128


EPSILON = 1e-06
ROPE_BASE = 500000.0
MASK_FILL = -1e30


def rms_forward(inputs, gain_vec):
    factor = lax.rsqrt(jnp.mean(inputs * inputs, axis=-1, keepdims=True) + EPSILON)
    normal = inputs * factor
    return (normal * gain_vec, normal, factor)


def rms_backward(grad_in, gain_vec, normal, factor):
    weighted = grad_in * gain_vec
    gain_grad = jnp.sum(grad_in * normal, axis=0)
    inner_mean = jnp.mean(weighted * normal, axis=-1, keepdims=True)
    return (factor * (weighted - normal * inner_mean), gain_grad)


def rope_tables(rot_places, head_size):
    frequency = jnp.power(ROPE_BASE, -jnp.arange(0, head_size, 2).astype(jnp.float32) / head_size)
    angles = rot_places.astype(jnp.float32)[:, None] * frequency[None, :]
    return (jnp.cos(angles), jnp.sin(angles))


def rotate(inputs, cos_table, sine_table, head_count, direction):
    row_count = inputs.shape[0]
    halves = inputs.reshape(row_count, head_count, 2, -1)
    first_half = halves[:, :, 0]
    second = halves[:, :, 1]
    cos_part = cos_table[:, None, :]
    sine_part = sine_table[:, None, :] * direction
    turned = jnp.stack(
        [first_half * cos_part - second * sine_part, second * cos_part + first_half * sine_part],
        axis=2,
    )
    return turned.reshape(row_count, -1)


def product(left, right):
    return jnp.dot(left, right, preferred_element_type=jnp.float32)


def weight_grad(left, right):
    return lax.dot_general(
        left, right, (((0,), (0,)), ((), ())), preferred_element_type=jnp.float32
    )


def back_product(left, right):
    return lax.dot_general(
        left, right, (((1,), (1,)), ((), ())), preferred_element_type=jnp.float32
    )


def heads_first(rows, group_count, head_size):
    shaped = rows.reshape(rows.shape[0], group_count, -1, head_size)
    return jnp.moveaxis(shaped, 1, 0)


def kv_first(rows, group_count, head_size):
    return jnp.moveaxis(rows.reshape(rows.shape[0], group_count, head_size), 1, 0)


def score_block(q_group, k_group, mask_rows, score_scale):
    raw_scores = (
        jnp.einsum("trd,ud->rtu", q_group, k_group, preferred_element_type=jnp.float32)
        * score_scale
    )
    return jnp.where(mask_rows[None], raw_scores, MASK_FILL)


def attend(pieces, score_scale, group_count, head_size):
    q_rows, key_rows, value_rows, mask_rows = pieces

    def attend_one_group(parts):
        q_group, k_group, v_group = parts
        masked = score_block(q_group, k_group, mask_rows, score_scale)
        row_max = jnp.max(masked, axis=-1)
        exp_terms = jnp.exp(masked - row_max[..., None])
        row_sum = jnp.sum(exp_terms, axis=-1)
        attn_prob = (exp_terms / row_sum[..., None]).astype(jnp.bfloat16)
        attended = jnp.einsum("rtu,ud->trd", attn_prob, v_group, preferred_element_type=jnp.float32)
        return (attended, row_max, row_sum)

    attended, row_max, row_sum = lax.map(
        attend_one_group,
        (
            heads_first(q_rows, group_count, head_size),
            kv_first(key_rows, group_count, head_size),
            kv_first(value_rows, group_count, head_size),
        ),
    )
    attended = jnp.moveaxis(attended, 0, 1)
    return (attended.reshape(q_rows.shape[0], -1), row_max, row_sum)


def score_grads(
    q_group, grad_group, k_group, v_group, mask_rows, row_max, row_sum, row_dot, score_scale
):
    masked = score_block(q_group, k_group, mask_rows, score_scale)
    attn_prob = jnp.exp(masked - row_max[..., None]) / row_sum[..., None]
    prob_grad = jnp.einsum("trd,ud->rtu", grad_group, v_group, preferred_element_type=jnp.float32)
    row_dot = jnp.sum(attn_prob * prob_grad, axis=-1)
    score_grad = (attn_prob * (prob_grad - row_dot[..., None])).astype(jnp.bfloat16)
    return (attn_prob.astype(jnp.bfloat16), score_grad, row_dot)


def on_device(
    tokens,
    cotangent,
    w_query,
    w_key,
    w_value,
    w_out,
    q_gain,
    k_gain,
    attn_gain,
    w_gate,
    w_up,
    w_down,
    mlp_gain,
    doc_lengths,
    block_order,
):
    micro_count = tokens.shape[0]
    block_len = tokens.shape[2]
    model_width = tokens.shape[3]
    seq_length = lax.axis_size("seq") * block_len
    head_count = w_query.shape[1] // HD
    group_count = w_key.shape[1] // HD
    score_scale = HD ** (-0.5)
    flat_tokens = tokens.reshape(micro_count * block_len, model_width)
    out_grad = cotangent.reshape(micro_count * block_len, model_width).astype(jnp.float32)
    first_lengths = doc_lengths[:, 0, 0]
    offsets = jnp.arange(block_len, dtype=jnp.int32)
    own_places = block_order[lax.axis_index("seq")] * block_len + offsets
    key_places = (block_order[:, None] * block_len + offsets[None, :]).reshape(seq_length)
    own_segments = (own_places[None, :] >= first_lengths[:, None]).astype(jnp.int32)
    all_segments = (key_places[None, :] >= first_lengths[:, None]).astype(jnp.int32)
    rot_places = (own_places[None, :] - own_segments * first_lengths[:, None]).reshape(-1)
    allowed = (own_segments[:, :, None] == all_segments[:, None, :]) & (
        key_places[None, None, :] <= own_places[None, :, None]
    )
    cos_table, sine_table = rope_tables(rot_places, HD)
    q_pre = product(flat_tokens, w_query)
    k_pre = product(flat_tokens, w_key)
    v_pre = product(flat_tokens, w_value)
    q_norm, q_hat, q_factor = rms_forward(q_pre, q_gain)
    k_norm, k_hat, k_factor = rms_forward(k_pre, k_gain)
    q_low = rotate(q_norm, cos_table, sine_table, head_count, 1.0).astype(jnp.bfloat16)
    k_low = rotate(k_norm, cos_table, sine_table, group_count, 1.0).astype(jnp.bfloat16)
    v_low = v_pre.astype(jnp.bfloat16)
    q_blocks = q_low.reshape(micro_count, block_len, -1)
    k_blocks = k_low.reshape(micro_count, block_len, -1)
    v_blocks = v_low.reshape(micro_count, block_len, -1)
    key_all, value_all = (
        lax.all_gather(k_blocks, "seq", axis=1, tiled=True),
        lax.all_gather(v_blocks, "seq", axis=1, tiled=True),
    )

    def forward_block(pieces):
        return attend(pieces, score_scale, group_count, HD)

    attended, row_max, row_sum = lax.map(forward_block, (q_blocks, key_all, value_all, allowed))
    att_low = attended.reshape(micro_count * block_len, -1).astype(jnp.bfloat16)
    attn_proj = product(att_low, w_out)
    attn_normed, attn_hat, attn_factor = rms_forward(attn_proj, attn_gain)
    hidden = flat_tokens.astype(jnp.float32) + attn_normed
    hidden_low = hidden.astype(jnp.bfloat16)
    gate_pre = product(hidden_low, w_gate)
    up_pre = product(hidden_low, w_up)
    mixed_low = (jax.nn.silu(gate_pre) * up_pre).astype(jnp.bfloat16)
    down_pre = product(mixed_low, w_down)
    down_normed, down_hat, down_factor = rms_forward(down_pre, mlp_gain)
    layer_out = (hidden + down_normed).astype(jnp.bfloat16).reshape(tokens.shape)
    down_grad, grad_mlp_gain = rms_backward(out_grad, mlp_gain, down_hat, down_factor)
    down_grad = down_grad.astype(jnp.bfloat16)
    grad_w_down = weight_grad(mixed_low, down_grad)
    mixed_grad = back_product(down_grad, w_down)
    sigmoid_gate = jax.nn.sigmoid(gate_pre)
    gate_grad = (
        mixed_grad * up_pre * sigmoid_gate * (1.0 + gate_pre * (1.0 - sigmoid_gate))
    ).astype(jnp.bfloat16)
    up_grad = (mixed_grad * gate_pre * sigmoid_gate).astype(jnp.bfloat16)
    grad_w_gate = weight_grad(hidden_low, gate_grad)
    grad_w_up = weight_grad(hidden_low, up_grad)
    hidden_grad = out_grad + back_product(gate_grad, w_gate) + back_product(up_grad, w_up)
    proj_grad, grad_attn_gain = rms_backward(hidden_grad, attn_gain, attn_hat, attn_factor)
    proj_grad = proj_grad.astype(jnp.bfloat16)
    grad_w_out = weight_grad(att_low, proj_grad)
    att_grad = back_product(proj_grad, w_out).astype(jnp.bfloat16)
    grad_blocks = att_grad.reshape(micro_count, block_len, -1)
    key_back, value_back = (key_all, value_all)

    def query_pass(pieces):
        q_rows, grad_rows, key_rows, value_rows, mask_rows, max_rows, sum_rows = pieces

        def query_one_group(parts):
            q_group, grad_group, k_group, v_group, max_group, sum_group = parts
            prob_low, score_grad, unused = score_grads(
                q_group,
                grad_group,
                k_group,
                v_group,
                mask_rows,
                max_group,
                sum_group,
                None,
                score_scale,
            )
            q_grad = (
                jnp.einsum("rtu,ud->trd", score_grad, k_group, preferred_element_type=jnp.float32)
                * score_scale
            )
            key_terms = (
                jnp.einsum("rtu,trd->ud", score_grad, q_group, preferred_element_type=jnp.float32)
                * score_scale
            )
            value_terms = jnp.einsum(
                "rtu,trd->ud", prob_low, grad_group, preferred_element_type=jnp.float32
            )
            return (q_grad, key_terms, value_terms)

        q_grad, key_terms, value_terms = lax.map(
            query_one_group,
            (
                heads_first(q_rows, group_count, HD),
                heads_first(grad_rows, group_count, HD),
                kv_first(key_rows, group_count, HD),
                kv_first(value_rows, group_count, HD),
                max_rows,
                sum_rows,
            ),
        )
        q_grad = jnp.moveaxis(q_grad, 0, 1).reshape(block_len, -1)
        key_terms = jnp.moveaxis(key_terms, 0, 1).reshape(seq_length, -1)
        value_terms = jnp.moveaxis(value_terms, 0, 1).reshape(seq_length, -1)
        key_own, value_own = (
            lax.psum_scatter(key_terms, "seq", scatter_dimension=0, tiled=True),
            lax.psum_scatter(value_terms, "seq", scatter_dimension=0, tiled=True),
        )
        return (q_grad, key_own, value_own)

    q_rot_grad, k_rot_grad, value_grad = lax.map(
        query_pass, (q_blocks, grad_blocks, key_back, value_back, allowed, row_max, row_sum)
    )
    q_rot_grad = q_rot_grad.reshape(micro_count * block_len, -1)
    k_rot_grad = k_rot_grad.reshape(micro_count * block_len, -1)
    v_grad = value_grad.reshape(micro_count * block_len, -1).astype(jnp.bfloat16)
    q_norm_grad = rotate(q_rot_grad, cos_table, sine_table, head_count, -1.0)
    k_norm_grad = rotate(k_rot_grad, cos_table, sine_table, group_count, -1.0)
    q_grad, grad_q_gain = rms_backward(q_norm_grad, q_gain, q_hat, q_factor)
    k_grad, grad_k_gain = rms_backward(k_norm_grad, k_gain, k_hat, k_factor)
    q_grad = q_grad.astype(jnp.bfloat16)
    k_grad = k_grad.astype(jnp.bfloat16)
    grad_w_query = weight_grad(flat_tokens, q_grad)
    grad_w_key = weight_grad(flat_tokens, k_grad)
    grad_w_value = weight_grad(flat_tokens, v_grad)
    input_grad = (
        hidden_grad
        + back_product(q_grad, w_query)
        + back_product(k_grad, w_key)
        + back_product(v_grad, w_value)
    )
    input_grad = input_grad.reshape(tokens.shape)
    summed = (
        lax.psum_scatter(grad_w_query, ("dp", "seq"), scatter_dimension=0, tiled=True),
        lax.psum_scatter(grad_w_key, ("dp", "seq"), scatter_dimension=0, tiled=True),
        lax.psum_scatter(grad_w_value, ("dp", "seq"), scatter_dimension=0, tiled=True),
        lax.psum_scatter(grad_w_out, ("dp", "seq"), scatter_dimension=0, tiled=True),
        lax.psum_scatter(grad_q_gain, ("dp", "seq"), scatter_dimension=0, tiled=True),
        lax.psum_scatter(grad_k_gain, ("dp", "seq"), scatter_dimension=0, tiled=True),
        lax.psum_scatter(grad_attn_gain, ("dp", "seq"), scatter_dimension=0, tiled=True),
        lax.psum_scatter(grad_w_gate, ("dp", "seq"), scatter_dimension=0, tiled=True),
        lax.psum_scatter(grad_w_up, ("dp", "seq"), scatter_dimension=0, tiled=True),
        lax.psum_scatter(grad_w_down, ("dp", "seq"), scatter_dimension=0, tiled=True),
        lax.psum_scatter(grad_mlp_gain, ("dp", "seq"), scatter_dimension=0, tiled=True),
    )
    return (
        layer_out,
        input_grad,
        summed[0],
        summed[1],
        summed[2],
        summed[3],
        summed[4],
        summed[5],
        summed[6],
        summed[7],
        summed[8],
        summed[9],
        summed[10],
    )


def solution(mesh):
    return jax.shard_map(
        on_device,
        mesh=mesh,
        in_specs=(
            P(None, "dp", "seq", None),
            P(None, "dp", "seq", None),
            P(),
            P(),
            P(),
            P(),
            P(),
            P(),
            P(),
            P(),
            P(),
            P(),
            P(),
            P(None, "dp", None),
            P(),
        ),
        out_specs=(
            P(None, "dp", "seq", None),
            P(None, "dp", "seq", None),
            P(("dp", "seq"), None),
            P(("dp", "seq"), None),
            P(("dp", "seq"), None),
            P(("dp", "seq"), None),
            P(("dp", "seq")),
            P(("dp", "seq")),
            P(("dp", "seq")),
            P(("dp", "seq"), None),
            P(("dp", "seq"), None),
            P(("dp", "seq"), None),
            P(("dp", "seq")),
        ),
        check_vma=False,
    )
```

profile of v0, /device:TPU:0, one launch (start us, length us, event | category | flops | bytes accessed | tf_op | source)
XLA Modules:
  0.0 1732.2 jit_solution(10723629766554410809)
XLA Ops:
  32.7 36.8 %all-gather.3.cloned.1.call-done = bf16[2,1024,1024]{2,1,0:T(8,128)(2,1)} async-done(((bf16[2,64,1024]{2,1,0:T(8,128)(2,1)}), bf16[2,1024,1024]{2,1,0:T(8,128)(2,1)}) %all-gather.3.cloned.1.call-update) | async-done | bytes 4194320 | tf_op jit(solution)/shard_map/all_gather | solution.py:165
  75.7 45.8 %all-gather.5.cloned.1.call-done = bf16[2,1024,1024]{2,0,1:T(2,128)(2,1)} async-done(((bf16[2,64,1024]{2,0,1:T(2,128)(2,1)}), bf16[2,1024,1024]{2,0,1:T(2,128)(2,1)}) %all-gather.5.cloned.1.call-update) | async-done | bytes 4194320 | tf_op jit(solution)/shard_map/all_gather | solution.py:166
  121.5 11.2 copy.85
  132.7 61.2 %while.63 = (s32[]{:T(128)}, bf16[2,64,2048]{2,1,0:T(8,128)(2,1)}, f32[2,8,2,64]{3,2,1,0:T(2,128)S(1)}, f32[2,8,2,64]{3,2,1,0:T(2,128)}, bf16[2,64,2048]{2,1,0:T...) while((s32[]{:T(128)}, bf16[2,64,2048]{2,1,0:T(8,128)(2,1)}, ...), condition=%wide.region_7.8_spmd.clone, body=%wide.region_2.7_spmd.sunk.clone | while | flops 68157184 | bytes 30288196 | solution.py:172
  138.7 22.7 %while.62 = (s32[]{:T(128)}, bf16[8,64,2,128]{3,1,2,0:T(8,128)(2,1)S(1)}, f32[8,2,64]{2,1,0:T(2,128)S(1)}, f32[8,2,64]{2,1,0:T(2,128)S(1)}, bf16[8,1024,128]{1,2...) while((s32[]{:T(128)}, ...), condition=%wide.region_6.6_spmd, body=%wide.region_3.5_spmd.sunk | while | flops 68157184 | bytes 2335845 | solution.py:93
  169.2 22.7 %while.62 = (s32[]{:T(128)}, bf16[8,64,2,128]{3,1,2,0:T(8,128)(2,1)S(1)}, f32[8,2,64]{2,1,0:T(2,128)S(1)}, f32[8,2,64]{2,1,0:T(2,128)S(1)}, bf16[8,1024,128]{1,2...) while((s32[]{:T(128)}, ...), condition=%wide.region_6.6_spmd, body=%wide.region_3.5_spmd.sunk | while | flops 68157184 | bytes 2335845 | solution.py:93
  216.2 426.2 %while.65 = (s32[]{:T(128)}, f32[2,64,2048]{2,1,0:T(8,128)}, f32[2,64,1024]{2,1,0:T(8,128)}, bf16[2,64,1024]{2,1,0:T(8,128)(2,1)}, bf16[2,64,2048]{2,1,0:T(8,128...) while((s32[]{:T(128)}, f32[2,64,2048]{2,1,0:T(8,128)}, ...), condition=%wide.region_18.19_spmd.clone, body=%wide.region_12.18_spmd.sunk.clone | while | flops 169230208 | bytes 64511444 | solution.py:252
  223.2 53.3 %while.64 = (s32[]{:T(128)}, f32[8,64,2,128]{3,1,2,0:T(8,128)}, f32[8,1024,128]{2,1,0:T(8,128)}, f32[8,1024,128]{2,1,0:T(8,128)}, bf16[8,1024,128]{1,2,0:T(8,128...) while((s32[]{:T(128)}, f32[8,64,2,128]{3,1,2,0:T(8,128)}, ...), condition=%wide.region_15.15_spmd, body=%wide.region_13.14_spmd.sunk | while | flops 169230208 | bytes 6167677 | solution.py:232
  288.9 63.5 %reduce-scatter.30.cloned.1.call-done = f32[64,1024]{1,0:T(8,128)} async-done(((f32[1024,1024]{1,0:T(8,128)}), f32[64,1024]{1,0:T(8,128)}) %reduce-scatter.30.cloned.1.call-update) | async-done | bytes 262160 | tf_op jit(solution)/shard_map/while/body/eval_jaxpr/reduce_scatter | solution.py:247
  354.1 73.5 %reduce-scatter.32.cloned.1.call-done = f32[64,1024]{1,0:T(8,128)} async-done(((f32[1024,1024]{1,0:T(8,128)}), f32[64,1024]{1,0:T(8,128)}) %reduce-scatter.32.cloned.1.call-update) | async-done | bytes 262160 | tf_op jit(solution)/shard_map/while/body/eval_jaxpr/reduce_scatter | solution.py:248
  436.0 53.3 %while.64 = (s32[]{:T(128)}, f32[8,64,2,128]{3,1,2,0:T(8,128)}, f32[8,1024,128]{2,1,0:T(8,128)}, f32[8,1024,128]{2,1,0:T(8,128)}, bf16[8,1024,128]{1,2,0:T(8,128...) while((s32[]{:T(128)}, f32[8,64,2,128]{3,1,2,0:T(8,128)}, ...), condition=%wide.region_15.15_spmd, body=%wide.region_13.14_spmd.sunk | while | flops 169230208 | bytes 6167677 | solution.py:232
  501.7 63.9 %reduce-scatter.30.cloned.1.call-done = f32[64,1024]{1,0:T(8,128)} async-done(((f32[1024,1024]{1,0:T(8,128)}), f32[64,1024]{1,0:T(8,128)}) %reduce-scatter.30.cloned.1.call-update) | async-done | bytes 262160 | tf_op jit(solution)/shard_map/while/body/eval_jaxpr/reduce_scatter | solution.py:247
  567.2 73.5 %reduce-scatter.32.cloned.1.call-done = f32[64,1024]{1,0:T(8,128)} async-done(((f32[1024,1024]{1,0:T(8,128)}), f32[64,1024]{1,0:T(8,128)}) %reduce-scatter.32.cloned.1.call-update) | async-done | bytes 262160 | tf_op jit(solution)/shard_map/while/body/eval_jaxpr/reduce_scatter | solution.py:248
  701.2 9.2 copy.103
  719.3 6.4 fusion.53
  726.7 6.4 fusion.54
  739.5 40.5 %all-reduce.4 = (f32[2048]{0:T(1024)S(1)}, f32[1024]{0:T(1024)S(1)}, f32[1024]{0:T(1024)S(1)}, f32[1024]{0:T(1024)S(1)}) all-reduce(f32[2048]{0:T(1024)S(1)} %get-tuple-element.340, f32[1024]{0:T(1024)S(1)} %get-tuple-element.344, f32[1024]{0:T(1024)S(1)} %copy-done.42, ...), channel_id=8, replica_groups=mesh['dp'=2,'seq'=16] {'dp','seq'}, use_global_device_ids=true, to_apply=%region_26.27.clone | all-reduce | flops 5120 | bytes 40960
  788.0 16.2 reduce-scatter.26.cloned.1.call-done
  804.2 140.7 %reduce-scatter.28.cloned.1.call-done = f32[32,1024]{1,0:T(8,128)} async-done(((f32[1024,1024]{1,0:T(8,128)}), f32[32,1024]{1,0:T(8,128)}) %reduce-scatter.28.cloned.1.call-update) | async-done | bytes 131088
  944.9 147.9 %reduce-scatter.24.cloned.1.call-done = f32[32,2048]{1,0:T(8,128)} async-done(((f32[1024,2048]{1,0:T(8,128)}), f32[32,2048]{1,0:T(8,128)}) %reduce-scatter.24.cloned.1.call-update) | async-done | bytes 262160
  1092.8 159.0 %reduce-scatter.22.cloned.1.call-done = f32[96,1024]{1,0:T(8,128)} async-done(((f32[3072,1024]{1,0:T(8,128)}), f32[96,1024]{1,0:T(8,128)}) %reduce-scatter.22.cloned.1.call-update) | async-done | bytes 393232 | tf_op jit(solution)/shard_map/reduce_scatter | solution.py:284
  1251.8 162.1 %reduce-scatter.18.cloned.1.call-done = f32[32,3072]{1,0:T(8,128)} async-done(((f32[1024,3072]{1,0:T(8,128)}), f32[32,3072]{1,0:T(8,128)}) %reduce-scatter.18.cloned.1.call-update) | async-done | bytes 393232 | tf_op jit(solution)/shard_map/reduce_scatter | solution.py:282
  1413.9 160.9 %reduce-scatter.20.cloned.1.call-done = f32[32,3072]{1,0:T(8,128)} async-done(((f32[1024,3072]{1,0:T(8,128)}), f32[32,3072]{1,0:T(8,128)}) %reduce-scatter.20.cloned.1.call-update) | async-done | bytes 393232 | tf_op jit(solution)/shard_map/reduce_scatter | solution.py:283
  1574.8 150.4 %reduce-scatter.16.cloned.1.call-done = f32[64,1024]{1,0:T(8,128)} async-done(((f32[2048,1024]{1,0:T(8,128)}), f32[64,1024]{1,0:T(8,128)}) %reduce-scatter.16.cloned.1.call-update) | async-done | bytes 262160 | tf_op jit(solution)/shard_map/reduce_scatter | solution.py:278
  (487 shorter events, 347.3 us)
Async XLA Ops:
  7.2 8.9 copy-start.3
  7.2 62.3 %all-gather.3.cloned.1.call-start = ((), (), s32[]{:S(2)}) async-start(), calls=%async_computation.9 | async-start | bytes 4456448 | tf_op jit(solution)/shard_map/all_gather | solution.py:165
  14.6 10.1 copy-start.33
  16.0 105.5 %all-gather.5.cloned.1.call-start = ((), (), s32[]{:S(2)}) async-start(), calls=%async_computation.10 | async-start | bytes 4456448 | tf_op jit(solution)/shard_map/all_gather | solution.py:166
  132.7 64.5 %copy-start.38 = (f32[1024]{0:T(1024)S(1)}, f32[1024]{0:T(1024)}, u32[]{:S(2)}) copy-start(f32[1024]{0:T(1024)} %param.31) | copy-start | bytes 12292
  216.4 136.0 %reduce-scatter.30.cloned.1.call-start = ((), (), s32[]{:S(2)}) async-start(), calls=%async_computation.18 | async-start | bytes 4456448 | tf_op jit(solution)/shard_map/while/body/eval_jaxpr/reduce_scatter | solution.py:247
  281.3 146.3 %reduce-scatter.32.cloned.1.call-start = ((), (), s32[]{:S(2)}) async-start(), calls=%async_computation.19 | async-start | bytes 4456448 | tf_op jit(solution)/shard_map/while/body/eval_jaxpr/reduce_scatter | solution.py:248
  429.2 136.3 %reduce-scatter.30.cloned.1.call-start = ((), (), s32[]{:S(2)}) async-start(), calls=%async_computation.18 | async-start | bytes 4456448 | tf_op jit(solution)/shard_map/while/body/eval_jaxpr/reduce_scatter | solution.py:247
  494.1 146.7 %reduce-scatter.32.cloned.1.call-start = ((), (), s32[]{:S(2)}) async-start(), calls=%async_computation.19 | async-start | bytes 4456448 | tf_op jit(solution)/shard_map/while/body/eval_jaxpr/reduce_scatter | solution.py:248
  642.4 9.0 copy-start.34
  642.4 9.0 copy-start.35
  642.4 161.9 %reduce-scatter.26.cloned.1.call-start = ((), (), s32[]{:S(2)}) async-start(), calls=%async_computation.16 | async-start | bytes 4325376
  642.4 12.2 copy-start.9
  642.4 12.2 copy-start.40
  642.4 12.2 copy-start.44
  663.9 281.0 %reduce-scatter.28.cloned.1.call-start = ((), (), s32[]{:S(2)}) async-start(), calls=%async_computation.17 | async-start | bytes 4325376
  672.9 419.9 %reduce-scatter.24.cloned.1.call-start = ((), (), s32[]{:S(2)}) async-start(), calls=%async_computation.15 | async-start | bytes 8650752
  710.5 541.3 %reduce-scatter.22.cloned.1.call-start = ((), (), s32[]{:S(2)}) async-start(), calls=%async_computation.14 | async-start | bytes 12976128 | tf_op jit(solution)/shard_map/reduce_scatter | solution.py:284
  718.1 695.9 %reduce-scatter.18.cloned.1.call-start = ((), (), s32[]{:S(2)}) async-start(), calls=%async_computation.12 | async-start | bytes 12976128 | tf_op jit(solution)/shard_map/reduce_scatter | solution.py:282
  725.6 849.2 %reduce-scatter.20.cloned.1.call-start = ((), (), s32[]{:S(2)}) async-start(), calls=%async_computation.13 | async-start | bytes 12976128 | tf_op jit(solution)/shard_map/reduce_scatter | solution.py:283
  733.2 992.0 %reduce-scatter.16.cloned.1.call-start = ((), (), s32[]{:S(2)}) async-start(), calls=%async_computation.11 | async-start | bytes 8650752 | tf_op jit(solution)/shard_map/reduce_scatter | solution.py:278
  738.8 43.5 %copy-start.28 = (bf16[128,1024]{1,0:T(8,128)(2,1)S(1)}, bf16[128,1024]{1,0:T(8,128)(2,1)}, u32[]{:S(2)}) copy-start(bf16[128,1024]{1,0:T(8,128)(2,1)} %copy-done.27) | copy-start | bytes 786436
  738.9 46.8 %copy-start.14 = (bf16[128,2048]{1,0:T(8,128)(2,1)S(1)}, bf16[128,2048]{1,0:T(8,128)(2,1)}, u32[]{:S(2)}) copy-start(bf16[128,2048]{1,0:T(8,128)(2,1)} %copy-done.13) | copy-start | bytes 1572868
  738.9 46.8 %copy-start.19 = (f32[128,1024]{1,0:T(8,128)S(1)}, f32[128,1024]{1,0:T(8,128)}, u32[]{:S(2)}) copy-start(f32[128,1024]{1,0:T(8,128)} %copy-done.18) | copy-start | bytes 1572868
  (41 other events, 121.5 us)
Sparse Core Ops, SparseCore 0:
  16.1 53.3 all-gather.2
  72.2 49.1 all-gather.4
  281.4 70.9 reduce-scatter.29
  356.1 71.4 reduce-scatter.31
  494.2 71.3 reduce-scatter.29
  569.2 71.4 reduce-scatter.31
  664.0 140.1 reduce-scatter.25
  807.1 137.7 reduce-scatter.27
  947.8 144.9 reduce-scatter.23
  1099.3 152.5 reduce-scatter.21
  1259.5 154.4 reduce-scatter.17
  1420.4 154.4 reduce-scatter.19
  1577.8 147.3 reduce-scatter.15
where the time goes:
time: 1740 us; the launch traced here: 1730 us
  waiting for transfers between devices  1290 us (74%)
  matrix products  206 us (12%)
  local copies, waits for them, and re-layouts  152 us (9%)
  blocking collectives  40.5 us (2%)
  other arithmetic  21.2 us (1%)
    unnamed x12, waiting for transfers between devices  305 us
    reduce_scatter x1, waiting for transfers between devices, on_device(): lax.psum_scatter(grad_w_gate, ('dp', 'seq'), scatter_dimension=0, tiled=T...  162 us
    reduce_scatter x1, waiting for transfers between devices, on_device(): lax.psum_scatter(grad_w_up, ('dp', 'seq'), scatter_dimension=0, tiled=True)  161 us
    reduce_scatter x1, waiting for transfers between devices, on_device(): lax.psum_scatter(grad_w_down, ('dp', 'seq'), scatter_dimension=0, tiled=T...  159 us
    reduce_scatter x1, waiting for transfers between devices, on_device(): lax.psum_scatter(grad_w_out, ('dp', 'seq'), scatter_dimension=0, tiled=True)  150 us
    reduce_scatter x2, waiting for transfers between devices, query_pass(): lax.psum_scatter(value_terms, 'seq', scatter_dimension=0, tiled=True)  147 us
    reduce_scatter x2, waiting for transfers between devices, query_pass(): lax.psum_scatter(key_terms, 'seq', scatter_dimension=0, tiled=True)  127 us
    all_gather x1, waiting for transfers between devices, on_device(): lax.all_gather(v_blocks, 'seq', axis=1, tiled=True)  45.8 us
  transfers between devices with their start and end apart: 13, of which 13 were waited for; matrix products, arithmetic and copies ran while one was open for 7% of the time, Pallas kernels for 0%

commit v1 on v0

--- a/solution.py
+++ b/solution.py
@@ -1,27 +1,726 @@
+import functools
+
 import jax
 import jax.numpy as jnp
+import numpy as np
 from jax import lax
+from jax.experimental import pallas as pl
+from jax.experimental.pallas import tpu as pltpu
 from jax.sharding import PartitionSpec as P
 
 HD = 128
-
-
 EPSILON = 1e-06
 ROPE_BASE = 500000.0
 MASK_FILL = -1e30
-
-
-def rms_forward(inputs, gain_vec):
-    factor = lax.rsqrt(jnp.mean(inputs * inputs, axis=-1, keepdims=True) + EPSILON)
-    normal = inputs * factor
-    return (normal * gain_vec, normal, factor)
-
-
-def rms_backward(grad_in, gain_vec, normal, factor):
-    weighted = grad_in * gain_vec
-    gain_grad = jnp.sum(grad_in * normal, axis=0)
-    inner_mean = jnp.mean(weighted * normal, axis=-1, keepdims=True)
-    return (factor * (weighted - normal * inner_mean), gain_grad)
+MESH = pl.DeviceIdType.MESH
+LOW = jnp.bfloat16
+WIDE = jnp.float32
+TILE = 128
+CHUNK = 256
+
+
+def remote(source, target, send_sem, recv_sem, place):
+    return pltpu.make_async_remote_copy(
+        src_ref=source,
+        dst_ref=target,
+        send_sem=send_sem,
+        recv_sem=recv_sem,
+        device_id=place,
+        device_id_type=MESH,
+    )
+
+
+def dot(left, right):
+    return jnp.dot(left, right, preferred_element_type=WIDE)
+
+
+def dot_nt(left, right):
+    return lax.dot_general(left, right, (((1,), (1,)), ((), ())), preferred_element_type=WIDE)
+
+
+def dot_tn(left, right):
+    return lax.dot_general(left, right, (((0,), (0,)), ((), ())), preferred_element_type=WIDE)
+
+
+class Spot:
+    def __init__(self):
+        self.dp = lax.axis_index("dp")
+        self.seq = lax.axis_index("seq")
+        self.core = self.seq % 2
+        self.chip = self.seq // 2
+        self.x = self.chip % 2
+        self.z = self.chip // 2
+        self.sibling = self.seq + 1 - 2 * self.core
+        self.flip_x = self.seq + 2 - 4 * self.x
+        self.far_z = (
+            self.z + 1 - 2 * (self.z % 2),
+            self.z + 2 - 4 * (self.z // 2),
+            3 - self.z,
+        )
+
+
+def greet_row(spot, devices):
+    barrier = pltpu.get_barrier_semaphore()
+    for step in range(1, devices):
+        pl.semaphore_signal(
+            barrier,
+            inc=1,
+            device_id=(spot.dp, (spot.seq + step) % devices),
+            device_id_type=MESH,
+        )
+    pl.semaphore_wait(barrier, devices - 1)
+
+
+class RowGather:
+    def __init__(self, spot, own, held, local_sem, send_sems, recv_sems):
+        self.spot, self.own, self.held = spot, own, held
+        self.send_sems, self.recv_sems = send_sems, recv_sems
+        self.sent = []
+        self.local = pltpu.make_async_copy(own.at[spot.core], held.at[spot.seq], local_sem)
+
+    def send(self, source, slots, recv_sem, target):
+        copy = remote(
+            source, slots, self.send_sems.at[len(self.sent)], recv_sem, (self.spot.dp, target)
+        )
+        copy.start()
+        self.sent.append(copy)
+
+    def start(self):
+        spot = self.spot
+        own_slot = self.held.at[spot.seq]
+        own_sem = self.recv_sems.at[spot.seq]
+        for far in spot.far_z:
+            for micro in range(2):
+                self.send(self.own.at[micro], own_slot, own_sem, far * 4 + spot.x * 2 + micro)
+        for micro in range(2):
+            self.send(
+                self.own.at[micro], own_slot, own_sem, spot.z * 4 + (1 - spot.x) * 2 + micro
+            )
+        self.send(self.own.at[1 - spot.core], own_slot, own_sem, spot.sibling)
+        self.local.start()
+
+    def arrived(self, slots, recv_sem):
+        remote(slots, slots, self.send_sems.at[0], recv_sem, (self.spot.dp, self.spot.sibling)).wait_recv()
+
+    def forward(self):
+        spot = self.spot
+        for far in spot.far_z:
+            first = far * 4 + spot.x * 2
+            for core in range(2):
+                self.arrived(self.held.at[first + core], self.recv_sems.at[first + core])
+            pair = self.held.at[pl.ds(first, 2)]
+            self.send(pair, pair, self.recv_sems.at[16 + far], spot.flip_x)
+
+    def finish(self):
+        spot = self.spot
+        self.arrived(self.held.at[spot.sibling], self.recv_sems.at[spot.sibling])
+        for core in range(2):
+            slot = spot.z * 4 + (1 - spot.x) * 2 + core
+            self.arrived(self.held.at[slot], self.recv_sems.at[slot])
+        for far in spot.far_z:
+            first = far * 4 + (1 - spot.x) * 2
+            self.arrived(self.held.at[pl.ds(first, 2)], self.recv_sems.at[16 + far])
+        self.local.wait()
+        for copy in self.sent:
+            copy.wait_send()
+
+
+GATHER_SENDS = 12
+GATHER_RECVS = 20
+
+
+def rope_rows(table, block, first_length):
+    start = block * 64
+    inside = table[pl.ds(64 + start, 64), :]
+    shifted = table[pl.ds(64 + jnp.maximum(start - first_length, -64), 64), :]
+    places = start + lax.broadcasted_iota(jnp.int32, (64, HD), 0)
+    return jnp.where(places < first_length, inside, shifted)
+
+
+def swap_halves(head):
+    return pltpu.roll(head, HD // 2, axis=1)
+
+
+def columns_of(rows):
+    return jnp.concatenate([rows] * 16, axis=0).T[:, :8]
+
+
+def rows_of(first, second):
+    lane = lax.broadcasted_iota(jnp.int32, (first.shape[0], HD), 1)
+    return jnp.where(lane == 0, first, second).T[:8]
+
+
+def allowed_places(tile, count, first_length):
+    keys = lax.broadcasted_iota(jnp.int32, (count, 2 * TILE), 0)
+    lanes = lax.broadcasted_iota(jnp.int32, (1, 2 * TILE), 1)
+    queries = tile * TILE + lanes % TILE
+    earliest = jnp.where(queries < first_length, 0, first_length)
+    return (keys >= earliest) & (keys <= queries)
+
+
+def forward_kernel(
+    tok_ref, wq_hbm, wk_hbm, wv_hbm, qgain_ref, kgain_ref, cos_ref, sine_ref,
+    order_ref, inverse_ref, first_ref,
+    att_tok, tok_nat, q_pair, kv_nat, hat, factors, lse, att_nat,
+    tok_all, w_own, stat_all, att_send, att_recv, kv_turned,
+    local_sems, send_sems, recv_sems, stat_send, stat_recv, att_ssem, att_rsem,
+):
+    spot = Spot()
+    devices = 16
+    chips = 8
+    chip = spot.chip
+    loads = [
+        pltpu.make_async_copy(wq_hbm.at[:, pl.ds(pl.multiple_of(chip * 256, 256), 256)], w_own.at[:, pl.ds(0, 256)], local_sems.at[1]),
+        pltpu.make_async_copy(wk_hbm.at[:, pl.ds(pl.multiple_of(chip * 128, 128), 128)], w_own.at[:, pl.ds(256, 128)], local_sems.at[2]),
+        pltpu.make_async_copy(wv_hbm.at[:, pl.ds(pl.multiple_of(chip * 128, 128), 128)], w_own.at[:, pl.ds(384, 128)], local_sems.at[3]),
+    ]
+    for load in loads:
+        load.start()
+    greet_row(spot, devices)
+    gather = RowGather(spot, tok_ref, tok_all, local_sems.at[0], send_sems, recv_sems)
+    gather.start()
+    gather.forward()
+    for load in loads:
+        load.wait()
+    gather.finish()
+
+    first_length = first_ref[spot.core]
+    for part in range(4):
+        rows = pl.ds(part * CHUNK, CHUNK)
+        chunk = jnp.concatenate([tok_all[inverse_ref[part * 4 + piece]] for piece in range(4)], axis=0)
+        tok_nat[rows, :] = chunk
+        pre = dot(chunk, w_own[...])
+        hat[rows, :] = pre[:, :384]
+        kv_nat[rows, 128:] = pre[:, 384:].astype(LOW)
+        squares = pre[:, :384] * pre[:, :384]
+        stat_all[pl.ds(chip, 1), :, rows] = rows_of(
+            jnp.sum(squares[:, :256], axis=-1, keepdims=True),
+            jnp.sum(squares[:, 256:], axis=-1, keepdims=True),
+        )[None]
+    stat_copies = []
+    for step in range(1, chips):
+        other = (chip + step) % chips
+        copy = remote(
+            stat_all.at[chip], stat_all.at[chip], stat_send.at[step - 1], stat_recv.at[chip],
+            (spot.dp, other * 2 + spot.core),
+        )
+        copy.start()
+        stat_copies.append(copy)
+    for step in range(1, chips):
+        other = (chip + step) % chips
+        remote(
+            stat_all.at[other], stat_all.at[other], stat_send.at[0], stat_recv.at[other],
+            (spot.dp, spot.sibling),
+        ).wait_recv()
+    total = stat_all[0]
+    for other in range(1, chips):
+        total = total + stat_all[other]
+    width = jnp.where(lax.broadcasted_iota(jnp.int32, total.shape, 0) == 0, 1.0 / 2048, 1.0 / 1024)
+    factors[...] = lax.rsqrt(total * width + EPSILON)
+    qgain = qgain_ref[pl.ds(chip * 2, 2), :]
+    kgain = kgain_ref[pl.ds(chip, 1), :]
+    for part in range(8):
+        rows = pl.ds(part * TILE, TILE)
+        scale = columns_of(factors[:, rows])
+        cos = jnp.concatenate([rope_rows(cos_ref, part * 2 + piece, first_length) for piece in range(2)], axis=0)
+        sine = jnp.concatenate([rope_rows(sine_ref, part * 2 + piece, first_length) for piece in range(2)], axis=0)
+        for head in range(3):
+            lanes = pl.ds(head * HD, HD)
+            column = scale[:, 0:1] if head < 2 else scale[:, 1:2]
+            gain = qgain[head : head + 1] if head < 2 else kgain
+            normal = hat[rows, lanes] * column
+            hat[rows, lanes] = normal
+            normed = normal * gain
+            turned = (normed * cos + swap_halves(normed) * sine).astype(LOW)
+            if head < 2:
+                q_pair[part, pl.ds(head * HD, HD), :] = turned
+            else:
+                kv_nat[rows, :HD] = turned
+    kv_turned[...] = kv_nat[:, HD:].T
+    for tile in range(8):
+        count = (tile + 1) * TILE
+        scores = dot_nt(kv_nat[:count, :HD], q_pair[tile]) * HD ** (-0.5)
+        masked = jnp.where(allowed_places(tile, count, first_length), scores, MASK_FILL)
+        top = jnp.max(masked, axis=0, keepdims=True)
+        terms = jnp.exp(masked - top)
+        weight = jnp.sum(terms, axis=0, keepdims=True)
+        lse[pl.ds(tile, 1), :] = top + jnp.log(weight)
+        turned = dot(kv_turned[:, :count], terms.astype(LOW)) / weight
+        attended = turned.T.astype(LOW)
+        att_nat[pl.ds(tile * 2, 2), :, :HD] = attended[:TILE].reshape(2, 64, HD)
+        att_nat[pl.ds(tile * 2, 2), :, HD:] = attended[TILE:].reshape(2, 64, HD)
+    own_part = (spot.core, slice(None), pl.ds(pl.multiple_of(chip * 256, 256), 256))
+    att_recv[pl.ds(chip, 1), pl.ds(spot.core, 1)] = att_nat[order_ref[spot.seq]][None, None]
+    sent = []
+    for step in range(1, devices):
+        other = (spot.seq + step) % devices
+        att_send[step] = att_nat[order_ref[other]]
+        copy = remote(
+            att_send.at[step], att_recv.at[chip, spot.core], att_ssem.at[step],
+            att_rsem.at[spot.seq], (spot.dp, other),
+        )
+        copy.start()
+        sent.append(copy)
+    for step in range(1, devices):
+        other = (spot.seq + step) % devices
+        slot = att_recv.at[other // 2, other % 2]
+        remote(slot, slot, att_ssem.at[0], att_rsem.at[other], (spot.dp, spot.sibling)).wait_recv()
+    for piece in range(chips):
+        for micro in range(2):
+            att_tok[micro, :, piece * 256 : (piece + 1) * 256] = att_recv[piece, micro]
+    for copy in sent + stat_copies:
+        copy.wait_send()
+
+
+def rope_constants(length):
+    frequency = np.power(np.float32(ROPE_BASE), -np.arange(0, HD, 2).astype(np.float32) / np.float32(HD)).astype(np.float32)
+    angles = (np.arange(length, dtype=np.float32)[:, None] * frequency[None, :]).astype(np.float32).astype(np.float64)
+    cos, sine = np.cos(angles), np.sin(angles)
+    front = np.zeros((64, HD))
+    cos = np.concatenate([front, np.concatenate([cos, cos], axis=1)], axis=0)
+    sine = np.concatenate([front, np.concatenate([-sine, sine], axis=1)], axis=0)
+    return jnp.asarray(cos, WIDE), jnp.asarray(sine, WIDE)
+
+
+def row_forward(tokens, w_query, w_key, w_value, q_gain, k_gain, cos, sine, order, inverse, first):
+    length = 1024
+    width = tokens.shape[-1]
+    any_spec = pl.BlockSpec(memory_space=pl.ANY)
+    vmem = pl.BlockSpec(memory_space=pltpu.VMEM)
+    smem = pl.BlockSpec(memory_space=pltpu.SMEM)
+    shape = jax.ShapeDtypeStruct
+    return pl.pallas_call(
+        forward_kernel,
+        out_shape=(
+            shape((2, 64, 2048), LOW),
+            shape((length, width), LOW),
+            shape((8, 2 * TILE, HD), LOW),
+            shape((length, 2 * HD), LOW),
+            shape((length, 3 * HD), WIDE),
+            shape((8, length), WIDE),
+            shape((8, 2 * TILE), WIDE),
+            shape((16, 64, 2 * HD), LOW),
+        ),
+        in_specs=[vmem, any_spec, any_spec, any_spec, vmem, vmem, vmem, vmem, smem, smem, smem],
+        out_specs=(vmem,) * 8,
+        scratch_shapes=[
+            pltpu.VMEM((16, 64, width), LOW),
+            pltpu.VMEM((width, 512), LOW),
+            pltpu.VMEM((8, 8, length), WIDE),
+            pltpu.VMEM((16, 64, 2 * HD), LOW),
+            pltpu.VMEM((8, 2, 64, 2 * HD), LOW),
+            pltpu.VMEM((HD, length), LOW),
+            pltpu.SemaphoreType.DMA((4,)),
+            pltpu.SemaphoreType.DMA((GATHER_SENDS,)),
+            pltpu.SemaphoreType.DMA((GATHER_RECVS,)),
+            pltpu.SemaphoreType.DMA((8,)),
+            pltpu.SemaphoreType.DMA((8,)),
+            pltpu.SemaphoreType.DMA((16,)),
+            pltpu.SemaphoreType.DMA((16,)),
+        ],
+        compiler_params=pltpu.CompilerParams(
+            collective_id=0, has_side_effects=True, vmem_limit_bytes=56 * 2**20
+        ),
+        name="row_forward",
+    )(tokens, w_query, w_key, w_value, q_gain, k_gain, cos, sine, order, inverse, first)
+
+
+class Post:
+    def __init__(self, sems):
+        self.sems, self.started = sems, []
+
+    def send(self, source, target, recv_sem, place):
+        copy = remote(source, target, self.sems.at[len(self.started)], recv_sem, place)
+        copy.start()
+        self.started.append(copy)
+
+    def finish(self):
+        for copy in self.started:
+            copy.wait_send()
+
+
+def arrived(spot, slot, recv_sem, spare_sem):
+    remote(slot, slot, spare_sem, recv_sem, (spot.dp, spot.sibling)).wait_recv()
+
+
+def backward_kernel(
+    proj_ref, hid_ref, down_ref, gate_ref, up_ref, mixed_ref, hgrad_ref, vec_ref,
+    tok_nat, q_pair, kv_nat, hat, factors, lse, att_nat,
+    wout_hbm, wq_hbm, wk_hbm, wv_hbm, qgain_ref, kgain_ref, cos_ref, sine_ref,
+    order_ref, inverse_ref, first_ref,
+    in_grad, g_query, g_key, g_value, g_out, vec_out, gain_out, g_gate, g_up, g_down,
+    wout_own, wq_all, wk_all, wv_all,
+    proj_all, proj_nat, mix_turned, hid_all, down_all, gu_all, mix_all, vec_all, vec_far,
+    ag_pair, k_turned, dq, dkv, grad_nat, stat_all, grad_send, grad_recv, grad_tok,
+    part_low, wqkv_recv, wout_low, wout_recv, gain_own, gain_recv, gu_low, gu_recv, down_low, down_recv,
+    local_sems, send_sems, recv_sems, post_sems, plane_sems, far_sems, stat_sems, grad_sems, wqkv_sems, wout_sems, gu_sems, self_sems,
+):
+    spot = Spot()
+    devices, chips = 16, 8
+    dp, seq, core, chip, z = spot.dp, spot.seq, spot.core, spot.chip, spot.z
+    me = dp * devices + seq
+    member = dp * 4 + spot.x * 2 + core
+    spare = post_sems.at[0]
+    loads = [
+        pltpu.make_async_copy(wout_hbm.at[pl.ds(pl.multiple_of(chip * 256, 256), 256)], wout_own, local_sems.at[1]),
+        pltpu.make_async_copy(wq_hbm, wq_all, local_sems.at[2]),
+        pltpu.make_async_copy(wk_hbm, wk_all, local_sems.at[3]),
+        pltpu.make_async_copy(wv_hbm, wv_all, local_sems.at[4]),
+    ]
+    for load in loads:
+        load.start()
+    barrier = pltpu.get_barrier_semaphore()
+    for step in range(1, 2 * devices):
+        other = (me + step) % (2 * devices)
+        pl.semaphore_signal(barrier, inc=1, device_id=(other // devices, other % devices), device_id_type=MESH)
+    for group in range(8):
+        block = mixed_ref[:, group * 384 : (group + 1) * 384].T
+        for piece in range(4):
+            mix_turned[(group // 4) * 4 + piece, pl.ds((group % 4) * 96, 96), :] = block[piece * 96 : (piece + 1) * 96]
+    pl.semaphore_wait(barrier, 2 * devices - 1)
+
+    gather = RowGather(spot, proj_ref, proj_all, local_sems.at[0], send_sems, recv_sems)
+    gather.start()
+
+    post = Post(post_sems)
+    plane_places = ((dp, spot.flip_x), (1 - dp, seq), (1 - dp, spot.flip_x))
+    plane_members = (
+        dp * 4 + (1 - spot.x) * 2 + core,
+        (1 - dp) * 4 + spot.x * 2 + core,
+        (1 - dp) * 4 + (1 - spot.x) * 2 + core,
+    )
+    sib_place = (dp, spot.sibling)
+    keeps = [
+        pltpu.make_async_copy(hid_ref, hid_all.at[member], local_sems.at[5]),
+        pltpu.make_async_copy(down_ref, down_all.at[member], local_sems.at[6]),
+        pltpu.make_async_copy(gate_ref.at[:, pl.ds(pl.multiple_of(member * 384, 128), 384)], gu_all.at[member, :, pl.ds(0, 384)], local_sems.at[7]),
+        pltpu.make_async_copy(up_ref.at[:, pl.ds(pl.multiple_of(member * 384, 128), 384)], gu_all.at[member, :, pl.ds(384, 384)], local_sems.at[8]),
+        pltpu.make_async_copy(mix_turned.at[member], mix_all.at[member], local_sems.at[9]),
+        pltpu.make_async_copy(vec_ref, vec_all.at[member], local_sems.at[10]),
+    ]
+    for keep in keeps:
+        keep.start()
+    for place in plane_places:
+        post.send(hid_ref, hid_all.at[member], plane_sems.at[0, member], place)
+        post.send(down_ref, down_all.at[member], plane_sems.at[1, member], place)
+    post.send(hid_ref, hid_all.at[member], plane_sems.at[0, member], sib_place)
+    post.send(down_ref, down_all.at[member], plane_sems.at[1, member], sib_place)
+    for step in range(1, 8):
+        other = (member + step) % 8
+        place = (other // 4, z * 4 + other % 4)
+        lanes = pl.ds(pl.multiple_of(other * 384, 128), 384)
+        post.send(mix_turned.at[other], mix_all.at[member], plane_sems.at[2, member], place)
+        post.send(gate_ref.at[:, lanes], gu_all.at[member, :, pl.ds(0, 384)], plane_sems.at[3, member], place)
+        post.send(up_ref.at[:, lanes], gu_all.at[member, :, pl.ds(384, 384)], plane_sems.at[4, member], place)
+        post.send(vec_ref, vec_all.at[member], plane_sems.at[5, member], place)
+
+    gather.forward()
+    for other in plane_members:
+        arrived(spot, hid_all.at[other], plane_sems.at[0, other], spare)
+        post.send(hid_all.at[other], hid_all.at[other], plane_sems.at[0, other], sib_place)
+        arrived(spot, down_all.at[other], plane_sems.at[1, other], spare)
+        post.send(down_all.at[other], down_all.at[other], plane_sems.at[1, other], sib_place)
+    gather.finish()
+
+    loads[0].wait()
+    for part in range(8):
+        rows = pl.ds(part * TILE, TILE)
+        chunk = jnp.concatenate([proj_all[inverse_ref[part * 2 + piece]] for piece in range(2)], axis=0)
+        proj_nat[rows, :] = chunk
+        att_grad = dot_nt(chunk, wout_own[...]).astype(LOW)
+        ag_pair[part, :TILE, :] = att_grad[:, :HD]
+        ag_pair[part, TILE:, :] = att_grad[:, HD:]
+    wout_low[...] = dot_tn(att_nat[...].reshape(1024, 2 * HD), proj_nat[...]).astype(LOW)
+    for piece in range(4):
+        target = chip * 4 + piece
+        rows = pl.ds(piece * 64, 64)
+        slot = wout_recv.at[dp * 2 + core]
+
+        @pl.when(target == me)
+        def _():
+            keep = pltpu.make_async_copy(wout_low.at[rows], slot, self_sems.at[0])
+            keep.start()
+            keep.wait()
+
+        @pl.when(target != me)
+        def _():
+            remote(
+                wout_low.at[rows], slot, wout_sems.at[piece], wout_sems.at[4 + dp * 2 + core],
+                (target // devices, target % devices),
+            ).start()
+
+    k_turned[...] = kv_nat[:, :HD].T
+    first_length = first_ref[core]
+    dkv[...] = jnp.zeros_like(dkv)
+    for tile in range(8):
+        count = (tile + 1) * TILE
+        queries, grads = q_pair[tile], ag_pair[tile]
+        scores = dot_nt(kv_nat[:count, :HD], queries) * HD ** (-0.5)
+        masked = jnp.where(allowed_places(tile, count, first_length), scores, MASK_FILL)
+        probs = jnp.exp(masked - lse[tile : tile + 1, :])
+        prob_grad = dot_nt(kv_nat[:count, HD:], grads)
+        row_dot = jnp.sum(probs * prob_grad, axis=0, keepdims=True)
+        score_grad = (probs * (prob_grad - row_dot)).astype(LOW)
+        dkv[:count, :HD] += dot(score_grad, queries)
+        dkv[:count, HD:] += dot(probs.astype(LOW), grads)
+        turned = (dot(k_turned[:, :count], score_grad) * HD ** (-0.5)).T
+        rows = pl.ds(tile * TILE, TILE)
+        dq[rows, :HD] = turned[:TILE]
+        dq[rows, HD:] = turned[TILE:]
+
+    qgain = qgain_ref[pl.ds(chip * 2, 2), :]
+    kgain = kgain_ref[pl.ds(chip, 1), :]
+    gains = [jnp.zeros((1, HD), WIDE) for _ in range(3)]
+    for part in range(8):
+        rows = pl.ds(part * TILE, TILE)
+        cos = jnp.concatenate([rope_rows(cos_ref, part * 2 + piece, first_length) for piece in range(2)], axis=0)
+        sine = jnp.concatenate([rope_rows(sine_ref, part * 2 + piece, first_length) for piece in range(2)], axis=0)
+        dots = []
+        for head in range(3):
+            turned = dq[rows, pl.ds(head * HD, HD)] if head < 2 else dkv[rows, :HD] * HD ** (-0.5)
+            back = turned * cos - swap_halves(turned) * sine
+            normal = hat[rows, pl.ds(head * HD, HD)]
+            gain = qgain[head : head + 1] if head < 2 else kgain
+            gains[head] = gains[head] + jnp.sum(back * normal, axis=0, keepdims=True)
+            weighted = back * gain
+            if head < 2:
+                dq[rows, pl.ds(head * HD, HD)] = weighted
+            else:
+                dkv[rows, :HD] = weighted
+            dots.append(jnp.sum(weighted * normal, axis=-1, keepdims=True))
+        stat_all[pl.ds(chip, 1), :, rows] = rows_of(dots[0] + dots[1], dots[2])[None]
+    for step in range(1, chips):
+        other = (chip + step) % chips
+        post.send(stat_all.at[chip], stat_all.at[chip], stat_sems.at[chip], (dp, other * 2 + core))
+    gain_own[...] = jnp.concatenate([jnp.broadcast_to(gain, (8, HD)) for gain in gains], axis=1)
+    for piece in range(4):
+        target = chip * 4 + piece
+        slot = gain_recv.at[dp * 2 + core]
+
+        @pl.when(target == me)
+        def _():
+            keep = pltpu.make_async_copy(gain_own, slot, self_sems.at[0])
+            keep.start()
+            keep.wait()
+
+        @pl.when(target != me)
+        def _():
+            remote(
+                gain_own, slot, wout_sems.at[8 + piece], wout_sems.at[12 + dp * 2 + core],
+                (target // devices, target % devices),
+            ).start()
+
+    for step in range(1, chips):
+        other = (chip + step) % chips
+        arrived(spot, stat_all.at[other], stat_sems.at[other], spare)
+    total = stat_all[0]
+    for other in range(1, chips):
+        total = total + stat_all[other]
+    width = jnp.where(lax.broadcasted_iota(jnp.int32, total.shape, 0) == 0, 1.0 / 2048, 1.0 / 1024)
+    means = total * width
+    for part in range(8):
+        rows = pl.ds(part * TILE, TILE)
+        mean = columns_of(means[:, part * TILE : (part + 1) * TILE])
+        scale = columns_of(factors[:, rows])
+        pieces = []
+        for head in range(3):
+            column = 0 if head < 2 else 1
+            weighted = dq[rows, pl.ds(head * HD, HD)] if head < 2 else dkv[rows, :HD]
+            normal = hat[rows, pl.ds(head * HD, HD)]
+            pieces.append(scale[:, column : column + 1] * (weighted - normal * mean[:, column : column + 1]))
+        pieces.append(dkv[rows, HD:])
+        grad_nat[pl.ds(part * 2, 2)] = jnp.concatenate(pieces, axis=1).astype(LOW).reshape(2, 64, 512)
+
+    grad_recv[pl.ds(chip, 1), pl.ds(core, 1)] = grad_nat[order_ref[seq]][None, None]
+    for step in range(1, devices):
+        other = (seq + step) % devices
+        grad_send[step] = grad_nat[order_ref[other]]
+        post.send(grad_send.at[step], grad_recv.at[chip, core], grad_sems.at[seq], (dp, other))
+    part_low[...] = dot_tn(tok_nat[...], grad_nat[...].reshape(1024, 512)).astype(LOW)
+    own_rows = pl.ds(pl.multiple_of(me * 32, 32), 32)
+    wqkv_recv[pl.ds(me, 1)] = part_low[own_rows, :][None]
+    for step in range(1, 2 * devices):
+        other = (me + step) % (2 * devices)
+        post.send(
+            part_low.at[pl.ds(pl.multiple_of(other * 32, 32), 32)], wqkv_recv.at[me], wqkv_sems.at[me],
+            (other // devices, other % devices),
+        )
+
+    for keep in keeps:
+        keep.wait()
+    for step in range(1, 8):
+        other = (member + step) % 8
+        arrived(spot, mix_all.at[other], plane_sems.at[2, other], spare)
+        arrived(spot, gu_all.at[other, :, pl.ds(0, 384)], plane_sems.at[3, other], spare)
+        arrived(spot, gu_all.at[other, :, pl.ds(384, 384)], plane_sems.at[4, other], spare)
+        arrived(spot, vec_all.at[other], plane_sems.at[5, other], spare)
+    for y in range(2):
+        for x in range(2):
+            other = y * 4 + x * 2 + 1 - core
+            arrived(spot, hid_all.at[other], plane_sems.at[0, other], spare)
+            arrived(spot, down_all.at[other], plane_sems.at[1, other], spare)
+    vec = vec_all[0]
+    for other in range(1, 8):
+        vec = vec + vec_all[other]
+    vec_far[pl.ds(z, 1)] = vec[None]
+    mixes = jnp.concatenate([mix_all[other] for other in range(8)], axis=1)
+    down_low[...] = dot(mixes, down_all[...].reshape(1024, 1024)).astype(LOW)
+    down_recv[pl.ds(z, 1)] = down_low[pl.ds(pl.multiple_of(z * 96, 96), 96), :][None]
+    for far in spot.far_z:
+        place = (dp, far * 4 + spot.x * 2 + core)
+        post.send(vec_far.at[z], vec_far.at[z], far_sems.at[0, z], place)
+        post.send(down_low.at[pl.ds(pl.multiple_of(far * 96, 96), 96)], down_recv.at[z], far_sems.at[1, z], place)
+    gu_low[...] = dot_tn(hid_all[...].reshape(1024, 1024), gu_all[...].reshape(1024, 768)).astype(LOW)
+    gu_recv[pl.ds(z, 1), pl.ds(member, 1)] = gu_low[own_rows, :][None, None]
+    for step in range(1, 2 * devices):
+        other = (me + step) % (2 * devices)
+        post.send(
+            gu_low.at[pl.ds(pl.multiple_of(other * 32, 32), 32)], gu_recv.at[z, member], gu_sems.at[z, member],
+            (other // devices, other % devices),
+        )
+
+    for step in range(1, devices):
+        other = (seq + step) % devices
+        arrived(spot, grad_recv.at[other // 2, other % 2], grad_sems.at[other], spare)
+    for piece in range(chips):
+        for micro in range(2):
+            rows = pl.ds(micro * 64, 64)
+            block = grad_recv[piece, micro]
+            grad_tok[rows, piece * 256 : (piece + 1) * 256] = block[:, :256]
+            grad_tok[rows, 2048 + piece * 128 : 2048 + (piece + 1) * 128] = block[:, 256:384]
+            grad_tok[rows, 3072 + piece * 128 : 3072 + (piece + 1) * 128] = block[:, 384:]
+    for load in loads[1:]:
+        load.wait()
+    in_grad[...] = (
+        hgrad_ref[...]
+        + dot_nt(grad_tok[:, :2048], wq_all[...])
+        + dot_nt(grad_tok[:, 2048:3072], wk_all[...])
+        + dot_nt(grad_tok[:, 3072:], wv_all[...])
+    )
+
+    for y in range(2):
+        for micro in range(2):
+            source = y * 2 + micro
+            sender = y * devices + (me // 4) * 2 + micro
+
+            @pl.when(sender != me)
+            def _():
+                arrived(spot, wout_recv.at[source], wout_sems.at[4 + source], spare)
+                arrived(spot, gain_recv.at[source], wout_sems.at[12 + source], spare)
+
+    g_out[...] = sum(wout_recv[source].astype(WIDE) for source in range(4))
+    gain_out[...] = sum(gain_recv[source] for source in range(4))
+    for step in range(1, 2 * devices):
+        other = (me + step) % (2 * devices)
+        arrived(spot, wqkv_recv.at[other], wqkv_sems.at[other], spare)
+    for piece in range(chips):
+        block = sum(
+            wqkv_recv[y * devices + piece * 2 + micro].astype(WIDE) for y in range(2) for micro in range(2)
+        )
+        g_query[:, piece * 256 : (piece + 1) * 256] = block[:, :256]
+        g_key[:, piece * 128 : (piece + 1) * 128] = block[:, 256:384]
+        g_value[:, piece * 128 : (piece + 1) * 128] = block[:, 384:]
+    for far in spot.far_z:
+        arrived(spot, vec_far.at[far], far_sems.at[0, far], spare)
+        arrived(spot, down_recv.at[far], far_sems.at[1, far], spare)
+    vec_out[...] = sum(vec_far[far] for far in range(4))
+    g_down[...] = sum(down_recv[far].astype(WIDE) for far in range(4))
+    for step in range(1, 2 * devices):
+        other = (me + step) % (2 * devices)
+        far, slot = (other % devices) // 4, (other // devices) * 4 + other % 4
+        arrived(spot, gu_recv.at[far, slot], gu_sems.at[far, slot], spare)
+    for slot in range(8):
+        block = sum(gu_recv[far, slot].astype(WIDE) for far in range(4))
+        g_gate[:, slot * 384 : (slot + 1) * 384] = block[:, :384]
+        g_up[:, slot * 384 : (slot + 1) * 384] = block[:, 384:]
+    post.finish()
+    for piece in range(4):
+
+        @pl.when(chip * 4 + piece != me)
+        def _():
+            place = ((chip * 4 + piece) // devices, (chip * 4 + piece) % devices)
+            rows = pl.ds(piece * 64, 64)
+            remote(wout_low.at[rows], wout_recv.at[0], wout_sems.at[piece], wout_sems.at[4], place).wait_send()
+            remote(gain_own, gain_recv.at[0], wout_sems.at[8 + piece], wout_sems.at[12], place).wait_send()
+
+
+POST_SENDS = 8 + 28 + 6 + 7 + 15 + 31 + 6 + 31
+
+
+def row_backward(*operands):
+    length, width = 1024, 1024
+    any_spec = pl.BlockSpec(memory_space=pl.ANY)
+    vmem = pl.BlockSpec(memory_space=pltpu.VMEM)
+    smem = pl.BlockSpec(memory_space=pltpu.SMEM)
+    shape = jax.ShapeDtypeStruct
+    dma = pltpu.SemaphoreType.DMA
+    return pl.pallas_call(
+        backward_kernel,
+        out_shape=(
+            shape((128, width), WIDE),
+            shape((32, 2048), WIDE),
+            shape((32, 1024), WIDE),
+            shape((32, 1024), WIDE),
+            shape((64, 1024), WIDE),
+            shape((8, 1024), WIDE),
+            shape((8, 384), WIDE),
+            shape((32, 3072), WIDE),
+            shape((32, 3072), WIDE),
+            shape((96, 1024), WIDE),
+        ),
+        in_specs=[vmem] * 15 + [any_spec] * 4 + [vmem] * 4 + [smem] * 3,
+        out_specs=(vmem,) * 10,
+        scratch_shapes=[
+            pltpu.VMEM((256, width), LOW),
+            pltpu.VMEM((width, 2048), LOW),
+            pltpu.VMEM((width, 1024), LOW),
+            pltpu.VMEM((width, 1024), LOW),
+            pltpu.VMEM((16, 64, width), LOW),
+            pltpu.VMEM((length, width), LOW),
+            pltpu.VMEM((8, 384, 128), LOW),
+            pltpu.VMEM((8, 128, width), LOW),
+            pltpu.VMEM((8, 128, width), LOW),
+            pltpu.VMEM((8, 128, 768), LOW),
+            pltpu.VMEM((8, 384, 128), LOW),
+            pltpu.VMEM((8, 8, 1024), WIDE),
+            pltpu.VMEM((4, 8, 1024), WIDE),
+            pltpu.VMEM((8, 2 * TILE, HD), LOW),
+            pltpu.VMEM((HD, length), LOW),
+            pltpu.VMEM((length, 2 * HD), WIDE),
+            pltpu.VMEM((length, 2 * HD), WIDE),
+            pltpu.VMEM((16, 64, 512), LOW),
+            pltpu.VMEM((8, 8, length), WIDE),
+            pltpu.VMEM((16, 64, 512), LOW),
+            pltpu.VMEM((8, 2, 64, 512), LOW),
+            pltpu.VMEM((128, 4096), LOW),
+            pltpu.VMEM((length, 512), LOW),
+            pltpu.VMEM((32, 32, 512), LOW),
+            pltpu.VMEM((256, width), LOW),
+            pltpu.VMEM((4, 64, width), LOW),
+            pltpu.VMEM((8, 384), WIDE),
+            pltpu.VMEM((4, 8, 384), WIDE),
+            pltpu.VMEM((1024, 768), LOW),
+            pltpu.VMEM((4, 8, 32, 768), LOW),
+            pltpu.VMEM((384, width), LOW),
+            pltpu.VMEM((4, 96, width), LOW),
+            dma((11,)),
+            dma((GATHER_SENDS,)),
+            dma((GATHER_RECVS,)),
+            dma((POST_SENDS,)),
+            dma((6, 8)),
+            dma((2, 4)),
+            dma((8,)),
+            dma((16,)),
+            dma((32,)),
+            dma((16,)),
+            dma((4, 8)),
+            dma((1,)),
+        ],
+        compiler_params=pltpu.CompilerParams(
+            collective_id=1, has_side_effects=True, vmem_limit_bytes=60 * 2**20
+        ),
+        name="row_backward",
+    )(*operands)
 
 
 def rope_tables(rot_places, head_size):
@@ -301,41 +1000,94 @@
     )
 
 
+def rms_forward(inputs, gain_vec):
+    factor = lax.rsqrt(jnp.mean(inputs * inputs, axis=-1, keepdims=True) + EPSILON)
+    normal = inputs * factor
+    return (normal * gain_vec, normal, factor)
+
+
+def rms_backward(grad_in, gain_vec, normal, factor):
+    weighted = grad_in * gain_vec
+    gain_grad = jnp.sum(grad_in * normal, axis=0)
+    inner_mean = jnp.mean(weighted * normal, axis=-1, keepdims=True)
+    return (factor * (weighted - normal * inner_mean), gain_grad)
+
+
+def split_by_heads(
+    tokens, cotangent, w_query, w_key, w_value, w_out, q_gain, k_gain, attn_gain,
+    w_gate, w_up, w_down, mlp_gain, doc_lengths, block_order,
+):
+    micro_count, _, block_len, width = tokens.shape
+    own_tokens = tokens[:, 0]
+    flat_tokens = tokens.reshape(micro_count * block_len, width)
+    out_grad = cotangent.reshape(micro_count * block_len, width).astype(WIDE)
+    first = doc_lengths[:, 0, 0]
+    cos, sine = rope_constants(1024)
+    index = jnp.arange(16, dtype=jnp.int32)
+    inverse = jnp.sum(jnp.where(block_order[None, :] == index[:, None], index[None, :], 0), axis=1).astype(jnp.int32)
+    q_gain_rows, k_gain_rows = q_gain.reshape(16, HD), k_gain.reshape(8, HD)
+    att_tok, tok_nat, q_pair, kv_nat, hat, factors, lse, att_nat = row_forward(
+        own_tokens, w_query, w_key, w_value, q_gain_rows, k_gain_rows, cos, sine, block_order, inverse, first
+    )
+    attn_proj = dot(att_tok.reshape(micro_count * block_len, -1), w_out)
+    attn_normed, attn_hat, attn_factor = rms_forward(attn_proj, attn_gain)
+    hidden = flat_tokens.astype(WIDE) + attn_normed
+    hidden_low = hidden.astype(LOW)
+    gate_pre = dot(hidden_low, w_gate)
+    up_pre = dot(hidden_low, w_up)
+    sigmoid_gate = jax.nn.sigmoid(gate_pre)
+    mixed_low = (gate_pre * sigmoid_gate * up_pre).astype(LOW)
+    down_pre = dot(mixed_low, w_down)
+    down_normed, down_hat, down_factor = rms_forward(down_pre, mlp_gain)
+    layer_out = (hidden + down_normed).astype(LOW).reshape(tokens.shape)
+    down_grad, grad_mlp_gain = rms_backward(out_grad, mlp_gain, down_hat, down_factor)
+    down_grad = down_grad.astype(LOW)
+    mixed_grad = dot_nt(down_grad, w_down)
+    gate_grad = (mixed_grad * up_pre * sigmoid_gate * (1.0 + gate_pre * (1.0 - sigmoid_gate))).astype(LOW)
+    up_grad = (mixed_grad * gate_pre * sigmoid_gate).astype(LOW)
+    hidden_grad = out_grad + dot_nt(gate_grad, w_gate) + dot_nt(up_grad, w_up)
+    proj_grad, grad_attn_gain = rms_backward(hidden_grad, attn_gain, attn_hat, attn_factor)
+    proj_grad = proj_grad.astype(LOW).reshape(micro_count, block_len, width)
+    vec = jnp.concatenate([grad_attn_gain[None], grad_mlp_gain[None], jnp.zeros((6, width), WIDE)], axis=0)
+    in_grad, g_query, g_key, g_value, g_out, vec_sum, gain_sum, g_gate, g_up, g_down = row_backward(
+        proj_grad, hidden_low, down_grad, gate_grad, up_grad, mixed_low, hidden_grad, vec,
+        tok_nat, q_pair, kv_nat, hat, factors, lse, att_nat,
+        w_out, w_query, w_key, w_value, q_gain_rows, k_gain_rows, cos, sine, block_order, inverse, first,
+    )
+    seq = lax.axis_index("seq")
+    me = lax.axis_index("dp") * 16 + seq
+    part = seq % 4
+    return (
+        layer_out,
+        in_grad.reshape(tokens.shape),
+        g_query,
+        g_key,
+        g_value,
+        g_out,
+        lax.dynamic_slice(gain_sum, (0, part * 64), (1, 64))[0],
+        lax.dynamic_slice(gain_sum, (0, 256 + part * 32), (1, 32))[0],
+        lax.dynamic_slice(vec_sum, (0, me * 32), (1, 32))[0],
+        g_gate,
+        g_up,
+        g_down,
+        lax.dynamic_slice(vec_sum, (1, me * 32), (1, 32))[0],
+    )
+
+
+SPECS_IN = (
+    P(None, "dp", "seq", None), P(None, "dp", "seq", None),
+    P(), P(), P(), P(), P(), P(), P(), P(), P(), P(), P(),
+    P(None, "dp", None), P(),
+)
+SPECS_OUT = (
+    P(None, "dp", "seq", None), P(None, "dp", "seq", None),
+    P(("dp", "seq"), None), P(("dp", "seq"), None), P(("dp", "seq"), None), P(("dp", "seq"), None),
+    P(("dp", "seq")), P(("dp", "seq")), P(("dp", "seq")),
+    P(("dp", "seq"), None), P(("dp", "seq"), None), P(("dp", "seq"), None),
+    P(("dp", "seq")),
+)
+
+
 def solution(mesh):
-    return jax.shard_map(
-        on_device,
-        mesh=mesh,
-        in_specs=(
-            P(None, "dp", "seq", None),
-            P(None, "dp", "seq", None),
-            P(),
-            P(),
-            P(),
-            P(),
-            P(),
-            P(),
-            P(),
-            P(),
-            P(),
-            P(),
-            P(),
-            P(None, "dp", None),
-            P(),
-        ),
-        out_specs=(
-            P(None, "dp", "seq", None),
-            P(None, "dp", "seq", None),
-            P(("dp", "seq"), None),
-            P(("dp", "seq"), None),
-            P(("dp", "seq"), None),
-            P(("dp", "seq"), None),
-            P(("dp", "seq")),
-            P(("dp", "seq")),
-            P(("dp", "seq")),
-            P(("dp", "seq"), None),
-            P(("dp", "seq"), None),
-            P(("dp", "seq"), None),
-            P(("dp", "seq")),
-        ),
-        check_vma=False,
-    )
+    body = split_by_heads if mesh.shape["seq"] == 16 and mesh.shape["dp"] == 2 else on_device
+    return jax.shard_map(body, mesh=mesh, in_specs=SPECS_IN, out_specs=SPECS_OUT, check_vma=False)

time: 1740 us -> 309 us (0.18)
  waiting for transfers between devices: 1290 us -> 0 us
  Pallas kernels: 0 us -> 272 us
  matrix products: 206 us -> 14.1 us
  local copies, waits for them, and re-layouts: 152 us -> 15 us
  blocking collectives: 40.5 us -> 0 us
  other arithmetic: 21.2 us -> 3.67 us
    reduce_scatter x8 -> x0, waiting for transfers between devices: 907 us -> none  [the longest x1 162 us: on_device(): lax.psum_scatter(grad_w_gate, ('dp', 'seq'), scatter_dimension=0, tiled=T...]
    unnamed x12 -> x0, waiting for transfers between devices: 305 us -> none
    pallas_call x0 -> x2, Pallas kernels: none -> 272 us  [the longest x1 212 us: row_backward(): pl.pallas_call(backward_kernel, out_shape=(shape((128, width), WIDE), sha...]
    dot_general x133 -> x7, matrix products: 206 us -> 14.1 us  [the longest x3 7.31 us: dot_nt(): lax.dot_general(left, right, (((1,), (1,)), ((), ())), preferred_element_...]
    all_gather x2 -> x0, waiting for transfers between devices: 82.6 us -> none  [the longest x1 45.8 us: on_device(): lax.all_gather(v_blocks, 'seq', axis=1, tiled=True)]
    unnamed x1 -> x0, blocking collectives: 40.5 us -> none
    unnamed x111 -> x48, local copies, waits for them, and re-layouts: 45.2 us -> 11 us
    dynamic_slice x43 -> x0, local copies, waits for them, and re-layouts: 24.8 us -> none  [the longest x10 23 us: on_device(): lax.map(forward_block, (q_blocks, key_all, value_all, allowed))]
  transfers between devices with their start and end apart: 13 -> 0, of which waited for: 13 -> 0; matrix products, arithmetic and copies ran while one was open for 7% -> 0% of each run, Pallas kernels for 0% -> 0%
where the time goes in v1:
time: 309 us; the launch traced here: 306 us
  Pallas kernels  272 us (88%)
  local copies, waits for them, and re-layouts  15 us (5%)
  matrix products  14.1 us (5%)
  other arithmetic  3.67 us (1%)
    pallas_call x1, Pallas kernels, row_backward(): pl.pallas_call(backward_kernel, out_shape=(shape((128, width), WIDE), sha...  212 us
    pallas_call x1, Pallas kernels, row_forward(): pl.pallas_call(forward_kernel, out_shape=(shape((2, 64, 2048), LOW), shap...  60.3 us
    unnamed x48, local copies, waits for them, and re-layouts  11 us
    dot_general x3, matrix products, dot_nt(): lax.dot_general(left, right, (((1,), (1,)), ((), ())), preferred_element_...  7.31 us
    dot_general x4, matrix products, dot(): return jnp.dot(left, right, preferred_element_type=WIDE)  6.82 us

profile of v1, /device:TPU:0, one launch (start us, length us, event | category | flops | bytes accessed | tf_op | source)
XLA Modules:
  0.0 305.7 jit_solution(14363596470841703528)
XLA Ops:
  0.6 1.3 select_reduce_fusion.inverse_ref
  1.9 1.3 slice_reduce_fusion.first_ref
  3.2 60.3 %row_forward.1 = (bf16[2,64,2048]{2,1,0:T(8,128)(2,1)}, bf16[1024,1024]{1,0:T(8,128)(2,1)}, bf16[8,256,128]{2,1,0:T(8,128)(2,1)}, bf16[1024,256]{1,0:T(8,128)(2,...) custom-call(bf16[2,64,1024]{2,1,0:T(8,128)(2,1)} %bitcast.51, ...), custom_call_target="tpu_custom_call" | custom-call | tf_op jit(solution)/shard_map/row_forward/pallas_call | solution.py:292
  63.6 3.3 %multiply_reduce_fusion.3 = (f32[128]{0:T(128)S(1)}, f32[128,1024]{1,0:T(8,128)S(1)}) fusion(bf16[128,2048]{1,0:T(8,128)(2,1)} %bitcast.54, bf16[2048,1024]{1,0:T(8,128)(2,1)} %wout_hbm.1), kind=kOutput, calls=%fused_computation.20 | convolution fusion | flops 537132928 | bytes 5243392 | tf_op jit(solution)/shard_map/dot_general | solution.py:34
  67.1 1.0 fusion.10
  68.1 0.7 slice-done.5
  68.8 1.4 multiply_convert_fusion.2
  70.8 1.1 multiply_reduce_fusion.2
  72.5 2.6 multiply_convert_fusion
  75.1 2.4 convolution_add_fusion.1
  77.5 2.4 multiply_reduce_fusion
  79.9 0.7 maximum_maximum_fusion.vec_ref
  80.6 1.1 multiply_convert_fusion.3
  81.7 211.6 %row_backward.1 = (f32[128,1024]{1,0:T(8,128)}, f32[32,2048]{1,0:T(8,128)}, f32[32,1024]{1,0:T(8,128)}, f32[32,1024]{1,0:T(8,128)}, f32[64,1024]{1,0:T(8,128)}, ...) custom-call(bf16[2,64,1024]{2,1,0:T(8,128)(2,1)} %bitcast.52, ...), custom_call_target="tpu_custom_call" | custom-call | tf_op jit(solution)/shard_map/row_backward/pallas_call | solution.py:657
  293.3 1.4 dynamic-slice_bitcast_fusion
  294.7 1.3 fusion.7
  296.0 1.9 copy.44
  297.9 1.7 copy.45
  299.6 1.6 copy.46
  301.1 1.6 copy.47
  302.7 0.7 copy.48
  303.4 0.7 copy.49
  304.2 0.7 copy.50
  304.9 0.7 copy.51
  (51 shorter events, 1.3 us)
Async XLA Ops:
  3.2 63.8 %slice-start = ((s8[6291456]{0:T(1024)(128)(4,1)}), s8[4194304]{0:T(1024)(128)(4,1)S(1)}, s32[]{:S(2)}) async-start(s8[6291456]{0:T(1024)(128)(4,1)} %bitcast.44), calls=%async_computation | async-start | bytes 8388608
  3.2 63.8 %slice-start.1 = ((s8[6291456]{0:T(1024)(128)(4,1)}), s8[2097152]{0:T(1024)(128)(4,1)S(1)}, s32[]{:S(2)}) async-start(s8[6291456]{0:T(1024)(128)(4,1)} %bitcast.44), calls=%async_computation.1 | async-start | bytes 4194304
  63.5 3.3 %copy-start.6 = (bf16[2,1,64,1024]{3,2,1,0:T(8,128)(2,1)S(1)}, bf16[2,1,64,1024]{3,2,1,0:T(8,128)(2,1)}, u32[]{:S(2)}) copy-start(bf16[2,1,64,1024]{3,2,1,0:T(8,128)(2,1)} %param.17) | copy-start | bytes 786436
  63.5 3.3 %copy-start.12 = (f32[1024]{0:T(1024)S(1)}, f32[1024]{0:T(1024)}, u32[]{:S(2)}) copy-start(f32[1024]{0:T(1024)} %param.25) | copy-start | bytes 12292
  63.6 4.6 %slice-start.4 = ((s8[6291456]{0:T(1024)(128)(4,1)}), s8[4194304]{0:T(1024)(128)(4,1)S(1)}, s32[]{:S(2)}) async-start(s8[6291456]{0:T(1024)(128)(4,1)} %bitcast.48), calls=%async_computation.4 | async-start | bytes 8388608
  67.1 1.0 copy-start.2
  67.1 1.7 slice-start.5
  67.1 3.2 %slice-start.2 = ((s8[6291456]{0:T(1024)(128)(4,1)}), s8[4194304]{0:T(1024)(128)(4,1)S(1)}, s32[]{:S(2)}) async-start(s8[6291456]{0:T(1024)(128)(4,1)} %bitcast.46), calls=%async_computation.2 | async-start | bytes 8388608
  68.8 2.0 slice-start.3
  70.2 1.7 copy-start
  70.8 1.2 copy-start.5
  70.8 1.2 copy-start.13
  72.5 2.6 copy-start.7
  75.1 2.4 copy-start.4
  75.1 2.4 copy-start.3
  79.8 1.9 copy-start.1
  293.3 9.4 %copy-start.11 = (f32[64,1024]{1,0:T(8,128)S(1)}, f32[64,1024]{1,0:T(8,128)}, u32[]{:S(2)}) copy-start(f32[64,1024]{1,0:T(8,128)} %get-tuple-element.124) | copy-start | bytes 786436
  293.3 10.1 %copy-start.10 = (f32[32,3072]{1,0:T(8,128)S(1)}, f32[32,3072]{1,0:T(8,128)}, u32[]{:S(2)}) copy-start(f32[32,3072]{1,0:T(8,128)} %get-tuple-element.128) | copy-start | bytes 1179652
  293.3 10.9 %copy-start.9 = (f32[32,3072]{1,0:T(8,128)S(1)}, f32[32,3072]{1,0:T(8,128)}, u32[]{:S(2)}) copy-start(f32[32,3072]{1,0:T(8,128)} %get-tuple-element.129) | copy-start | bytes 1179652
  296.0 8.9 %copy-start.8 = (f32[96,1024]{1,0:T(8,128)S(1)}, f32[96,1024]{1,0:T(8,128)}, u32[]{:S(2)}) copy-start(f32[96,1024]{1,0:T(8,128)} %get-tuple-element.130) | copy-start | bytes 1179652

commit v2 on v1

--- a/solution.py
+++ b/solution.py
@@ -158,12 +158,23 @@
     return (keys >= earliest) & (keys <= queries)
 
 
+def invert(order_ref, inverse_ref):
+    def fill(block, carry):
+        place = jnp.int32(0)
+        for slot in range(16):
+            place = jnp.maximum(place, jnp.where(order_ref[slot] == block, slot, 0))
+        inverse_ref[block] = place
+        return carry
+
+    lax.fori_loop(0, 16, fill, 0)
+
+
 def forward_kernel(
     tok_ref, wq_hbm, wk_hbm, wv_hbm, qgain_ref, kgain_ref, cos_ref, sine_ref,
-    order_ref, inverse_ref, first_ref,
-    att_tok, tok_nat, q_pair, kv_nat, hat, factors, lse, att_nat,
-    tok_all, w_own, stat_all, att_send, att_recv, kv_turned,
-    local_sems, send_sems, recv_sems, stat_send, stat_recv, att_ssem, att_rsem,
+    order_ref, docs_ref,
+    att_tok, tok_nat, q_pair, kv_nat, hat, factors, lse,
+    att_nat, tok_all, w_own, stat_all, att_send, att_recv, kv_turned,
+    inverse_ref, local_sems, send_sems, recv_sems, stat_send, stat_recv, att_ssem, att_rsem,
 ):
     spot = Spot()
     devices = 16
@@ -179,12 +190,13 @@
     greet_row(spot, devices)
     gather = RowGather(spot, tok_ref, tok_all, local_sems.at[0], send_sems, recv_sems)
     gather.start()
+    invert(order_ref, inverse_ref)
     gather.forward()
     for load in loads:
         load.wait()
     gather.finish()
 
-    first_length = first_ref[spot.core]
+    first_length = docs_ref[spot.core, 0, 0]
     for part in range(4):
         rows = pl.ds(part * CHUNK, CHUNK)
         chunk = jnp.concatenate([tok_all[inverse_ref[part * 4 + piece]] for piece in range(4)], axis=0)
@@ -282,7 +294,7 @@
     return jnp.asarray(cos, WIDE), jnp.asarray(sine, WIDE)
 
 
-def row_forward(tokens, w_query, w_key, w_value, q_gain, k_gain, cos, sine, order, inverse, first):
+def row_forward(tokens, w_query, w_key, w_value, q_gain, k_gain, cos, sine, order, docs):
     length = 1024
     width = tokens.shape[-1]
     any_spec = pl.BlockSpec(memory_space=pl.ANY)
@@ -299,17 +311,18 @@
             shape((length, 3 * HD), WIDE),
             shape((8, length), WIDE),
             shape((8, 2 * TILE), WIDE),
-            shape((16, 64, 2 * HD), LOW),
         ),
-        in_specs=[vmem, any_spec, any_spec, any_spec, vmem, vmem, vmem, vmem, smem, smem, smem],
-        out_specs=(vmem,) * 8,
+        in_specs=[vmem, any_spec, any_spec, any_spec, vmem, vmem, vmem, vmem, smem, smem],
+        out_specs=(vmem,) * 7,
         scratch_shapes=[
+            pltpu.VMEM((16, 64, 2 * HD), LOW),
             pltpu.VMEM((16, 64, width), LOW),
             pltpu.VMEM((width, 512), LOW),
             pltpu.VMEM((8, 8, length), WIDE),
             pltpu.VMEM((16, 64, 2 * HD), LOW),
             pltpu.VMEM((8, 2, 64, 2 * HD), LOW),
             pltpu.VMEM((HD, length), LOW),
+            pltpu.SMEM((16,), jnp.int32),
             pltpu.SemaphoreType.DMA((4,)),
             pltpu.SemaphoreType.DMA((GATHER_SENDS,)),
             pltpu.SemaphoreType.DMA((GATHER_RECVS,)),
@@ -322,38 +335,98 @@
             collective_id=0, has_side_effects=True, vmem_limit_bytes=56 * 2**20
         ),
         name="row_forward",
-    )(tokens, w_query, w_key, w_value, q_gain, k_gain, cos, sine, order, inverse, first)
+    )(tokens, w_query, w_key, w_value, q_gain, k_gain, cos, sine, order, docs)
 
 
 class Post:
     def __init__(self, sems):
-        self.sems, self.started = sems, []
-
-    def send(self, source, target, recv_sem, place):
-        copy = remote(source, target, self.sems.at[len(self.started)], recv_sem, place)
-        copy.start()
-        self.started.append(copy)
+        self.sems, self.started, self.used = sems, [], 0
+
+    def send(self, source, target, recv_sem, place, when=None):
+        copy = remote(source, target, self.sems.at[self.used], recv_sem, place)
+        self.used += 1
+        self.started.append((copy, when))
+        if when is None:
+            copy.start()
+        else:
+            pl.when(when)(copy.start)
 
     def finish(self):
-        for copy in self.started:
-            copy.wait_send()
+        for copy, when in self.started:
+            if when is None:
+                copy.wait_send()
+            else:
+                pl.when(when)(copy.wait_send)
 
 
 def arrived(spot, slot, recv_sem, spare_sem):
     remote(slot, slot, spare_sem, recv_sem, (spot.dp, spot.sibling)).wait_recv()
 
 
+def aligned(start, size):
+    return pl.ds(pl.multiple_of(start, size), size)
+
+
+class AlongZ:
+    def __init__(self, spot, post, spare):
+        self.spot, self.post, self.spare = spot, post, spare
+        half = spot.z // 2
+        self.partner = spot.far_z[0]
+        self.far_inner = 2 - half
+        self.far_outer = 3 - 3 * half
+        self.inner = ((spot.z + 1) // 2) % 2 == 1
+        self.outer = ((spot.z + 1) // 2) % 2 == 0
+
+    def place(self, z):
+        return (self.spot.dp, z * 4 + self.spot.x * 2 + self.spot.core)
+
+    def send(self, part, size, landing, transit, sems):
+        spot, post = self.spot, self.post
+        landing[2] = part[aligned(spot.z * size, size), :]
+        post.send(part.at[aligned(self.partner * size, size)], landing.at[0], sems.at[0], self.place(self.partner))
+        for slot, far in enumerate((self.far_inner, self.far_outer)):
+            post.send(
+                part.at[aligned(far * size, size)], transit.at[slot], sems.at[2 + slot], self.place(self.partner),
+                self.outer,
+            )
+
+    def combine(self, part, size, landing, transit, sems):
+        for slot, far in enumerate((self.far_inner, self.far_outer)):
+
+            @pl.when(self.inner)
+            def _():
+                arrived(self.spot, transit.at[slot], sems.at[2 + slot], self.spare)
+                added = transit[slot].astype(WIDE) + part[aligned(far * size, size), :].astype(WIDE)
+                transit[slot] = added.astype(LOW)
+
+            self.post.send(transit.at[slot], landing.at[1], sems.at[1], self.place(far), self.inner)
+
+    def total(self, landing, sems):
+        arrived(self.spot, landing.at[0], sems.at[0], self.spare)
+        arrived(self.spot, landing.at[1], sems.at[1], self.spare)
+        return landing[0].astype(WIDE) + landing[1].astype(WIDE) + landing[2].astype(WIDE)
+
+
+def row_scale(values):
+    return lax.rsqrt(jnp.mean(values * values, axis=-1, keepdims=True) + EPSILON)
+
+
+def norm_back(grad, gain, normal, factor):
+    weighted = grad * gain
+    return factor * (weighted - normal * jnp.mean(weighted * normal, axis=-1, keepdims=True))
+
+
 def backward_kernel(
-    proj_ref, hid_ref, down_ref, gate_ref, up_ref, mixed_ref, hgrad_ref, vec_ref,
-    tok_nat, q_pair, kv_nat, hat, factors, lse, att_nat,
-    wout_hbm, wq_hbm, wk_hbm, wv_hbm, qgain_ref, kgain_ref, cos_ref, sine_ref,
-    order_ref, inverse_ref, first_ref,
-    in_grad, g_query, g_key, g_value, g_out, vec_out, gain_out, g_gate, g_up, g_down,
-    wout_own, wq_all, wk_all, wv_all,
-    proj_all, proj_nat, mix_turned, hid_all, down_all, gu_all, mix_all, vec_all, vec_far,
-    ag_pair, k_turned, dq, dkv, grad_nat, stat_all, grad_send, grad_recv, grad_tok,
-    part_low, wqkv_recv, wout_low, wout_recv, gain_own, gain_recv, gu_low, gu_recv, down_low, down_recv,
-    local_sems, send_sems, recv_sems, post_sems, plane_sems, far_sems, stat_sems, grad_sems, wqkv_sems, wout_sems, gu_sems, self_sems,
+    att_ref, tok_ref, cot_ref, again_ref, mgain_ref, qgain_ref, kgain_ref, factors, lse,
+    tok_hbm, q_hbm, kv_hbm, hat_hbm, cos_hbm, sine_hbm,
+    wout_hbm, wg_hbm, wu_hbm, wd_hbm, wq_hbm, wk_hbm, wv_hbm, order_ref, docs_ref,
+    layer_out, in_grad, g_query, g_key, g_value, g_out, vec_out, gain_out, g_gate, g_up, g_down,
+    wout, wgate, wup, wdown, q_pair, kv_nat, hat, cos_ref, sine_ref,
+    att_hat, hidden, hid_own, gate_pre, up_pre, mixed, mix_turned, att_turned, down_own, gu_own, proj_own, ag_own, vec_own,
+    hid_all, down_all, proj_all, gu_all, mix_all, att_all, vec_all, vec_far,
+    down_land, down_transit, wout_part, wout_land, wout_transit, gu_land, gu_transit,
+    ag_recv, ag_pair, k_turned, stat_all, grad_nat, grad_recv, part_sib, wqkv_recv, gain_own, gain_recv,
+    inverse_ref, local_sems, post_sems, plane_sems, vec_sems, down_sems, wout_sems, gu_sems, gut_sems, ag_sems, stat_sems, grad_sems, sib_sem, wqkv_sems, gain_sems,
 ):
     spot = Spot()
     devices, chips = 16, 8
@@ -361,28 +434,39 @@
     me = dp * devices + seq
     member = dp * 4 + spot.x * 2 + core
     spare = post_sems.at[0]
-    loads = [
-        pltpu.make_async_copy(wout_hbm.at[pl.ds(pl.multiple_of(chip * 256, 256), 256)], wout_own, local_sems.at[1]),
-        pltpu.make_async_copy(wq_hbm, wq_all, local_sems.at[2]),
-        pltpu.make_async_copy(wk_hbm, wk_all, local_sems.at[3]),
-        pltpu.make_async_copy(wv_hbm, wv_all, local_sems.at[4]),
-    ]
-    for load in loads:
-        load.start()
+    post = Post(post_sems)
+    along = AlongZ(spot, post, spare)
+
+    def load(source, target, index):
+        copy = pltpu.make_async_copy(source, target, local_sems.at[index])
+        copy.start()
+        return copy
+
     barrier = pltpu.get_barrier_semaphore()
     for step in range(1, 2 * devices):
         other = (me + step) % (2 * devices)
         pl.semaphore_signal(barrier, inc=1, device_id=(other // devices, other % devices), device_id_type=MESH)
+    load_out = load(wout_hbm, wout, 0)
+    load_gate = load(wg_hbm, wgate, 1)
+    load_up = load(wu_hbm, wup, 2)
+    load_down = load(wd_hbm, wdown, 3)
+    later = [load(kv_hbm, kv_nat, 4), load(q_hbm, q_pair, 5), load(hat_hbm, hat, 6), load(cos_hbm, cos_ref, 7), load(sine_hbm, sine_ref, 8)]
+    invert(order_ref, inverse_ref)
+
     for group in range(8):
-        block = mixed_ref[:, group * 384 : (group + 1) * 384].T
+        block = att_ref[:, :, group * 256 : (group + 1) * 256].reshape(128, 256).T
         for piece in range(4):
-            mix_turned[(group // 4) * 4 + piece, pl.ds((group % 4) * 96, 96), :] = block[piece * 96 : (piece + 1) * 96]
+            att_turned[(group // 4) * 4 + piece, pl.ds((group % 4) * 64, 64), :] = block[piece * 64 : (piece + 1) * 64]
+    load_out.wait()
+    attn_proj = dot(att_ref[...].reshape(128, 2048), wout[...])
+    att_factor = row_scale(attn_proj)
+    normal = attn_proj * att_factor
+    att_hat[...] = normal
+    stream = tok_ref[...].reshape(128, 1024).astype(WIDE) + normal * again_ref[...]
+    hidden[...] = stream
+    hid_own[...] = stream.astype(LOW)
     pl.semaphore_wait(barrier, 2 * devices - 1)
 
-    gather = RowGather(spot, proj_ref, proj_all, local_sems.at[0], send_sems, recv_sems)
-    gather.start()
-
-    post = Post(post_sems)
     plane_places = ((dp, spot.flip_x), (1 - dp, seq), (1 - dp, spot.flip_x))
     plane_members = (
         dp * 4 + (1 - spot.x) * 2 + core,
@@ -390,68 +474,125 @@
         (1 - dp) * 4 + (1 - spot.x) * 2 + core,
     )
     sib_place = (dp, spot.sibling)
-    keeps = [
-        pltpu.make_async_copy(hid_ref, hid_all.at[member], local_sems.at[5]),
-        pltpu.make_async_copy(down_ref, down_all.at[member], local_sems.at[6]),
-        pltpu.make_async_copy(gate_ref.at[:, pl.ds(pl.multiple_of(member * 384, 128), 384)], gu_all.at[member, :, pl.ds(0, 384)], local_sems.at[7]),
-        pltpu.make_async_copy(up_ref.at[:, pl.ds(pl.multiple_of(member * 384, 128), 384)], gu_all.at[member, :, pl.ds(384, 384)], local_sems.at[8]),
-        pltpu.make_async_copy(mix_turned.at[member], mix_all.at[member], local_sems.at[9]),
-        pltpu.make_async_copy(vec_ref, vec_all.at[member], local_sems.at[10]),
-    ]
-    for keep in keeps:
-        keep.start()
-    for place in plane_places:
-        post.send(hid_ref, hid_all.at[member], plane_sems.at[0, member], place)
-        post.send(down_ref, down_all.at[member], plane_sems.at[1, member], place)
-    post.send(hid_ref, hid_all.at[member], plane_sems.at[0, member], sib_place)
-    post.send(down_ref, down_all.at[member], plane_sems.at[1, member], sib_place)
+    keeps = {}
+
+    def spread(own, held, kind, index):
+        keeps[kind] = load(own, held.at[member], index)
+        for place in plane_places + (sib_place,):
+            post.send(own, held.at[member], plane_sems.at[kind, member], place)
+
+    def pass_on(held, kind):
+        for other in plane_members:
+            arrived(spot, held.at[other], plane_sems.at[kind, other], spare)
+            post.send(held.at[other], held.at[other], plane_sems.at[kind, other], sib_place)
+
+    def whole(held, kind):
+        keeps[kind].wait()
+        for y in range(2):
+            for x in range(2):
+                other = y * 4 + x * 2 + 1 - core
+                arrived(spot, held.at[other], plane_sems.at[kind, other], spare)
+
+    def deal(own, held, kind, index):
+        keeps[kind] = load(own.at[member], held.at[member], index)
+        for step in range(1, 8):
+            other = (member + step) % 8
+            post.send(own.at[other], held.at[member], plane_sems.at[kind, member], (other // 4, z * 4 + other % 4))
+
+    def dealt(held, kind):
+        keeps[kind].wait()
+        for step in range(1, 8):
+            other = (member + step) % 8
+            arrived(spot, held.at[other], plane_sems.at[kind, other], spare)
+
+    spread(hid_own, hid_all, 0, 9)
+    deal(att_turned, att_all, 3, 10)
+
+    load_gate.wait()
+    load_up.wait()
+    for group in range(8):
+        lanes = slice(group * 384, (group + 1) * 384)
+        gate = dot(hid_own[...], wgate[:, lanes])
+        up = dot(hid_own[...], wup[:, lanes])
+        gate_pre[group] = gate
+        up_pre[group] = up
+        block = (gate * jax.nn.sigmoid(gate) * up).astype(LOW)
+        mixed[:, lanes] = block
+        turned = block.T
+        for piece in range(4):
+            mix_turned[(group // 4) * 4 + piece, pl.ds((group % 4) * 96, 96), :] = turned[piece * 96 : (piece + 1) * 96]
+    deal(mix_turned, mix_all, 4, 11)
+    load_down.wait()
+    down_pre = dot(mixed[...], wdown[...])
+    factor = row_scale(down_pre)
+    normal = down_pre * factor
+    cot = cot_ref[...].reshape(128, 1024).astype(WIDE)
+    layer_out[...] = (hidden[...] + normal * mgain_ref[...]).astype(LOW)
+    down_own[...] = norm_back(cot, mgain_ref[...], normal, factor).astype(LOW)
+    vec_own[...] = jnp.zeros_like(vec_own)
+    vec_own[1:2, :] = jnp.sum(cot * normal, axis=0, keepdims=True)
+    spread(down_own, down_all, 1, 12)
+
+    for step in range(1, 9):
+        group = (member + step) % 8
+        grad = dot_nt(down_own[...], wdown[aligned(group * 384, 384), :])
+        gate, up = gate_pre[group], up_pre[group]
+        sigmoid = jax.nn.sigmoid(gate)
+        gu_own[group, :, :384] = (grad * up * sigmoid * (1.0 + gate * (1.0 - sigmoid))).astype(LOW)
+        gu_own[group, :, 384:] = (grad * gate * sigmoid).astype(LOW)
+        if step < 8:
+            post.send(gu_own.at[group], gu_all.at[member], plane_sems.at[5, member], (group // 4, z * 4 + group % 4))
+    keeps[5] = load(gu_own.at[member], gu_all.at[member], 13)
+    hgrad = cot
+    for group in range(8):
+        lanes = slice(group * 384, (group + 1) * 384)
+        hgrad = hgrad + dot_nt(gu_own[group, :, :384], wgate[:, lanes]) + dot_nt(gu_own[group, :, 384:], wup[:, lanes])
+    hidden[...] = hgrad
+    normal = att_hat[...]
+    proj_own[...] = norm_back(hgrad, again_ref[...], normal, att_factor).astype(LOW)
+    vec_own[0:1, :] = jnp.sum(hgrad * normal, axis=0, keepdims=True)
+    load_query = load(wq_hbm, wgate.at[:, pl.ds(0, 2048)], 1)
+    load_key = load(wk_hbm, wgate.at[:, pl.ds(2048, 1024)], 2)
+    load_value = load(wv_hbm, wup.at[:, pl.ds(0, 1024)], 3)
+
+    att_grad = dot_nt(proj_own[...], wout[...]).astype(LOW)
+    ag_own[...] = att_grad.reshape(2, 64, 2048)
+    keep_ag = load(ag_own.at[core, :, aligned(chip * 256, 256)], ag_recv.at[seq], 14)
+    for step in range(1, devices):
+        other = (seq + step) % devices
+        post.send(
+            ag_own.at[other % 2, :, aligned((other // 2) * 256, 256)], ag_recv.at[seq], ag_sems.at[seq], (dp, other)
+        )
+    load_tok = load(tok_hbm, wout.at[pl.ds(0, 1024)], 0)
+    spread(proj_own, proj_all, 2, 15)
+    keep_vec = load(vec_own, vec_all.at[member], 16)
     for step in range(1, 8):
         other = (member + step) % 8
-        place = (other // 4, z * 4 + other % 4)
-        lanes = pl.ds(pl.multiple_of(other * 384, 128), 384)
-        post.send(mix_turned.at[other], mix_all.at[member], plane_sems.at[2, member], place)
-        post.send(gate_ref.at[:, lanes], gu_all.at[member, :, pl.ds(0, 384)], plane_sems.at[3, member], place)
-        post.send(up_ref.at[:, lanes], gu_all.at[member, :, pl.ds(384, 384)], plane_sems.at[4, member], place)
-        post.send(vec_ref, vec_all.at[member], plane_sems.at[5, member], place)
-
-    gather.forward()
-    for other in plane_members:
-        arrived(spot, hid_all.at[other], plane_sems.at[0, other], spare)
-        post.send(hid_all.at[other], hid_all.at[other], plane_sems.at[0, other], sib_place)
-        arrived(spot, down_all.at[other], plane_sems.at[1, other], spare)
-        post.send(down_all.at[other], down_all.at[other], plane_sems.at[1, other], sib_place)
-    gather.finish()
-
-    loads[0].wait()
-    for part in range(8):
-        rows = pl.ds(part * TILE, TILE)
-        chunk = jnp.concatenate([proj_all[inverse_ref[part * 2 + piece]] for piece in range(2)], axis=0)
-        proj_nat[rows, :] = chunk
-        att_grad = dot_nt(chunk, wout_own[...]).astype(LOW)
-        ag_pair[part, :TILE, :] = att_grad[:, :HD]
-        ag_pair[part, TILE:, :] = att_grad[:, HD:]
-    wout_low[...] = dot_tn(att_nat[...].reshape(1024, 2 * HD), proj_nat[...]).astype(LOW)
-    for piece in range(4):
-        target = chip * 4 + piece
-        rows = pl.ds(piece * 64, 64)
-        slot = wout_recv.at[dp * 2 + core]
-
-        @pl.when(target == me)
-        def _():
-            keep = pltpu.make_async_copy(wout_low.at[rows], slot, self_sems.at[0])
-            keep.start()
-            keep.wait()
-
-        @pl.when(target != me)
-        def _():
-            remote(
-                wout_low.at[rows], slot, wout_sems.at[piece], wout_sems.at[4 + dp * 2 + core],
-                (target // devices, target % devices),
-            ).start()
-
+        post.send(vec_own, vec_all.at[member], vec_sems.at[member], (other // 4, z * 4 + other % 4))
+    pass_on(hid_all, 0)
+    pass_on(down_all, 1)
+
+    dealt(mix_all, 4)
+    whole(down_all, 1)
+    down_part = wdown.at[pl.ds(0, 384)]
+    mixes = jnp.concatenate([mix_all[other] for other in range(8)], axis=1)
+    down_part[...] = dot(mixes, down_all[...].reshape(1024, 1024)).astype(LOW)
+    along.send(down_part, 96, down_land, down_transit, down_sems)
+    pass_on(proj_all, 2)
+
+    for copy in later:
+        copy.wait()
+    keep_ag.wait()
+    for step in range(1, devices):
+        other = (seq + step) % devices
+        arrived(spot, ag_recv.at[other], ag_sems.at[other], spare)
+    for tile in range(8):
+        block = jnp.concatenate([ag_recv[inverse_ref[tile * 2 + piece]] for piece in range(2)], axis=0)
+        ag_pair[tile, :TILE, :] = block[:, :HD]
+        ag_pair[tile, TILE:, :] = block[:, HD:]
     k_turned[...] = kv_nat[:, :HD].T
-    first_length = first_ref[core]
-    dkv[...] = jnp.zeros_like(dkv)
+    first_length = docs_ref[core, 0, 0]
+    up_pre[:, :, :256] = jnp.zeros((8, TILE, 256), WIDE)
     for tile in range(8):
         count = (tile + 1) * TILE
         queries, grads = q_pair[tile], ag_pair[tile]
@@ -461,12 +602,11 @@
         prob_grad = dot_nt(kv_nat[:count, HD:], grads)
         row_dot = jnp.sum(probs * prob_grad, axis=0, keepdims=True)
         score_grad = (probs * (prob_grad - row_dot)).astype(LOW)
-        dkv[:count, :HD] += dot(score_grad, queries)
-        dkv[:count, HD:] += dot(probs.astype(LOW), grads)
+        up_pre[: tile + 1, :, :HD] += dot(score_grad, queries).reshape(tile + 1, TILE, HD)
+        up_pre[: tile + 1, :, HD:256] += dot(probs.astype(LOW), grads).reshape(tile + 1, TILE, HD)
         turned = (dot(k_turned[:, :count], score_grad) * HD ** (-0.5)).T
-        rows = pl.ds(tile * TILE, TILE)
-        dq[rows, :HD] = turned[:TILE]
-        dq[rows, HD:] = turned[TILE:]
+        gate_pre[tile, :, :HD] = turned[:TILE]
+        gate_pre[tile, :, HD:256] = turned[TILE:]
 
     qgain = qgain_ref[pl.ds(chip * 2, 2), :]
     kgain = kgain_ref[pl.ds(chip, 1), :]
@@ -477,16 +617,17 @@
         sine = jnp.concatenate([rope_rows(sine_ref, part * 2 + piece, first_length) for piece in range(2)], axis=0)
         dots = []
         for head in range(3):
-            turned = dq[rows, pl.ds(head * HD, HD)] if head < 2 else dkv[rows, :HD] * HD ** (-0.5)
+            lanes = slice(head * HD, (head + 1) * HD)
+            turned = gate_pre[part, :, lanes] if head < 2 else up_pre[part, :, :HD] * HD ** (-0.5)
             back = turned * cos - swap_halves(turned) * sine
-            normal = hat[rows, pl.ds(head * HD, HD)]
+            normal = hat[rows, lanes]
             gain = qgain[head : head + 1] if head < 2 else kgain
             gains[head] = gains[head] + jnp.sum(back * normal, axis=0, keepdims=True)
             weighted = back * gain
             if head < 2:
-                dq[rows, pl.ds(head * HD, HD)] = weighted
+                gate_pre[part, :, lanes] = weighted
             else:
-                dkv[rows, :HD] = weighted
+                up_pre[part, :, :HD] = weighted
             dots.append(jnp.sum(weighted * normal, axis=-1, keepdims=True))
         stat_all[pl.ds(chip, 1), :, rows] = rows_of(dots[0] + dots[1], dots[2])[None]
     for step in range(1, chips):
@@ -499,16 +640,36 @@
 
         @pl.when(target == me)
         def _():
-            keep = pltpu.make_async_copy(gain_own, slot, self_sems.at[0])
-            keep.start()
-            keep.wait()
-
-        @pl.when(target != me)
-        def _():
-            remote(
-                gain_own, slot, wout_sems.at[8 + piece], wout_sems.at[12 + dp * 2 + core],
-                (target // devices, target % devices),
-            ).start()
+            gain_recv[pl.ds(dp * 2 + core, 1)] = gain_own[...][None]
+
+        post.send(gain_own, slot, gain_sems.at[dp * 2 + core], (target // devices, target % devices), target != me)
+
+    keeps[5].wait()
+    for step in range(1, 8):
+        other = (member + step) % 8
+        arrived(spot, gu_all.at[other], plane_sems.at[5, other], spare)
+    whole(hid_all, 0)
+    gu_part = wout.at[pl.ds(1024, 1024), pl.ds(0, 768)]
+    gu_part[...] = dot_tn(hid_all[...].reshape(1024, 1024), gu_all[...].reshape(1024, 768)).astype(LOW)
+    for y in range(2):
+        for slot, far in enumerate((along.far_inner, along.far_outer)):
+            post.send(
+                gu_part.at[aligned(y * 512 + far * 128, 128)], gu_transit.at[slot, y], gut_sems.at[slot, y],
+                along.place(along.partner), along.outer,
+            )
+    for step in range(8):
+        other = (member + step) % 8
+        first = (other // 4) * 512 + (other % 4) * 32
+        post.send(
+            gu_part.at[aligned(first + along.partner * 128, 32)], gu_land.at[0, member], gu_sems.at[0, member],
+            (other // 4, along.partner * 4 + other % 4),
+        )
+        if step > 0:
+            post.send(
+                gu_part.at[aligned(first + z * 128, 32)], gu_land.at[2, member], gu_sems.at[2, member],
+                (other // 4, z * 4 + other % 4),
+            )
+    gu_land[2, pl.ds(member, 1)] = gu_part[aligned((member // 4) * 512 + z * 128 + (member % 4) * 32, 32), :][None]
 
     for step in range(1, chips):
         other = (chip + step) % chips
@@ -518,85 +679,92 @@
         total = total + stat_all[other]
     width = jnp.where(lax.broadcasted_iota(jnp.int32, total.shape, 0) == 0, 1.0 / 2048, 1.0 / 1024)
     means = total * width
+    grad_send = wdown.at[pl.ds(1024, 1024), pl.ds(512, 512)]
     for part in range(8):
         rows = pl.ds(part * TILE, TILE)
         mean = columns_of(means[:, part * TILE : (part + 1) * TILE])
         scale = columns_of(factors[:, rows])
-        pieces = []
         for head in range(3):
             column = 0 if head < 2 else 1
-            weighted = dq[rows, pl.ds(head * HD, HD)] if head < 2 else dkv[rows, :HD]
+            weighted = gate_pre[part, :, head * HD : (head + 1) * HD] if head < 2 else up_pre[part, :, :HD]
             normal = hat[rows, pl.ds(head * HD, HD)]
-            pieces.append(scale[:, column : column + 1] * (weighted - normal * mean[:, column : column + 1]))
-        pieces.append(dkv[rows, HD:])
-        grad_nat[pl.ds(part * 2, 2)] = jnp.concatenate(pieces, axis=1).astype(LOW).reshape(2, 64, 512)
-
+            grad = scale[:, column : column + 1] * (weighted - normal * mean[:, column : column + 1])
+            grad_nat[pl.ds(part * 2, 2), :, head * HD : (head + 1) * HD] = grad.astype(LOW).reshape(2, 64, HD)
+        grad_nat[pl.ds(part * 2, 2), :, 3 * HD :] = up_pre[part, :, HD:256].astype(LOW).reshape(2, 64, HD)
     grad_recv[pl.ds(chip, 1), pl.ds(core, 1)] = grad_nat[order_ref[seq]][None, None]
     for step in range(1, devices):
         other = (seq + step) % devices
-        grad_send[step] = grad_nat[order_ref[other]]
-        post.send(grad_send.at[step], grad_recv.at[chip, core], grad_sems.at[seq], (dp, other))
-    part_low[...] = dot_tn(tok_nat[...], grad_nat[...].reshape(1024, 512)).astype(LOW)
-    own_rows = pl.ds(pl.multiple_of(me * 32, 32), 32)
-    wqkv_recv[pl.ds(me, 1)] = part_low[own_rows, :][None]
-    for step in range(1, 2 * devices):
-        other = (me + step) % (2 * devices)
-        post.send(
-            part_low.at[pl.ds(pl.multiple_of(other * 32, 32), 32)], wqkv_recv.at[me], wqkv_sems.at[me],
-            (other // devices, other % devices),
-        )
-
-    for keep in keeps:
-        keep.wait()
+        rows = pl.ds(step * 64, 64)
+        grad_send[rows, :] = grad_nat[order_ref[other]]
+        post.send(grad_send.at[rows], grad_recv.at[chip, core], grad_sems.at[seq], (dp, other))
+
+    load_tok.wait()
+    part_low = wdown.at[pl.ds(2048, 1024), pl.ds(0, 512)]
+    part_low[...] = dot_tn(wout[:1024, :], grad_nat[...].reshape(1024, 512)).astype(LOW)
+    post.send(part_low.at[aligned((1 - core) * 512, 512)], part_sib, sib_sem.at[0], sib_place)
+
+    along.combine(down_part, 96, down_land, down_transit, down_sems)
+    for slot, far in enumerate((along.far_inner, along.far_outer)):
+        for y in range(2):
+
+            @pl.when(along.inner)
+            def _():
+                arrived(spot, gu_transit.at[slot, y], gut_sems.at[slot, y], spare)
+                added = gu_transit[slot, y].astype(WIDE) + gu_part[aligned(y * 512 + far * 128, 128), :].astype(WIDE)
+                gu_transit[slot, y] = added.astype(LOW)
+
+            for piece in range(4):
+                post.send(
+                    gu_transit.at[slot, y, pl.ds(piece * 32, 32)], gu_land.at[1, member], gu_sems.at[1, member],
+                    (y, far * 4 + piece), along.inner,
+                )
+
+    arrived(spot, part_sib, sib_sem.at[0], spare)
+    part_sum = wdown.at[pl.ds(2048, 512), pl.ds(512, 512)]
+    part_sum[...] = (part_low[aligned(core * 512, 512), :].astype(WIDE) + part_sib[...].astype(WIDE)).astype(LOW)
+    own_slot = dp * chips + chip
+
+    @pl.when(core == dp)
+    def _():
+        wqkv_recv[pl.ds(own_slot, 1)] = part_sum[aligned(seq * 32, 32), :][None]
+
+    post.send(part_sum.at[aligned(seq * 32, 32)], wqkv_recv.at[own_slot], wqkv_sems.at[own_slot], (1 - dp, seq), core != dp)
+    for step in range(1, devices):
+        other = (seq + step) % devices
+        post.send(part_sum.at[aligned(other * 32, 32)], wqkv_recv.at[own_slot], wqkv_sems.at[own_slot], (core, other))
+
+    dealt(att_all, 3)
+    whole(proj_all, 2)
+    turned = jnp.concatenate([att_all[other] for other in range(8)], axis=1)
+    wout_part[...] = dot(turned, proj_all[...].reshape(1024, 1024)).astype(LOW)
+    along.send(wout_part, 64, wout_land, wout_transit, wout_sems)
+    keep_vec.wait()
     for step in range(1, 8):
         other = (member + step) % 8
-        arrived(spot, mix_all.at[other], plane_sems.at[2, other], spare)
-        arrived(spot, gu_all.at[other, :, pl.ds(0, 384)], plane_sems.at[3, other], spare)
-        arrived(spot, gu_all.at[other, :, pl.ds(384, 384)], plane_sems.at[4, other], spare)
-        arrived(spot, vec_all.at[other], plane_sems.at[5, other], spare)
-    for y in range(2):
-        for x in range(2):
-            other = y * 4 + x * 2 + 1 - core
-            arrived(spot, hid_all.at[other], plane_sems.at[0, other], spare)
-            arrived(spot, down_all.at[other], plane_sems.at[1, other], spare)
+        arrived(spot, vec_all.at[other], vec_sems.at[other], spare)
     vec = vec_all[0]
     for other in range(1, 8):
         vec = vec + vec_all[other]
     vec_far[pl.ds(z, 1)] = vec[None]
-    mixes = jnp.concatenate([mix_all[other] for other in range(8)], axis=1)
-    down_low[...] = dot(mixes, down_all[...].reshape(1024, 1024)).astype(LOW)
-    down_recv[pl.ds(z, 1)] = down_low[pl.ds(pl.multiple_of(z * 96, 96), 96), :][None]
     for far in spot.far_z:
-        place = (dp, far * 4 + spot.x * 2 + core)
-        post.send(vec_far.at[z], vec_far.at[z], far_sems.at[0, z], place)
-        post.send(down_low.at[pl.ds(pl.multiple_of(far * 96, 96), 96)], down_recv.at[z], far_sems.at[1, z], place)
-    gu_low[...] = dot_tn(hid_all[...].reshape(1024, 1024), gu_all[...].reshape(1024, 768)).astype(LOW)
-    gu_recv[pl.ds(z, 1), pl.ds(member, 1)] = gu_low[own_rows, :][None, None]
-    for step in range(1, 2 * devices):
-        other = (me + step) % (2 * devices)
-        post.send(
-            gu_low.at[pl.ds(pl.multiple_of(other * 32, 32), 32)], gu_recv.at[z, member], gu_sems.at[z, member],
-            (other // devices, other % devices),
-        )
+        post.send(vec_far.at[z], vec_far.at[z], vec_sems.at[8 + z], along.place(far))
+    along.combine(wout_part, 64, wout_land, wout_transit, wout_sems)
 
     for step in range(1, devices):
         other = (seq + step) % devices
         arrived(spot, grad_recv.at[other // 2, other % 2], grad_sems.at[other], spare)
+    load_query.wait()
+    load_key.wait()
+    load_value.wait()
+    grad_k, grad_v = [], []
+    gradient = hidden[...]
     for piece in range(chips):
-        for micro in range(2):
-            rows = pl.ds(micro * 64, 64)
-            block = grad_recv[piece, micro]
-            grad_tok[rows, piece * 256 : (piece + 1) * 256] = block[:, :256]
-            grad_tok[rows, 2048 + piece * 128 : 2048 + (piece + 1) * 128] = block[:, 256:384]
-            grad_tok[rows, 3072 + piece * 128 : 3072 + (piece + 1) * 128] = block[:, 384:]
-    for load in loads[1:]:
-        load.wait()
-    in_grad[...] = (
-        hgrad_ref[...]
-        + dot_nt(grad_tok[:, :2048], wq_all[...])
-        + dot_nt(grad_tok[:, 2048:3072], wk_all[...])
-        + dot_nt(grad_tok[:, 3072:], wv_all[...])
-    )
+        block = grad_recv[piece].reshape(128, 512)
+        gradient = gradient + dot_nt(block[:, :256], wgate[:, piece * 256 : (piece + 1) * 256])
+        grad_k.append(block[:, 256:384])
+        grad_v.append(block[:, 384:])
+    gradient = gradient + dot_nt(jnp.concatenate(grad_k, axis=1), wgate[:, 2048:])
+    in_grad[...] = gradient + dot_nt(jnp.concatenate(grad_v, axis=1), wup[:, :1024])
 
     for y in range(2):
         for micro in range(2):
@@ -605,46 +773,39 @@
 
             @pl.when(sender != me)
             def _():
-                arrived(spot, wout_recv.at[source], wout_sems.at[4 + source], spare)
-                arrived(spot, gain_recv.at[source], wout_sems.at[12 + source], spare)
-
-    g_out[...] = sum(wout_recv[source].astype(WIDE) for source in range(4))
+                arrived(spot, gain_recv.at[source], gain_sems.at[source], spare)
+
     gain_out[...] = sum(gain_recv[source] for source in range(4))
-    for step in range(1, 2 * devices):
-        other = (me + step) % (2 * devices)
-        arrived(spot, wqkv_recv.at[other], wqkv_sems.at[other], spare)
+    for source in range(16):
+        sender = (source // chips) * devices + (source % chips) * 2 + dp
+
+        @pl.when(sender != me)
+        def _():
+            arrived(spot, wqkv_recv.at[source], wqkv_sems.at[source], spare)
+
     for piece in range(chips):
-        block = sum(
-            wqkv_recv[y * devices + piece * 2 + micro].astype(WIDE) for y in range(2) for micro in range(2)
-        )
+        block = wqkv_recv[piece].astype(WIDE) + wqkv_recv[chips + piece].astype(WIDE)
         g_query[:, piece * 256 : (piece + 1) * 256] = block[:, :256]
         g_key[:, piece * 128 : (piece + 1) * 128] = block[:, 256:384]
         g_value[:, piece * 128 : (piece + 1) * 128] = block[:, 384:]
     for far in spot.far_z:
-        arrived(spot, vec_far.at[far], far_sems.at[0, far], spare)
-        arrived(spot, down_recv.at[far], far_sems.at[1, far], spare)
+        arrived(spot, vec_far.at[far], vec_sems.at[8 + far], spare)
     vec_out[...] = sum(vec_far[far] for far in range(4))
-    g_down[...] = sum(down_recv[far].astype(WIDE) for far in range(4))
-    for step in range(1, 2 * devices):
-        other = (me + step) % (2 * devices)
-        far, slot = (other % devices) // 4, (other // devices) * 4 + other % 4
-        arrived(spot, gu_recv.at[far, slot], gu_sems.at[far, slot], spare)
+    g_down[...] = along.total(down_land, down_sems)
+    for step in range(8):
+        other = (member + step) % 8
+        for kind in range(3):
+            if kind < 2 or step > 0:
+                arrived(spot, gu_land.at[kind, other], gu_sems.at[kind, other], spare)
     for slot in range(8):
-        block = sum(gu_recv[far, slot].astype(WIDE) for far in range(4))
+        block = sum(gu_land[kind, slot].astype(WIDE) for kind in range(3))
         g_gate[:, slot * 384 : (slot + 1) * 384] = block[:, :384]
         g_up[:, slot * 384 : (slot + 1) * 384] = block[:, 384:]
+    g_out[...] = along.total(wout_land, wout_sems)
     post.finish()
-    for piece in range(4):
-
-        @pl.when(chip * 4 + piece != me)
-        def _():
-            place = ((chip * 4 + piece) // devices, (chip * 4 + piece) % devices)
-            rows = pl.ds(piece * 64, 64)
-            remote(wout_low.at[rows], wout_recv.at[0], wout_sems.at[piece], wout_sems.at[4], place).wait_send()
-            remote(gain_own, gain_recv.at[0], wout_sems.at[8 + piece], wout_sems.at[12], place).wait_send()
-
-
-POST_SENDS = 8 + 28 + 6 + 7 + 15 + 31 + 6 + 31
+
+
+POST_SENDS = 288
 
 
 def row_backward(*operands):
@@ -657,6 +818,7 @@
     return pl.pallas_call(
         backward_kernel,
         out_shape=(
+            shape((128, width), LOW),
             shape((128, width), WIDE),
             shape((32, 2048), WIDE),
             shape((32, 1024), WIDE),
@@ -668,59 +830,124 @@
             shape((32, 3072), WIDE),
             shape((96, 1024), WIDE),
         ),
-        in_specs=[vmem] * 15 + [any_spec] * 4 + [vmem] * 4 + [smem] * 3,
-        out_specs=(vmem,) * 10,
+        in_specs=[vmem] * 9 + [any_spec] * 13 + [smem] * 2,
+        out_specs=(vmem,) * 11,
         scratch_shapes=[
-            pltpu.VMEM((256, width), LOW),
-            pltpu.VMEM((width, 2048), LOW),
-            pltpu.VMEM((width, 1024), LOW),
-            pltpu.VMEM((width, 1024), LOW),
-            pltpu.VMEM((16, 64, width), LOW),
-            pltpu.VMEM((length, width), LOW),
+            pltpu.VMEM((2048, width), LOW),
+            pltpu.VMEM((width, 3072), LOW),
+            pltpu.VMEM((width, 3072), LOW),
+            pltpu.VMEM((3072, width), LOW),
+            pltpu.VMEM((8, 2 * TILE, HD), LOW),
+            pltpu.VMEM((length, 2 * HD), LOW),
+            pltpu.VMEM((length, 3 * HD), WIDE),
+            pltpu.VMEM((length + 64, HD), WIDE),
+            pltpu.VMEM((length + 64, HD), WIDE),
+            pltpu.VMEM((128, width), WIDE),
+            pltpu.VMEM((128, width), WIDE),
+            pltpu.VMEM((128, width), LOW),
+            pltpu.VMEM((8, 128, 384), WIDE),
+            pltpu.VMEM((8, 128, 384), WIDE),
+            pltpu.VMEM((128, 3072), LOW),
             pltpu.VMEM((8, 384, 128), LOW),
+            pltpu.VMEM((8, 256, 128), LOW),
+            pltpu.VMEM((128, width), LOW),
+            pltpu.VMEM((8, 128, 768), LOW),
+            pltpu.VMEM((128, width), LOW),
+            pltpu.VMEM((2, 64, 2048), LOW),
+            pltpu.VMEM((8, width), WIDE),
+            pltpu.VMEM((8, 128, width), LOW),
             pltpu.VMEM((8, 128, width), LOW),
             pltpu.VMEM((8, 128, width), LOW),
             pltpu.VMEM((8, 128, 768), LOW),
             pltpu.VMEM((8, 384, 128), LOW),
-            pltpu.VMEM((8, 8, 1024), WIDE),
-            pltpu.VMEM((4, 8, 1024), WIDE),
+            pltpu.VMEM((8, 256, 128), LOW),
+            pltpu.VMEM((8, 8, width), WIDE),
+            pltpu.VMEM((4, 8, width), WIDE),
+            pltpu.VMEM((3, 96, width), LOW),
+            pltpu.VMEM((2, 96, width), LOW),
+            pltpu.VMEM((256, width), LOW),
+            pltpu.VMEM((3, 64, width), LOW),
+            pltpu.VMEM((2, 64, width), LOW),
+            pltpu.VMEM((3, 8, 32, 768), LOW),
+            pltpu.VMEM((2, 2, 128, 768), LOW),
+            pltpu.VMEM((16, 64, 256), LOW),
             pltpu.VMEM((8, 2 * TILE, HD), LOW),
             pltpu.VMEM((HD, length), LOW),
-            pltpu.VMEM((length, 2 * HD), WIDE),
-            pltpu.VMEM((length, 2 * HD), WIDE),
-            pltpu.VMEM((16, 64, 512), LOW),
             pltpu.VMEM((8, 8, length), WIDE),
             pltpu.VMEM((16, 64, 512), LOW),
             pltpu.VMEM((8, 2, 64, 512), LOW),
-            pltpu.VMEM((128, 4096), LOW),
-            pltpu.VMEM((length, 512), LOW),
-            pltpu.VMEM((32, 32, 512), LOW),
-            pltpu.VMEM((256, width), LOW),
-            pltpu.VMEM((4, 64, width), LOW),
+            pltpu.VMEM((512, 512), LOW),
+            pltpu.VMEM((16, 32, 512), LOW),
             pltpu.VMEM((8, 384), WIDE),
             pltpu.VMEM((4, 8, 384), WIDE),
-            pltpu.VMEM((1024, 768), LOW),
-            pltpu.VMEM((4, 8, 32, 768), LOW),
-            pltpu.VMEM((384, width), LOW),
-            pltpu.VMEM((4, 96, width), LOW),
-            dma((11,)),
-            dma((GATHER_SENDS,)),
-            dma((GATHER_RECVS,)),
+            pltpu.SMEM((16,), jnp.int32),
+            dma((17,)),
             dma((POST_SENDS,)),
             dma((6, 8)),
-            dma((2, 4)),
+            dma((12,)),
+            dma((4,)),
+            dma((4,)),
+            dma((3, 8)),
+            dma((2, 2)),
+            dma((16,)),
             dma((8,)),
             dma((16,)),
-            dma((32,)),
+            dma((1,)),
             dma((16,)),
-            dma((4, 8)),
-            dma((1,)),
+            dma((4,)),
         ],
         compiler_params=pltpu.CompilerParams(
-            collective_id=1, has_side_effects=True, vmem_limit_bytes=60 * 2**20
+            collective_id=1, has_side_effects=True, vmem_limit_bytes=63 * 2**20
         ),
         name="row_backward",
     )(*operands)
+
+
+def finish_kernel(*refs):
+    count = 9
+    sources, vec_ref, gain_ref = refs[:count], refs[count], refs[count + 1]
+    targets, small = refs[count + 2 : 2 * count + 2], refs[2 * count + 2 :]
+    for source, target in zip(sources, targets):
+        target[...] = source[...]
+    seq = lax.axis_index("seq")
+    me = lax.axis_index("dp") * 16 + seq
+    part = seq % 4
+    gains, vec = gain_ref[...], vec_ref[...]
+    q_out, k_out, attn_out, mlp_out = small
+    q_all = pltpu.roll(gains[:, :256], (256 - part * 64) % 256, axis=1)
+    k_all = pltpu.roll(gains[:, 256:], (128 - part * 32) % 128, axis=1)
+    vec = pltpu.roll(vec, (1024 - me * 32) % 1024, axis=1)
+    q_out[...] = q_all[0:1, :64]
+    k_out[...] = k_all[0:1, :32]
+    attn_out[...] = vec[0:1, :32]
+    mlp_out[...] = vec[1:2, :32]
+
+
+def finish(arrays, vec, gains):
+    vmem = pl.BlockSpec(memory_space=pltpu.VMEM)
+    shape = jax.ShapeDtypeStruct
+    count = len(arrays)
+    return pl.pallas_call(
+        finish_kernel,
+        out_shape=tuple(shape(a.shape, a.dtype) for a in arrays)
+        + (shape((1, 64), WIDE), shape((1, 32), WIDE), shape((1, 32), WIDE), shape((1, 32), WIDE)),
+        in_specs=[vmem] * (count + 2),
+        out_specs=(vmem,) * (count + 4),
+        name="finish",
+    )(*arrays, vec, gains)
+
+
+def rms_forward(inputs, gain_vec):
+    factor = lax.rsqrt(jnp.mean(inputs * inputs, axis=-1, keepdims=True) + EPSILON)
+    normal = inputs * factor
+    return (normal * gain_vec, normal, factor)
+
+
+def rms_backward(grad_in, gain_vec, normal, factor):
+    weighted = grad_in * gain_vec
+    gain_grad = jnp.sum(grad_in * normal, axis=0)
+    inner_mean = jnp.mean(weighted * normal, axis=-1, keepdims=True)
+    return (factor * (weighted - normal * inner_mean), gain_grad)
 
 
 def rope_tables(rot_places, head_size):
@@ -1000,77 +1227,39 @@
     )
 
 
-def rms_forward(inputs, gain_vec):
-    factor = lax.rsqrt(jnp.mean(inputs * inputs, axis=-1, keepdims=True) + EPSILON)
-    normal = inputs * factor
-    return (normal * gain_vec, normal, factor)
-
-
-def rms_backward(grad_in, gain_vec, normal, factor):
-    weighted = grad_in * gain_vec
-    gain_grad = jnp.sum(grad_in * normal, axis=0)
-    inner_mean = jnp.mean(weighted * normal, axis=-1, keepdims=True)
-    return (factor * (weighted - normal * inner_mean), gain_grad)
-
-
 def split_by_heads(
     tokens, cotangent, w_query, w_key, w_value, w_out, q_gain, k_gain, attn_gain,
     w_gate, w_up, w_down, mlp_gain, doc_lengths, block_order,
 ):
-    micro_count, _, block_len, width = tokens.shape
+    cos, sine = rope_constants(1024)
+    q_gain_rows, k_gain_rows = q_gain.reshape(16, HD), k_gain.reshape(8, HD)
     own_tokens = tokens[:, 0]
-    flat_tokens = tokens.reshape(micro_count * block_len, width)
-    out_grad = cotangent.reshape(micro_count * block_len, width).astype(WIDE)
-    first = doc_lengths[:, 0, 0]
-    cos, sine = rope_constants(1024)
-    index = jnp.arange(16, dtype=jnp.int32)
-    inverse = jnp.sum(jnp.where(block_order[None, :] == index[:, None], index[None, :], 0), axis=1).astype(jnp.int32)
-    q_gain_rows, k_gain_rows = q_gain.reshape(16, HD), k_gain.reshape(8, HD)
-    att_tok, tok_nat, q_pair, kv_nat, hat, factors, lse, att_nat = row_forward(
-        own_tokens, w_query, w_key, w_value, q_gain_rows, k_gain_rows, cos, sine, block_order, inverse, first
-    )
-    attn_proj = dot(att_tok.reshape(micro_count * block_len, -1), w_out)
-    attn_normed, attn_hat, attn_factor = rms_forward(attn_proj, attn_gain)
-    hidden = flat_tokens.astype(WIDE) + attn_normed
-    hidden_low = hidden.astype(LOW)
-    gate_pre = dot(hidden_low, w_gate)
-    up_pre = dot(hidden_low, w_up)
-    sigmoid_gate = jax.nn.sigmoid(gate_pre)
-    mixed_low = (gate_pre * sigmoid_gate * up_pre).astype(LOW)
-    down_pre = dot(mixed_low, w_down)
-    down_normed, down_hat, down_factor = rms_forward(down_pre, mlp_gain)
-    layer_out = (hidden + down_normed).astype(LOW).reshape(tokens.shape)
-    down_grad, grad_mlp_gain = rms_backward(out_grad, mlp_gain, down_hat, down_factor)
-    down_grad = down_grad.astype(LOW)
-    mixed_grad = dot_nt(down_grad, w_down)
-    gate_grad = (mixed_grad * up_pre * sigmoid_gate * (1.0 + gate_pre * (1.0 - sigmoid_gate))).astype(LOW)
-    up_grad = (mixed_grad * gate_pre * sigmoid_gate).astype(LOW)
-    hidden_grad = out_grad + dot_nt(gate_grad, w_gate) + dot_nt(up_grad, w_up)
-    proj_grad, grad_attn_gain = rms_backward(hidden_grad, attn_gain, attn_hat, attn_factor)
-    proj_grad = proj_grad.astype(LOW).reshape(micro_count, block_len, width)
-    vec = jnp.concatenate([grad_attn_gain[None], grad_mlp_gain[None], jnp.zeros((6, width), WIDE)], axis=0)
-    in_grad, g_query, g_key, g_value, g_out, vec_sum, gain_sum, g_gate, g_up, g_down = row_backward(
-        proj_grad, hidden_low, down_grad, gate_grad, up_grad, mixed_low, hidden_grad, vec,
-        tok_nat, q_pair, kv_nat, hat, factors, lse, att_nat,
-        w_out, w_query, w_key, w_value, q_gain_rows, k_gain_rows, cos, sine, block_order, inverse, first,
-    )
-    seq = lax.axis_index("seq")
-    me = lax.axis_index("dp") * 16 + seq
-    part = seq % 4
+    att_tok, tok_nat, q_pair, kv_nat, hat, factors, lse = row_forward(
+        own_tokens, w_query, w_key, w_value, q_gain_rows, k_gain_rows, cos, sine, block_order, doc_lengths
+    )
+    layer_out, in_grad, g_query, g_key, g_value, g_out, vec, gains, g_gate, g_up, g_down = row_backward(
+        att_tok, own_tokens, cotangent[:, 0], attn_gain[None], mlp_gain[None], q_gain_rows, k_gain_rows, factors, lse,
+        tok_nat, q_pair, kv_nat, hat, cos, sine,
+        w_out, w_gate, w_up, w_down, w_query, w_key, w_value, block_order, doc_lengths,
+    )
+    (
+        layer_out, in_grad, g_query, g_key, g_value, g_out, g_gate, g_up, g_down,
+        g_q_gain, g_k_gain, g_attn_gain, g_mlp_gain,
+    ) = finish((layer_out, in_grad, g_query, g_key, g_value, g_out, g_gate, g_up, g_down), vec, gains)
     return (
-        layer_out,
+        layer_out.reshape(tokens.shape),
         in_grad.reshape(tokens.shape),
         g_query,
         g_key,
         g_value,
         g_out,
-        lax.dynamic_slice(gain_sum, (0, part * 64), (1, 64))[0],
-        lax.dynamic_slice(gain_sum, (0, 256 + part * 32), (1, 32))[0],
-        lax.dynamic_slice(vec_sum, (0, me * 32), (1, 32))[0],
+        g_q_gain[0],
+        g_k_gain[0],
+        g_attn_gain[0],
         g_gate,
         g_up,
         g_down,
-        lax.dynamic_slice(vec_sum, (1, me * 32), (1, 32))[0],
+        g_mlp_gain[0],
     )
 
 

time: 309 us -> 237 us (0.77)
  Pallas kernels: 272 us -> 236 us
  local copies, waits for them, and re-layouts: 15 us -> 0 us
  matrix products: 14.1 us -> 0 us
  other arithmetic: 3.67 us -> 0 us
    pallas_call x1 -> x2, Pallas kernels: 212 us -> 176 us  [the longest x1 172 us: row_backward(): pl.pallas_call(backward_kernel, out_shape=(shape((128, width), LOW), shap...]
    dot_general x7 -> x0, matrix products: 14.1 us -> none  [the longest x3 7.31 us: dot_nt(): lax.dot_general(left, right, (((1,), (1,)), ((), ())), preferred_element_...]
    unnamed x48 -> x0, local copies, waits for them, and re-layouts: 11 us -> none
where the time goes in v2:
time: 237 us
  Pallas kernels  236 us (100%)
    pallas_call x1, Pallas kernels, row_backward(): pl.pallas_call(backward_kernel, out_shape=(shape((128, width), LOW), shap...  172 us
    pallas_call x1, Pallas kernels, row_forward(): pl.pallas_call(forward_kernel, out_shape=(shape((2, 64, 2048), LOW), shap...  60.1 us

profile of v2, /device:TPU:0, one launch (start us, length us, event | category | flops | bytes accessed | tf_op | source)
XLA Modules:
  0.0 236.5 jit_solution(1748737023419134379)
XLA Ops:
  0.6 60.1 %row_forward.1 = (bf16[2,64,2048]{2,1,0:T(8,128)(2,1)}, bf16[1024,1024]{1,0:T(8,128)(2,1)}, bf16[8,256,128]{2,1,0:T(8,128)(2,1)}, bf16[1024,256]{1,0:T(8,128)(2,...) custom-call(bf16[2,64,1024]{2,1,0:T(8,128)(2,1)} %bitcast.16, bf16[1024,2048]{1,0:T(8,128)(2,1)} %wq_hbm.3, ...), custom_call_target="tpu_custom_call" | custom-call | tf_op jit(solution)/shard_map/row_forward/pallas_call | solution.py:304
  60.7 172.3 %row_backward.1 = (bf16[128,1024]{1,0:T(8,128)(2,1)}, f32[128,1024]{1,0:T(8,128)}, f32[32,2048]{1,0:T(8,128)}, f32[32,1024]{1,0:T(8,128)}, f32[32,1024]{1,0:T(8,...) custom-call(bf16[2,64,2048]{2,1,0:T(8,128)(2,1)} %get-tuple-element., ...), custom_call_target="tpu_custom_call" | custom-call | tf_op jit(solution)/shard_map/row_backward/pallas_call | solution.py:818
  233.0 3.3 %finish.1 = (bf16[128,1024]{1,0:T(8,128)(2,1)}, f32[128,1024]{1,0:T(8,128)}, f32[32,2048]{1,0:T(8,128)}, f32[32,1024]{1,0:T(8,128)}, f32[32,1024]{1,0:T(8,128)},...) custom-call(bf16[128,1024]{1,0:T(8,128)(2,1)} %get-tuple-element.51., ...), custom_call_target="tpu_custom_call" | custom-call | tf_op jit(solution)/shard_map/finish/pallas_call | solution.py:930

commit v3 on v2

--- a/solution.py
+++ b/solution.py
@@ -173,7 +173,7 @@
     tok_ref, wq_hbm, wk_hbm, wv_hbm, qgain_ref, kgain_ref, cos_ref, sine_ref,
     order_ref, docs_ref,
     att_tok, tok_nat, q_pair, kv_nat, hat, factors, lse,
-    att_nat, tok_all, w_own, stat_all, att_send, att_recv, kv_turned,
+    att_nat, tok_all, wq_all, wk_all, wv_own, stat_all, att_send, att_recv, kv_turned,
     inverse_ref, local_sems, send_sems, recv_sems, stat_send, stat_recv, att_ssem, att_rsem,
 ):
     spot = Spot()
@@ -181,9 +181,11 @@
     chips = 8
     chip = spot.chip
     loads = [
-        pltpu.make_async_copy(wq_hbm.at[:, pl.ds(pl.multiple_of(chip * 256, 256), 256)], w_own.at[:, pl.ds(0, 256)], local_sems.at[1]),
-        pltpu.make_async_copy(wk_hbm.at[:, pl.ds(pl.multiple_of(chip * 128, 128), 128)], w_own.at[:, pl.ds(256, 128)], local_sems.at[2]),
-        pltpu.make_async_copy(wv_hbm.at[:, pl.ds(pl.multiple_of(chip * 128, 128), 128)], w_own.at[:, pl.ds(384, 128)], local_sems.at[3]),
+        pltpu.make_async_copy(wq_hbm, wq_all, local_sems.at[1]),
+        pltpu.make_async_copy(wk_hbm, wk_all, local_sems.at[2]),
+        pltpu.make_async_copy(
+            wv_hbm.at[:, pl.ds(pl.multiple_of(chip * 128, 128), 128)], wv_own, local_sems.at[3]
+        ),
     ]
     for load in loads:
         load.start()
@@ -191,9 +193,29 @@
     gather = RowGather(spot, tok_ref, tok_all, local_sems.at[0], send_sems, recv_sems)
     gather.start()
     invert(order_ref, inverse_ref)
-    gather.forward()
+
     for load in loads:
         load.wait()
+    own = tok_ref[...].reshape(128, tok_ref.shape[-1])
+    sums = []
+    for weight in (wq_all, wk_all):
+        parts = [dot(own, weight[:, first : first + 512]) for first in range(0, weight.shape[1], 512)]
+        sums.append(sum(jnp.sum(part * part, axis=-1, keepdims=True) for part in parts) / weight.shape[1])
+    stat_all[pl.ds(spot.seq, 1)] = lax.rsqrt(rows_of(sums[0], sums[1]) + EPSILON)[None]
+    stat_copies = []
+    for step in range(1, devices):
+        other = (spot.seq + step) % devices
+        copy = remote(
+            stat_all.at[spot.seq], stat_all.at[spot.seq], stat_send.at[step], stat_recv.at[spot.seq], (spot.dp, other)
+        )
+        copy.start()
+        stat_copies.append(copy)
+    gather.forward()
+    for step in range(1, devices):
+        other = (spot.seq + step) % devices
+        remote(
+            stat_all.at[other], stat_all.at[other], stat_send.at[0], stat_recv.at[other], (spot.dp, spot.sibling)
+        ).wait_recv()
     gather.finish()
 
     first_length = docs_ref[spot.core, 0, 0]
@@ -201,34 +223,13 @@
         rows = pl.ds(part * CHUNK, CHUNK)
         chunk = jnp.concatenate([tok_all[inverse_ref[part * 4 + piece]] for piece in range(4)], axis=0)
         tok_nat[rows, :] = chunk
-        pre = dot(chunk, w_own[...])
-        hat[rows, :] = pre[:, :384]
-        kv_nat[rows, 128:] = pre[:, 384:].astype(LOW)
-        squares = pre[:, :384] * pre[:, :384]
-        stat_all[pl.ds(chip, 1), :, rows] = rows_of(
-            jnp.sum(squares[:, :256], axis=-1, keepdims=True),
-            jnp.sum(squares[:, 256:], axis=-1, keepdims=True),
-        )[None]
-    stat_copies = []
-    for step in range(1, chips):
-        other = (chip + step) % chips
-        copy = remote(
-            stat_all.at[chip], stat_all.at[chip], stat_send.at[step - 1], stat_recv.at[chip],
-            (spot.dp, other * 2 + spot.core),
-        )
-        copy.start()
-        stat_copies.append(copy)
-    for step in range(1, chips):
-        other = (chip + step) % chips
-        remote(
-            stat_all.at[other], stat_all.at[other], stat_send.at[0], stat_recv.at[other],
-            (spot.dp, spot.sibling),
-        ).wait_recv()
-    total = stat_all[0]
-    for other in range(1, chips):
-        total = total + stat_all[other]
-    width = jnp.where(lax.broadcasted_iota(jnp.int32, total.shape, 0) == 0, 1.0 / 2048, 1.0 / 1024)
-    factors[...] = lax.rsqrt(total * width + EPSILON)
+        hat[rows, :256] = dot(chunk, wq_all[:, pl.ds(pl.multiple_of(chip * 256, 256), 256)])
+        hat[rows, 256:] = dot(chunk, wk_all[:, pl.ds(pl.multiple_of(chip * 128, 128), 128)])
+        kv_nat[rows, 128:] = dot(chunk, wv_own[...]).astype(LOW)
+    for block in range(16):
+        both = stat_all[inverse_ref[block]]
+        both = jnp.where(spot.core == 0, both, pltpu.roll(both, 64, axis=1))
+        factors[:, block * 64 : (block + 1) * 64] = both[:, :64]
     qgain = qgain_ref[pl.ds(chip * 2, 2), :]
     kgain = kgain_ref[pl.ds(chip, 1), :]
     for part in range(8):
@@ -317,8 +318,10 @@
         scratch_shapes=[
             pltpu.VMEM((16, 64, 2 * HD), LOW),
             pltpu.VMEM((16, 64, width), LOW),
-            pltpu.VMEM((width, 512), LOW),
-            pltpu.VMEM((8, 8, length), WIDE),
+            pltpu.VMEM((width, 2048), LOW),
+            pltpu.VMEM((width, 1024), LOW),
+            pltpu.VMEM((width, 128), LOW),
+            pltpu.VMEM((16, 8, 128), WIDE),
             pltpu.VMEM((16, 64, 2 * HD), LOW),
             pltpu.VMEM((8, 2, 64, 2 * HD), LOW),
             pltpu.VMEM((HD, length), LOW),
@@ -326,8 +329,8 @@
             pltpu.SemaphoreType.DMA((4,)),
             pltpu.SemaphoreType.DMA((GATHER_SENDS,)),
             pltpu.SemaphoreType.DMA((GATHER_RECVS,)),
-            pltpu.SemaphoreType.DMA((8,)),
-            pltpu.SemaphoreType.DMA((8,)),
+            pltpu.SemaphoreType.DMA((16,)),
+            pltpu.SemaphoreType.DMA((16,)),
             pltpu.SemaphoreType.DMA((16,)),
             pltpu.SemaphoreType.DMA((16,)),
         ],
@@ -383,12 +386,12 @@
     def send(self, part, size, landing, transit, sems):
         spot, post = self.spot, self.post
         landing[2] = part[aligned(spot.z * size, size), :]
-        post.send(part.at[aligned(self.partner * size, size)], landing.at[0], sems.at[0], self.place(self.partner))
         for slot, far in enumerate((self.far_inner, self.far_outer)):
             post.send(
                 part.at[aligned(far * size, size)], transit.at[slot], sems.at[2 + slot], self.place(self.partner),
                 self.outer,
             )
+        post.send(part.at[aligned(self.partner * size, size)], landing.at[0], sems.at[0], self.place(self.partner))
 
     def combine(self, part, size, landing, transit, sems):
         for slot, far in enumerate((self.far_inner, self.far_outer)):
@@ -424,9 +427,9 @@
     wout, wgate, wup, wdown, q_pair, kv_nat, hat, cos_ref, sine_ref,
     att_hat, hidden, hid_own, gate_pre, up_pre, mixed, mix_turned, att_turned, down_own, gu_own, proj_own, ag_own, vec_own,
     hid_all, down_all, proj_all, gu_all, mix_all, att_all, vec_all, vec_far,
-    down_land, down_transit, wout_part, wout_land, wout_transit, gu_land, gu_transit,
+    down_land, down_transit, wout_part, wout_land, gu_land, gu_transit,
     ag_recv, ag_pair, k_turned, stat_all, grad_nat, grad_recv, part_sib, wqkv_recv, gain_own, gain_recv,
-    inverse_ref, local_sems, post_sems, plane_sems, vec_sems, down_sems, wout_sems, gu_sems, gut_sems, ag_sems, stat_sems, grad_sems, sib_sem, wqkv_sems, gain_sems,
+    inverse_ref, local_sems, post_sems, hid_sems, dpl_sems, proj_sems, attp_sems, mix_sems, gup_sems, vec_sems, down_sems, wout_sems, gu_sems, gut_sems, ag_sems, stat_sems, grad_sems, sib_sem, wqkv_sems, gain_sems,
 ):
     spot = Spot()
     devices, chips = 16, 8
@@ -467,46 +470,49 @@
     hid_own[...] = stream.astype(LOW)
     pl.semaphore_wait(barrier, 2 * devices - 1)
 
-    plane_places = ((dp, spot.flip_x), (1 - dp, seq), (1 - dp, spot.flip_x))
-    plane_members = (
-        dp * 4 + (1 - spot.x) * 2 + core,
-        (1 - dp) * 4 + spot.x * 2 + core,
-        (1 - dp) * 4 + (1 - spot.x) * 2 + core,
-    )
-    sib_place = (dp, spot.sibling)
+    x_place, y_place, sib_place = (dp, spot.flip_x), (1 - dp, seq), (dp, spot.sibling)
+    x_member = dp * 4 + (1 - spot.x) * 2 + core
+    y_member = (1 - dp) * 4 + spot.x * 2 + core
+    diagonal = (1 - dp) * 4 + (1 - spot.x) * 2 + core
     keeps = {}
 
-    def spread(own, held, kind, index):
-        keeps[kind] = load(own, held.at[member], index)
-        for place in plane_places + (sib_place,):
-            post.send(own, held.at[member], plane_sems.at[kind, member], place)
-
-    def pass_on(held, kind):
-        for other in plane_members:
-            arrived(spot, held.at[other], plane_sems.at[kind, other], spare)
-            post.send(held.at[other], held.at[other], plane_sems.at[kind, other], sib_place)
-
-    def whole(held, kind):
-        keeps[kind].wait()
+    def spread(own, held, sems, index):
+        keeps[index] = load(own, held.at[member], index)
+        for place in (x_place, y_place, sib_place):
+            post.send(own, held.at[member], sems.at[member], place)
+
+    def pass_on(held, sems, across):
+        turn = (x_member, y_place) if across == "y" else (y_member, x_place)
+        straight = y_member if across == "y" else x_member
+        for other, places in ((turn[0], (turn[1], sib_place)), (straight, (sib_place,))):
+            arrived(spot, held.at[other], sems.at[other], spare)
+            for place in places:
+                post.send(held.at[other], held.at[other], sems.at[other], place)
+
+    def pass_diagonal(held, sems):
+        arrived(spot, held.at[diagonal], sems.at[diagonal], spare)
+        post.send(held.at[diagonal], held.at[diagonal], sems.at[diagonal], sib_place)
+
+    def whole(held, sems, index):
+        keeps[index].wait()
         for y in range(2):
             for x in range(2):
                 other = y * 4 + x * 2 + 1 - core
-                arrived(spot, held.at[other], plane_sems.at[kind, other], spare)
-
-    def deal(own, held, kind, index):
-        keeps[kind] = load(own.at[member], held.at[member], index)
+                arrived(spot, held.at[other], sems.at[other], spare)
+
+    def deal(own, held, sems, index):
+        keeps[index] = load(own.at[member], held.at[member], index)
         for step in range(1, 8):
             other = (member + step) % 8
-            post.send(own.at[other], held.at[member], plane_sems.at[kind, member], (other // 4, z * 4 + other % 4))
-
-    def dealt(held, kind):
-        keeps[kind].wait()
+            post.send(own.at[other], held.at[member], sems.at[member], (other // 4, z * 4 + other % 4))
+
+    def dealt(held, sems, index):
+        keeps[index].wait()
         for step in range(1, 8):
             other = (member + step) % 8
-            arrived(spot, held.at[other], plane_sems.at[kind, other], spare)
-
-    spread(hid_own, hid_all, 0, 9)
-    deal(att_turned, att_all, 3, 10)
+            arrived(spot, held.at[other], sems.at[other], spare)
+
+    spread(hid_own, hid_all, hid_sems, 9)
 
     load_gate.wait()
     load_up.wait()
@@ -521,7 +527,8 @@
         turned = block.T
         for piece in range(4):
             mix_turned[(group // 4) * 4 + piece, pl.ds((group % 4) * 96, 96), :] = turned[piece * 96 : (piece + 1) * 96]
-    deal(mix_turned, mix_all, 4, 11)
+    deal(mix_turned, mix_all, mix_sems, 11)
+    pass_on(hid_all, hid_sems, "y")
     load_down.wait()
     down_pre = dot(mixed[...], wdown[...])
     factor = row_scale(down_pre)
@@ -531,7 +538,7 @@
     down_own[...] = norm_back(cot, mgain_ref[...], normal, factor).astype(LOW)
     vec_own[...] = jnp.zeros_like(vec_own)
     vec_own[1:2, :] = jnp.sum(cot * normal, axis=0, keepdims=True)
-    spread(down_own, down_all, 1, 12)
+    spread(down_own, down_all, dpl_sems, 12)
 
     for step in range(1, 9):
         group = (member + step) % 8
@@ -540,9 +547,6 @@
         sigmoid = jax.nn.sigmoid(gate)
         gu_own[group, :, :384] = (grad * up * sigmoid * (1.0 + gate * (1.0 - sigmoid))).astype(LOW)
         gu_own[group, :, 384:] = (grad * gate * sigmoid).astype(LOW)
-        if step < 8:
-            post.send(gu_own.at[group], gu_all.at[member], plane_sems.at[5, member], (group // 4, z * 4 + group % 4))
-    keeps[5] = load(gu_own.at[member], gu_all.at[member], 13)
     hgrad = cot
     for group in range(8):
         lanes = slice(group * 384, (group + 1) * 384)
@@ -564,22 +568,15 @@
             ag_own.at[other % 2, :, aligned((other // 2) * 256, 256)], ag_recv.at[seq], ag_sems.at[seq], (dp, other)
         )
     load_tok = load(tok_hbm, wout.at[pl.ds(0, 1024)], 0)
-    spread(proj_own, proj_all, 2, 15)
+    pass_diagonal(hid_all, hid_sems)
+    pass_on(down_all, dpl_sems, "x")
+    deal(gu_own, gu_all, gup_sems, 13)
+    deal(att_turned, att_all, attp_sems, 10)
+    spread(proj_own, proj_all, proj_sems, 15)
     keep_vec = load(vec_own, vec_all.at[member], 16)
     for step in range(1, 8):
         other = (member + step) % 8
         post.send(vec_own, vec_all.at[member], vec_sems.at[member], (other // 4, z * 4 + other % 4))
-    pass_on(hid_all, 0)
-    pass_on(down_all, 1)
-
-    dealt(mix_all, 4)
-    whole(down_all, 1)
-    down_part = wdown.at[pl.ds(0, 384)]
-    mixes = jnp.concatenate([mix_all[other] for other in range(8)], axis=1)
-    down_part[...] = dot(mixes, down_all[...].reshape(1024, 1024)).astype(LOW)
-    along.send(down_part, 96, down_land, down_transit, down_sems)
-    pass_on(proj_all, 2)
-
     for copy in later:
         copy.wait()
     keep_ag.wait()
@@ -593,7 +590,15 @@
     k_turned[...] = kv_nat[:, :HD].T
     first_length = docs_ref[core, 0, 0]
     up_pre[:, :, :256] = jnp.zeros((8, TILE, 256), WIDE)
-    for tile in range(8):
+    down_part = wdown.at[pl.ds(0, 384)]
+    for tile in range(7, -1, -1):
+        if tile == 4:
+            pass_diagonal(down_all, dpl_sems)
+            dealt(mix_all, mix_sems, 11)
+            whole(down_all, dpl_sems, 12)
+            mixes = jnp.concatenate([mix_all[other] for other in range(8)], axis=1)
+            down_part[...] = dot(mixes, down_all[...].reshape(1024, 1024)).astype(LOW)
+            along.send(down_part, 96, down_land, down_transit, down_sems)
         count = (tile + 1) * TILE
         queries, grads = q_pair[tile], ag_pair[tile]
         scores = dot_nt(kv_nat[:count, :HD], queries) * HD ** (-0.5)
@@ -644,33 +649,7 @@
 
         post.send(gain_own, slot, gain_sems.at[dp * 2 + core], (target // devices, target % devices), target != me)
 
-    keeps[5].wait()
-    for step in range(1, 8):
-        other = (member + step) % 8
-        arrived(spot, gu_all.at[other], plane_sems.at[5, other], spare)
-    whole(hid_all, 0)
-    gu_part = wout.at[pl.ds(1024, 1024), pl.ds(0, 768)]
-    gu_part[...] = dot_tn(hid_all[...].reshape(1024, 1024), gu_all[...].reshape(1024, 768)).astype(LOW)
-    for y in range(2):
-        for slot, far in enumerate((along.far_inner, along.far_outer)):
-            post.send(
-                gu_part.at[aligned(y * 512 + far * 128, 128)], gu_transit.at[slot, y], gut_sems.at[slot, y],
-                along.place(along.partner), along.outer,
-            )
-    for step in range(8):
-        other = (member + step) % 8
-        first = (other // 4) * 512 + (other % 4) * 32
-        post.send(
-            gu_part.at[aligned(first + along.partner * 128, 32)], gu_land.at[0, member], gu_sems.at[0, member],
-            (other // 4, along.partner * 4 + other % 4),
-        )
-        if step > 0:
-            post.send(
-                gu_part.at[aligned(first + z * 128, 32)], gu_land.at[2, member], gu_sems.at[2, member],
-                (other // 4, z * 4 + other % 4),
-            )
-    gu_land[2, pl.ds(member, 1)] = gu_part[aligned((member // 4) * 512 + z * 128 + (member % 4) * 32, 32), :][None]
-
+    along.combine(down_part, 96, down_land, down_transit, down_sems)
     for step in range(1, chips):
         other = (chip + step) % chips
         arrived(spot, stat_all.at[other], stat_sems.at[other], spare)
@@ -703,21 +682,29 @@
     part_low[...] = dot_tn(wout[:1024, :], grad_nat[...].reshape(1024, 512)).astype(LOW)
     post.send(part_low.at[aligned((1 - core) * 512, 512)], part_sib, sib_sem.at[0], sib_place)
 
-    along.combine(down_part, 96, down_land, down_transit, down_sems)
-    for slot, far in enumerate((along.far_inner, along.far_outer)):
-        for y in range(2):
-
-            @pl.when(along.inner)
-            def _():
-                arrived(spot, gu_transit.at[slot, y], gut_sems.at[slot, y], spare)
-                added = gu_transit[slot, y].astype(WIDE) + gu_part[aligned(y * 512 + far * 128, 128), :].astype(WIDE)
-                gu_transit[slot, y] = added.astype(LOW)
-
-            for piece in range(4):
-                post.send(
-                    gu_transit.at[slot, y, pl.ds(piece * 32, 32)], gu_land.at[1, member], gu_sems.at[1, member],
-                    (y, far * 4 + piece), along.inner,
-                )
+    dealt(gu_all, gup_sems, 13)
+    whole(hid_all, hid_sems, 9)
+    gu_part = wout.at[pl.ds(1024, 1024), pl.ds(0, 768)]
+    gu_part[...] = dot_tn(hid_all[...].reshape(1024, 1024), gu_all[...].reshape(1024, 768)).astype(LOW)
+    for y in range(2):
+        for slot, far in enumerate((along.far_inner, along.far_outer)):
+            post.send(
+                gu_part.at[aligned(y * 512 + far * 128, 128)], gu_transit.at[slot, y], gut_sems.at[slot, y],
+                along.place(along.partner), along.outer,
+            )
+    for step in range(8):
+        other = (member + step) % 8
+        first = (other // 4) * 512 + (other % 4) * 32
+        post.send(
+            gu_part.at[aligned(first + along.partner * 128, 32)], gu_land.at[0, member], gu_sems.at[0, member],
+            (other // 4, along.partner * 4 + other % 4),
+        )
+        if step > 0:
+            post.send(
+                gu_part.at[aligned(first + z * 128, 32)], gu_land.at[2, member], gu_sems.at[2, member],
+                (other // 4, z * 4 + other % 4),
+            )
+    gu_land[2, pl.ds(member, 1)] = gu_part[aligned((member // 4) * 512 + z * 128 + (member % 4) * 32, 32), :][None]
 
     arrived(spot, part_sib, sib_sem.at[0], spare)
     part_sum = wdown.at[pl.ds(2048, 512), pl.ds(512, 512)]
@@ -733,11 +720,15 @@
         other = (seq + step) % devices
         post.send(part_sum.at[aligned(other * 32, 32)], wqkv_recv.at[own_slot], wqkv_sems.at[own_slot], (core, other))
 
-    dealt(att_all, 3)
-    whole(proj_all, 2)
+    pass_on(proj_all, proj_sems, "y")
+    pass_diagonal(proj_all, proj_sems)
+    dealt(att_all, attp_sems, 10)
+    whole(proj_all, proj_sems, 15)
     turned = jnp.concatenate([att_all[other] for other in range(8)], axis=1)
     wout_part[...] = dot(turned, proj_all[...].reshape(1024, 1024)).astype(LOW)
-    along.send(wout_part, 64, wout_land, wout_transit, wout_sems)
+    wout_land[pl.ds(z, 1)] = wout_part[aligned(z * 64, 64), :][None]
+    for far in spot.far_z:
+        post.send(wout_part.at[aligned(far * 64, 64)], wout_land.at[z], wout_sems.at[z], along.place(far))
     keep_vec.wait()
     for step in range(1, 8):
         other = (member + step) % 8
@@ -748,7 +739,6 @@
     vec_far[pl.ds(z, 1)] = vec[None]
     for far in spot.far_z:
         post.send(vec_far.at[z], vec_far.at[z], vec_sems.at[8 + z], along.place(far))
-    along.combine(wout_part, 64, wout_land, wout_transit, wout_sems)
 
     for step in range(1, devices):
         other = (seq + step) % devices
@@ -765,6 +755,21 @@
         grad_v.append(block[:, 384:])
     gradient = gradient + dot_nt(jnp.concatenate(grad_k, axis=1), wgate[:, 2048:])
     in_grad[...] = gradient + dot_nt(jnp.concatenate(grad_v, axis=1), wup[:, :1024])
+
+    for slot, far in enumerate((along.far_inner, along.far_outer)):
+        for y in range(2):
+
+            @pl.when(along.inner)
+            def _():
+                arrived(spot, gu_transit.at[slot, y], gut_sems.at[slot, y], spare)
+                added = gu_transit[slot, y].astype(WIDE) + gu_part[aligned(y * 512 + far * 128, 128), :].astype(WIDE)
+                gu_transit[slot, y] = added.astype(LOW)
+
+            for piece in range(4):
+                post.send(
+                    gu_transit.at[slot, y, pl.ds(piece * 32, 32)], gu_land.at[1, member], gu_sems.at[1, member],
+                    (y, far * 4 + piece), along.inner,
+                )
 
     for y in range(2):
         for micro in range(2):
@@ -801,7 +806,9 @@
         block = sum(gu_land[kind, slot].astype(WIDE) for kind in range(3))
         g_gate[:, slot * 384 : (slot + 1) * 384] = block[:, :384]
         g_up[:, slot * 384 : (slot + 1) * 384] = block[:, 384:]
-    g_out[...] = along.total(wout_land, wout_sems)
+    for far in spot.far_z:
+        arrived(spot, wout_land.at[far], wout_sems.at[far], spare)
+    g_out[...] = sum(wout_land[far].astype(WIDE) for far in range(4))
     post.finish()
 
 
@@ -866,8 +873,7 @@
             pltpu.VMEM((3, 96, width), LOW),
             pltpu.VMEM((2, 96, width), LOW),
             pltpu.VMEM((256, width), LOW),
-            pltpu.VMEM((3, 64, width), LOW),
-            pltpu.VMEM((2, 64, width), LOW),
+            pltpu.VMEM((4, 64, width), LOW),
             pltpu.VMEM((3, 8, 32, 768), LOW),
             pltpu.VMEM((2, 2, 128, 768), LOW),
             pltpu.VMEM((16, 64, 256), LOW),
@@ -883,7 +889,12 @@
             pltpu.SMEM((16,), jnp.int32),
             dma((17,)),
             dma((POST_SENDS,)),
-            dma((6, 8)),
+            dma((8,)),
+            dma((8,)),
+            dma((8,)),
+            dma((8,)),
+            dma((8,)),
+            dma((8,)),
             dma((12,)),
             dma((4,)),
             dma((4,)),

time: 237 us -> 209 us (0.88)
  Pallas kernels: 236 us -> 208 us
    pallas_call x1, Pallas kernels: 172 us -> 150 us  [row_backward(): pl.pallas_call(backward_kernel, out_shape=(shape((128, width), LOW), shap...]
    pallas_call x1, Pallas kernels: 60.1 us -> 54.8 us  [row_forward(): pl.pallas_call(forward_kernel, out_shape=(shape((2, 64, 2048), LOW), shap...]
where the time goes in v3:
time: 209 us
  Pallas kernels  208 us (100%)
    pallas_call x1, Pallas kernels, row_backward(): pl.pallas_call(backward_kernel, out_shape=(shape((128, width), LOW), shap...  150 us
    pallas_call x1, Pallas kernels, row_forward(): pl.pallas_call(forward_kernel, out_shape=(shape((2, 64, 2048), LOW), shap...  54.8 us

profile of v3, /device:TPU:0, one launch (start us, length us, event | category | flops | bytes accessed | tf_op | source)
XLA Modules:
  0.0 208.5 jit_solution(6044795572668653319)
XLA Ops:
  0.6 54.8 %row_forward.1 = (bf16[2,64,2048]{2,1,0:T(8,128)(2,1)}, bf16[1024,1024]{1,0:T(8,128)(2,1)}, bf16[8,256,128]{2,1,0:T(8,128)(2,1)}, bf16[1024,256]{1,0:T(8,128)(2,...) custom-call(bf16[2,64,1024]{2,1,0:T(8,128)(2,1)} %bitcast.16, bf16[1024,2048]{1,0:T(8,128)(2,1)} %wq_hbm.3, ...), custom_call_target="tpu_custom_call" | custom-call | tf_op jit(solution)/shard_map/row_forward/pallas_call | solution.py:305
  55.4 149.6 %row_backward.1 = (bf16[128,1024]{1,0:T(8,128)(2,1)}, f32[128,1024]{1,0:T(8,128)}, f32[32,2048]{1,0:T(8,128)}, f32[32,1024]{1,0:T(8,128)}, f32[32,1024]{1,0:T(8,...) custom-call(bf16[2,64,2048]{2,1,0:T(8,128)(2,1)} %get-tuple-element., ...), custom_call_target="tpu_custom_call" | custom-call | tf_op jit(solution)/shard_map/row_backward/pallas_call | solution.py:825
  205.0 3.3 %finish.1 = (bf16[128,1024]{1,0:T(8,128)(2,1)}, f32[128,1024]{1,0:T(8,128)}, f32[32,2048]{1,0:T(8,128)}, f32[32,1024]{1,0:T(8,128)}, f32[32,1024]{1,0:T(8,128)},...) custom-call(bf16[128,1024]{1,0:T(8,128)(2,1)} %get-tuple-element.51., ...), custom_call_target="tpu_custom_call" | custom-call | tf_op jit(solution)/shard_map/finish/pallas_call | solution.py:941

commit v4 on v3

--- a/solution.py
+++ b/solution.py
@@ -59,18 +59,6 @@
         )
 
 
-def greet_row(spot, devices):
-    barrier = pltpu.get_barrier_semaphore()
-    for step in range(1, devices):
-        pl.semaphore_signal(
-            barrier,
-            inc=1,
-            device_id=(spot.dp, (spot.seq + step) % devices),
-            device_id_type=MESH,
-        )
-    pl.semaphore_wait(barrier, devices - 1)
-
-
 class RowGather:
     def __init__(self, spot, own, held, local_sem, send_sems, recv_sems):
         self.spot, self.own, self.held = spot, own, held
@@ -121,6 +109,8 @@
             first = far * 4 + (1 - spot.x) * 2
             self.arrived(self.held.at[pl.ds(first, 2)], self.recv_sems.at[16 + far])
         self.local.wait()
+
+    def drain(self):
         for copy in self.sent:
             copy.wait_send()
 
@@ -134,7 +124,15 @@
     inside = table[pl.ds(64 + start, 64), :]
     shifted = table[pl.ds(64 + jnp.maximum(start - first_length, -64), 64), :]
     places = start + lax.broadcasted_iota(jnp.int32, (64, HD), 0)
-    return jnp.where(places < first_length, inside, shifted)
+    both = jnp.where(places < first_length, inside, shifted)
+    swapped = swap_halves(both)
+    low_half = lax.broadcasted_iota(jnp.int32, (64, HD), 1) < HD // 2
+    return jnp.where(low_half, both, swapped), jnp.where(low_half, -swapped, both)
+
+
+def rope_part(table, part, first_length):
+    first, second = (rope_rows(table, part * 2 + piece, first_length) for piece in range(2))
+    return jnp.concatenate([first[0], second[0]], axis=0), jnp.concatenate([first[1], second[1]], axis=0)
 
 
 def swap_halves(head):
@@ -169,74 +167,165 @@
     lax.fori_loop(0, 16, fill, 0)
 
 
-def forward_kernel(
-    tok_ref, wq_hbm, wk_hbm, wv_hbm, qgain_ref, kgain_ref, cos_ref, sine_ref,
-    order_ref, docs_ref,
-    att_tok, tok_nat, q_pair, kv_nat, hat, factors, lse,
-    att_nat, tok_all, wq_all, wk_all, wv_own, stat_all, att_send, att_recv, kv_turned,
-    inverse_ref, local_sems, send_sems, recv_sems, stat_send, stat_recv, att_ssem, att_rsem,
+class Post:
+    def __init__(self, sems):
+        self.sems, self.started, self.used = sems, [], 0
+
+    def send(self, source, target, recv_sem, place, when=None):
+        copy = remote(source, target, self.sems.at[self.used], recv_sem, place)
+        self.used += 1
+        self.started.append((copy, when))
+        if when is None:
+            copy.start()
+        else:
+            pl.when(when)(copy.start)
+
+    def finish(self):
+        started, self.started = self.started, []
+        for copy, when in started:
+            if when is None:
+                copy.wait_send()
+            else:
+                pl.when(when)(copy.wait_send)
+
+
+def arrived(spot, slot, recv_sem, spare_sem):
+    remote(slot, slot, spare_sem, recv_sem, (spot.dp, spot.sibling)).wait_recv()
+
+
+def aligned(start, size):
+    return pl.ds(pl.multiple_of(start, size), size)
+
+
+class AlongZ:
+    def __init__(self, spot, post, spare):
+        self.spot, self.post, self.spare = spot, post, spare
+        half = spot.z // 2
+        self.partner = spot.far_z[0]
+        self.far_inner = 2 - half
+        self.far_outer = 3 - 3 * half
+        self.inner = ((spot.z + 1) // 2) % 2 == 1
+        self.outer = ((spot.z + 1) // 2) % 2 == 0
+
+    def place(self, z):
+        return (self.spot.dp, z * 4 + self.spot.x * 2 + self.spot.core)
+
+    def send(self, part, size, landing, transit, sems):
+        spot, post = self.spot, self.post
+        landing[2] = part[aligned(spot.z * size, size), :]
+        for slot, far in enumerate((self.far_inner, self.far_outer)):
+            post.send(
+                part.at[aligned(far * size, size)], transit.at[slot], sems.at[2 + slot], self.place(self.partner),
+                self.outer,
+            )
+        post.send(part.at[aligned(self.partner * size, size)], landing.at[0], sems.at[0], self.place(self.partner))
+
+    def combine(self, part, size, landing, transit, sems):
+        for slot, far in enumerate((self.far_inner, self.far_outer)):
+
+            @pl.when(self.inner)
+            def _():
+                arrived(self.spot, transit.at[slot], sems.at[2 + slot], self.spare)
+                added = transit[slot].astype(WIDE) + part[aligned(far * size, size), :].astype(WIDE)
+                transit[slot] = added.astype(LOW)
+
+            self.post.send(transit.at[slot], landing.at[1], sems.at[1], self.place(far), self.inner)
+
+    def total(self, landing, sems):
+        arrived(self.spot, landing.at[0], sems.at[0], self.spare)
+        arrived(self.spot, landing.at[1], sems.at[1], self.spare)
+        return landing[0].astype(WIDE) + landing[1].astype(WIDE) + landing[2].astype(WIDE)
+
+
+def row_scale(values):
+    return lax.rsqrt(jnp.mean(values * values, axis=-1, keepdims=True) + EPSILON)
+
+
+def norm_back(grad, gain, normal, factor):
+    weighted = grad * gain
+    return factor * (weighted - normal * jnp.mean(weighted * normal, axis=-1, keepdims=True))
+
+
+def layer_kernel(
+    tok_ref, cot_ref, again_ref, mgain_ref, qgain_ref, kgain_ref,
+    rope_hbm, wout_hbm, wg_hbm, wu_hbm, wd_hbm, wq_hbm, wk_hbm, wv_hbm, order_ref, docs_ref,
+    layer_out, in_grad, g_query, g_key, g_value, g_out, vec_out, gain_out, g_gate, g_up, g_down,
+    tok_all, own_stats, factors, lse, att_recv,
+    wout, wgate, wup, wdown, q_pair, kv_nat, hat, rope_ref,
+    hidden, hid_own, gate_pre, up_pre, mix_turned, att_turned, down_own, gu_own, proj_own, ag_own, vec_own,
+    hid_all, down_all, proj_all, gu_all, mix_all, att_all, vec_all, vec_far,
+    down_land, down_transit, wout_land, gu_land, gu_transit,
+    ag_recv, ag_pair, k_turned, stat_all, grad_nat, grad_recv, part_sib, part_far, wqkv_recv, gain_own, gain_recv,
+    inverse_ref, send_sems, recv_sems, own_sems, att_sems,
+    local_sems, post_sems, hid_sems, dpl_sems, proj_sems, attp_sems, mix_sems, gup_sems,
+    vec_sems, down_sems, wout_sems, gu_sems, gut_sems, ag_sems, stat_sems, grad_sems, sib_sem, wqkv_sems, gain_sems,
 ):
     spot = Spot()
-    devices = 16
-    chips = 8
-    chip = spot.chip
-    loads = [
-        pltpu.make_async_copy(wq_hbm, wq_all, local_sems.at[1]),
-        pltpu.make_async_copy(wk_hbm, wk_all, local_sems.at[2]),
-        pltpu.make_async_copy(
-            wv_hbm.at[:, pl.ds(pl.multiple_of(chip * 128, 128), 128)], wv_own, local_sems.at[3]
-        ),
-    ]
-    for load in loads:
-        load.start()
-    greet_row(spot, devices)
-    gather = RowGather(spot, tok_ref, tok_all, local_sems.at[0], send_sems, recv_sems)
+    devices, chips = 16, 8
+    dp, seq, core, chip, z = spot.dp, spot.seq, spot.core, spot.chip, spot.z
+    me = dp * devices + seq
+    member = dp * 4 + spot.x * 2 + core
+    spare = post_sems.at[0]
+    post = Post(post_sems)
+    along = AlongZ(spot, post, spare)
+
+    def load(source, target, index):
+        copy = pltpu.make_async_copy(source, target, local_sems.at[index])
+        copy.start()
+        return copy
+
+    barrier = pltpu.get_barrier_semaphore()
+    for step in range(1, 2 * devices):
+        other = (me + step) % (2 * devices)
+        pl.semaphore_signal(barrier, inc=1, device_id=(other // devices, other % devices), device_id_type=MESH)
+    load_query = load(wq_hbm, wgate.at[:, pl.ds(0, 2048)], 1)
+    load_key = load(wk_hbm, wgate.at[:, pl.ds(2048, 1024)], 2)
+    load_value = load(wv_hbm.at[:, aligned(chip * 128, 128)], wup.at[:, pl.ds(0, 128)], 4)
+    load_rope = load(rope_hbm, rope_ref, 5)
+    load_out = load(wout_hbm, wout, 0)
+    load_down = load(wd_hbm, wdown, 3)
+    invert(order_ref, inverse_ref)
+    pl.semaphore_wait(barrier, 2 * devices - 1)
+    gather = RowGather(spot, tok_ref, tok_all, local_sems.at[8], send_sems, recv_sems)
     gather.start()
-    invert(order_ref, inverse_ref)
-
-    for load in loads:
-        load.wait()
+
+    load_query.wait()
+    load_key.wait()
     own = tok_ref[...].reshape(128, tok_ref.shape[-1])
     sums = []
-    for weight in (wq_all, wk_all):
-        parts = [dot(own, weight[:, first : first + 512]) for first in range(0, weight.shape[1], 512)]
-        sums.append(sum(jnp.sum(part * part, axis=-1, keepdims=True) for part in parts) / weight.shape[1])
-    stat_all[pl.ds(spot.seq, 1)] = lax.rsqrt(rows_of(sums[0], sums[1]) + EPSILON)[None]
-    stat_copies = []
+    for start, stop in ((0, 2048), (2048, 3072)):
+        parts = [dot(own, wgate[:, first : first + 512]) for first in range(start, stop, 512)]
+        sums.append(sum(jnp.sum(part * part, axis=-1, keepdims=True) for part in parts) / (stop - start))
+    own_stats[pl.ds(seq, 1)] = lax.rsqrt(rows_of(sums[0], sums[1]) + EPSILON)[None]
     for step in range(1, devices):
-        other = (spot.seq + step) % devices
-        copy = remote(
-            stat_all.at[spot.seq], stat_all.at[spot.seq], stat_send.at[step], stat_recv.at[spot.seq], (spot.dp, other)
-        )
-        copy.start()
-        stat_copies.append(copy)
+        post.send(own_stats.at[seq], own_stats.at[seq], own_sems.at[seq], (dp, (seq + step) % devices))
     gather.forward()
     for step in range(1, devices):
-        other = (spot.seq + step) % devices
-        remote(
-            stat_all.at[other], stat_all.at[other], stat_send.at[0], stat_recv.at[other], (spot.dp, spot.sibling)
-        ).wait_recv()
+        other = (seq + step) % devices
+        arrived(spot, own_stats.at[other], own_sems.at[other], spare)
     gather.finish()
 
-    first_length = docs_ref[spot.core, 0, 0]
+    first_length = docs_ref[core, 0, 0]
+    load_value.wait()
     for part in range(4):
         rows = pl.ds(part * CHUNK, CHUNK)
         chunk = jnp.concatenate([tok_all[inverse_ref[part * 4 + piece]] for piece in range(4)], axis=0)
-        tok_nat[rows, :] = chunk
-        hat[rows, :256] = dot(chunk, wq_all[:, pl.ds(pl.multiple_of(chip * 256, 256), 256)])
-        hat[rows, 256:] = dot(chunk, wk_all[:, pl.ds(pl.multiple_of(chip * 128, 128), 128)])
-        kv_nat[rows, 128:] = dot(chunk, wv_own[...]).astype(LOW)
+        hat[rows, :256] = dot(chunk, wgate[:, aligned(chip * 256, 256)])
+        hat[rows, 256:] = dot(chunk, wgate[:, pl.ds(pl.multiple_of(2048 + chip * 128, 128), 128)])
+        kv_nat[rows, 128:] = dot(chunk, wup[:, :128]).astype(LOW)
+    load_gate = load(wg_hbm, wgate, 1)
+    load_up = load(wu_hbm, wup, 7)
     for block in range(16):
-        both = stat_all[inverse_ref[block]]
-        both = jnp.where(spot.core == 0, both, pltpu.roll(both, 64, axis=1))
+        both = own_stats[inverse_ref[block]]
+        both = jnp.where(core == 0, both, pltpu.roll(both, 64, axis=1))
         factors[:, block * 64 : (block + 1) * 64] = both[:, :64]
+    load_rope.wait()
     qgain = qgain_ref[pl.ds(chip * 2, 2), :]
     kgain = kgain_ref[pl.ds(chip, 1), :]
     for part in range(8):
         rows = pl.ds(part * TILE, TILE)
         scale = columns_of(factors[:, rows])
-        cos = jnp.concatenate([rope_rows(cos_ref, part * 2 + piece, first_length) for piece in range(2)], axis=0)
-        sine = jnp.concatenate([rope_rows(sine_ref, part * 2 + piece, first_length) for piece in range(2)], axis=0)
+        cos, sine = rope_part(rope_ref, part, first_length)
         for head in range(3):
             lanes = pl.ds(head * HD, HD)
             column = scale[:, 0:1] if head < 2 else scale[:, 1:2]
@@ -249,7 +338,7 @@
                 q_pair[part, pl.ds(head * HD, HD), :] = turned
             else:
                 kv_nat[rows, :HD] = turned
-    kv_turned[...] = kv_nat[:, HD:].T
+    k_turned[...] = kv_nat[:, HD:].T
     for tile in range(8):
         count = (tile + 1) * TILE
         scores = dot_nt(kv_nat[:count, :HD], q_pair[tile]) * HD ** (-0.5)
@@ -258,218 +347,27 @@
         terms = jnp.exp(masked - top)
         weight = jnp.sum(terms, axis=0, keepdims=True)
         lse[pl.ds(tile, 1), :] = top + jnp.log(weight)
-        turned = dot(kv_turned[:, :count], terms.astype(LOW)) / weight
+        turned = dot(k_turned[:, :count], terms.astype(LOW)) / weight
         attended = turned.T.astype(LOW)
-        att_nat[pl.ds(tile * 2, 2), :, :HD] = attended[:TILE].reshape(2, 64, HD)
-        att_nat[pl.ds(tile * 2, 2), :, HD:] = attended[TILE:].reshape(2, 64, HD)
-    own_part = (spot.core, slice(None), pl.ds(pl.multiple_of(chip * 256, 256), 256))
-    att_recv[pl.ds(chip, 1), pl.ds(spot.core, 1)] = att_nat[order_ref[spot.seq]][None, None]
-    sent = []
+        grad_nat[pl.ds(tile * 2, 2), :, :HD] = attended[:TILE].reshape(2, 64, HD)
+        grad_nat[pl.ds(tile * 2, 2), :, HD : 2 * HD] = attended[TILE:].reshape(2, 64, HD)
+    att_recv[pl.ds(chip, 1), pl.ds(core, 1)] = grad_nat[order_ref[seq], :, : 2 * HD][None, None]
     for step in range(1, devices):
-        other = (spot.seq + step) % devices
-        att_send[step] = att_nat[order_ref[other]]
-        copy = remote(
-            att_send.at[step], att_recv.at[chip, spot.core], att_ssem.at[step],
-            att_rsem.at[spot.seq], (spot.dp, other),
-        )
-        copy.start()
-        sent.append(copy)
+        other = (seq + step) % devices
+        slot = (step % 2, slice(None), slice((step // 2) * 256, (step // 2 + 1) * 256))
+        ag_own[slot] = grad_nat[order_ref[other], :, : 2 * HD]
+        post.send(ag_own.at[slot], att_recv.at[chip, core], att_sems.at[seq], (dp, other))
     for step in range(1, devices):
-        other = (spot.seq + step) % devices
-        slot = att_recv.at[other // 2, other % 2]
-        remote(slot, slot, att_ssem.at[0], att_rsem.at[other], (spot.dp, spot.sibling)).wait_recv()
-    for piece in range(chips):
-        for micro in range(2):
-            att_tok[micro, :, piece * 256 : (piece + 1) * 256] = att_recv[piece, micro]
-    for copy in sent + stat_copies:
-        copy.wait_send()
-
-
-def rope_constants(length):
-    frequency = np.power(np.float32(ROPE_BASE), -np.arange(0, HD, 2).astype(np.float32) / np.float32(HD)).astype(np.float32)
-    angles = (np.arange(length, dtype=np.float32)[:, None] * frequency[None, :]).astype(np.float32).astype(np.float64)
-    cos, sine = np.cos(angles), np.sin(angles)
-    front = np.zeros((64, HD))
-    cos = np.concatenate([front, np.concatenate([cos, cos], axis=1)], axis=0)
-    sine = np.concatenate([front, np.concatenate([-sine, sine], axis=1)], axis=0)
-    return jnp.asarray(cos, WIDE), jnp.asarray(sine, WIDE)
-
-
-def row_forward(tokens, w_query, w_key, w_value, q_gain, k_gain, cos, sine, order, docs):
-    length = 1024
-    width = tokens.shape[-1]
-    any_spec = pl.BlockSpec(memory_space=pl.ANY)
-    vmem = pl.BlockSpec(memory_space=pltpu.VMEM)
-    smem = pl.BlockSpec(memory_space=pltpu.SMEM)
-    shape = jax.ShapeDtypeStruct
-    return pl.pallas_call(
-        forward_kernel,
-        out_shape=(
-            shape((2, 64, 2048), LOW),
-            shape((length, width), LOW),
-            shape((8, 2 * TILE, HD), LOW),
-            shape((length, 2 * HD), LOW),
-            shape((length, 3 * HD), WIDE),
-            shape((8, length), WIDE),
-            shape((8, 2 * TILE), WIDE),
-        ),
-        in_specs=[vmem, any_spec, any_spec, any_spec, vmem, vmem, vmem, vmem, smem, smem],
-        out_specs=(vmem,) * 7,
-        scratch_shapes=[
-            pltpu.VMEM((16, 64, 2 * HD), LOW),
-            pltpu.VMEM((16, 64, width), LOW),
-            pltpu.VMEM((width, 2048), LOW),
-            pltpu.VMEM((width, 1024), LOW),
-            pltpu.VMEM((width, 128), LOW),
-            pltpu.VMEM((16, 8, 128), WIDE),
-            pltpu.VMEM((16, 64, 2 * HD), LOW),
-            pltpu.VMEM((8, 2, 64, 2 * HD), LOW),
-            pltpu.VMEM((HD, length), LOW),
-            pltpu.SMEM((16,), jnp.int32),
-            pltpu.SemaphoreType.DMA((4,)),
-            pltpu.SemaphoreType.DMA((GATHER_SENDS,)),
-            pltpu.SemaphoreType.DMA((GATHER_RECVS,)),
-            pltpu.SemaphoreType.DMA((16,)),
-            pltpu.SemaphoreType.DMA((16,)),
-            pltpu.SemaphoreType.DMA((16,)),
-            pltpu.SemaphoreType.DMA((16,)),
-        ],
-        compiler_params=pltpu.CompilerParams(
-            collective_id=0, has_side_effects=True, vmem_limit_bytes=56 * 2**20
-        ),
-        name="row_forward",
-    )(tokens, w_query, w_key, w_value, q_gain, k_gain, cos, sine, order, docs)
-
-
-class Post:
-    def __init__(self, sems):
-        self.sems, self.started, self.used = sems, [], 0
-
-    def send(self, source, target, recv_sem, place, when=None):
-        copy = remote(source, target, self.sems.at[self.used], recv_sem, place)
-        self.used += 1
-        self.started.append((copy, when))
-        if when is None:
-            copy.start()
-        else:
-            pl.when(when)(copy.start)
-
-    def finish(self):
-        for copy, when in self.started:
-            if when is None:
-                copy.wait_send()
-            else:
-                pl.when(when)(copy.wait_send)
-
-
-def arrived(spot, slot, recv_sem, spare_sem):
-    remote(slot, slot, spare_sem, recv_sem, (spot.dp, spot.sibling)).wait_recv()
-
-
-def aligned(start, size):
-    return pl.ds(pl.multiple_of(start, size), size)
-
-
-class AlongZ:
-    def __init__(self, spot, post, spare):
-        self.spot, self.post, self.spare = spot, post, spare
-        half = spot.z // 2
-        self.partner = spot.far_z[0]
-        self.far_inner = 2 - half
-        self.far_outer = 3 - 3 * half
-        self.inner = ((spot.z + 1) // 2) % 2 == 1
-        self.outer = ((spot.z + 1) // 2) % 2 == 0
-
-    def place(self, z):
-        return (self.spot.dp, z * 4 + self.spot.x * 2 + self.spot.core)
-
-    def send(self, part, size, landing, transit, sems):
-        spot, post = self.spot, self.post
-        landing[2] = part[aligned(spot.z * size, size), :]
-        for slot, far in enumerate((self.far_inner, self.far_outer)):
-            post.send(
-                part.at[aligned(far * size, size)], transit.at[slot], sems.at[2 + slot], self.place(self.partner),
-                self.outer,
-            )
-        post.send(part.at[aligned(self.partner * size, size)], landing.at[0], sems.at[0], self.place(self.partner))
-
-    def combine(self, part, size, landing, transit, sems):
-        for slot, far in enumerate((self.far_inner, self.far_outer)):
-
-            @pl.when(self.inner)
-            def _():
-                arrived(self.spot, transit.at[slot], sems.at[2 + slot], self.spare)
-                added = transit[slot].astype(WIDE) + part[aligned(far * size, size), :].astype(WIDE)
-                transit[slot] = added.astype(LOW)
-
-            self.post.send(transit.at[slot], landing.at[1], sems.at[1], self.place(far), self.inner)
-
-    def total(self, landing, sems):
-        arrived(self.spot, landing.at[0], sems.at[0], self.spare)
-        arrived(self.spot, landing.at[1], sems.at[1], self.spare)
-        return landing[0].astype(WIDE) + landing[1].astype(WIDE) + landing[2].astype(WIDE)
-
-
-def row_scale(values):
-    return lax.rsqrt(jnp.mean(values * values, axis=-1, keepdims=True) + EPSILON)
-
-
-def norm_back(grad, gain, normal, factor):
-    weighted = grad * gain
-    return factor * (weighted - normal * jnp.mean(weighted * normal, axis=-1, keepdims=True))
-
-
-def backward_kernel(
-    att_ref, tok_ref, cot_ref, again_ref, mgain_ref, qgain_ref, kgain_ref, factors, lse,
-    tok_hbm, q_hbm, kv_hbm, hat_hbm, cos_hbm, sine_hbm,
-    wout_hbm, wg_hbm, wu_hbm, wd_hbm, wq_hbm, wk_hbm, wv_hbm, order_ref, docs_ref,
-    layer_out, in_grad, g_query, g_key, g_value, g_out, vec_out, gain_out, g_gate, g_up, g_down,
-    wout, wgate, wup, wdown, q_pair, kv_nat, hat, cos_ref, sine_ref,
-    att_hat, hidden, hid_own, gate_pre, up_pre, mixed, mix_turned, att_turned, down_own, gu_own, proj_own, ag_own, vec_own,
-    hid_all, down_all, proj_all, gu_all, mix_all, att_all, vec_all, vec_far,
-    down_land, down_transit, wout_part, wout_land, gu_land, gu_transit,
-    ag_recv, ag_pair, k_turned, stat_all, grad_nat, grad_recv, part_sib, wqkv_recv, gain_own, gain_recv,
-    inverse_ref, local_sems, post_sems, hid_sems, dpl_sems, proj_sems, attp_sems, mix_sems, gup_sems, vec_sems, down_sems, wout_sems, gu_sems, gut_sems, ag_sems, stat_sems, grad_sems, sib_sem, wqkv_sems, gain_sems,
-):
-    spot = Spot()
-    devices, chips = 16, 8
-    dp, seq, core, chip, z = spot.dp, spot.seq, spot.core, spot.chip, spot.z
-    me = dp * devices + seq
-    member = dp * 4 + spot.x * 2 + core
-    spare = post_sems.at[0]
-    post = Post(post_sems)
-    along = AlongZ(spot, post, spare)
-
-    def load(source, target, index):
-        copy = pltpu.make_async_copy(source, target, local_sems.at[index])
-        copy.start()
-        return copy
-
-    barrier = pltpu.get_barrier_semaphore()
-    for step in range(1, 2 * devices):
-        other = (me + step) % (2 * devices)
-        pl.semaphore_signal(barrier, inc=1, device_id=(other // devices, other % devices), device_id_type=MESH)
-    load_out = load(wout_hbm, wout, 0)
-    load_gate = load(wg_hbm, wgate, 1)
-    load_up = load(wu_hbm, wup, 2)
-    load_down = load(wd_hbm, wdown, 3)
-    later = [load(kv_hbm, kv_nat, 4), load(q_hbm, q_pair, 5), load(hat_hbm, hat, 6), load(cos_hbm, cos_ref, 7), load(sine_hbm, sine_ref, 8)]
-    invert(order_ref, inverse_ref)
+        other = (seq + step) % devices
+        arrived(spot, att_recv.at[other // 2, other % 2], att_sems.at[other], spare)
+    post.finish()
 
     for group in range(8):
-        block = att_ref[:, :, group * 256 : (group + 1) * 256].reshape(128, 256).T
+        attended = att_recv[group]
+        ag_own[:, :, group * 256 : (group + 1) * 256] = attended
+        block = attended.reshape(128, 256).T
         for piece in range(4):
             att_turned[(group // 4) * 4 + piece, pl.ds((group % 4) * 64, 64), :] = block[piece * 64 : (piece + 1) * 64]
-    load_out.wait()
-    attn_proj = dot(att_ref[...].reshape(128, 2048), wout[...])
-    att_factor = row_scale(attn_proj)
-    normal = attn_proj * att_factor
-    att_hat[...] = normal
-    stream = tok_ref[...].reshape(128, 1024).astype(WIDE) + normal * again_ref[...]
-    hidden[...] = stream
-    hid_own[...] = stream.astype(LOW)
-    pl.semaphore_wait(barrier, 2 * devices - 1)
-
     x_place, y_place, sib_place = (dp, spot.flip_x), (1 - dp, seq), (dp, spot.sibling)
     x_member = dp * 4 + (1 - spot.x) * 2 + core
     y_member = (1 - dp) * 4 + spot.x * 2 + core
@@ -512,6 +410,15 @@
             other = (member + step) % 8
             arrived(spot, held.at[other], sems.at[other], spare)
 
+    deal(att_turned, att_all, attp_sems, 10)
+    load_out.wait()
+    attn_proj = dot(ag_own[...].reshape(128, 2048), wout[...])
+    att_factor = row_scale(attn_proj)
+    normal = attn_proj * att_factor
+    in_grad[...] = normal
+    stream = tok_ref[...].reshape(128, 1024).astype(WIDE) + normal * again_ref[...]
+    hidden[...] = stream
+    hid_own[...] = stream.astype(LOW)
     spread(hid_own, hid_all, hid_sems, 9)
 
     load_gate.wait()
@@ -523,21 +430,24 @@
         gate_pre[group] = gate
         up_pre[group] = up
         block = (gate * jax.nn.sigmoid(gate) * up).astype(LOW)
-        mixed[:, lanes] = block
+        gu_own[group, :, :384] = block
         turned = block.T
         for piece in range(4):
             mix_turned[(group // 4) * 4 + piece, pl.ds((group % 4) * 96, 96), :] = turned[piece * 96 : (piece + 1) * 96]
     deal(mix_turned, mix_all, mix_sems, 11)
     pass_on(hid_all, hid_sems, "y")
     load_down.wait()
-    down_pre = dot(mixed[...], wdown[...])
+    down_pre = jnp.zeros((128, 1024), WIDE)
+    for group in range(8):
+        down_pre = down_pre + dot(gu_own[group, :, :384], wdown[group * 384 : (group + 1) * 384, :])
     factor = row_scale(down_pre)
     normal = down_pre * factor
     cot = cot_ref[...].reshape(128, 1024).astype(WIDE)
     layer_out[...] = (hidden[...] + normal * mgain_ref[...]).astype(LOW)
     down_own[...] = norm_back(cot, mgain_ref[...], normal, factor).astype(LOW)
-    vec_own[...] = jnp.zeros_like(vec_own)
-    vec_own[1:2, :] = jnp.sum(cot * normal, axis=0, keepdims=True)
+    mlp_sum = jnp.sum(cot * normal, axis=0, keepdims=True)
+    for piece in range(4):
+        vec_own[4 + piece : 5 + piece, :] = mlp_sum[:, piece * 256 : (piece + 1) * 256]
     spread(down_own, down_all, dpl_sems, 12)
 
     for step in range(1, 9):
@@ -552,9 +462,11 @@
         lanes = slice(group * 384, (group + 1) * 384)
         hgrad = hgrad + dot_nt(gu_own[group, :, :384], wgate[:, lanes]) + dot_nt(gu_own[group, :, 384:], wup[:, lanes])
     hidden[...] = hgrad
-    normal = att_hat[...]
+    normal = in_grad[...]
     proj_own[...] = norm_back(hgrad, again_ref[...], normal, att_factor).astype(LOW)
-    vec_own[0:1, :] = jnp.sum(hgrad * normal, axis=0, keepdims=True)
+    attn_sum = jnp.sum(hgrad * normal, axis=0, keepdims=True)
+    for piece in range(4):
+        vec_own[piece : piece + 1, :] = attn_sum[:, piece * 256 : (piece + 1) * 256]
     load_query = load(wq_hbm, wgate.at[:, pl.ds(0, 2048)], 1)
     load_key = load(wk_hbm, wgate.at[:, pl.ds(2048, 1024)], 2)
     load_value = load(wv_hbm, wup.at[:, pl.ds(0, 1024)], 3)
@@ -567,18 +479,14 @@
         post.send(
             ag_own.at[other % 2, :, aligned((other // 2) * 256, 256)], ag_recv.at[seq], ag_sems.at[seq], (dp, other)
         )
-    load_tok = load(tok_hbm, wout.at[pl.ds(0, 1024)], 0)
-    pass_diagonal(hid_all, hid_sems)
-    pass_on(down_all, dpl_sems, "x")
-    deal(gu_own, gu_all, gup_sems, 13)
-    deal(att_turned, att_all, attp_sems, 10)
-    spread(proj_own, proj_all, proj_sems, 15)
     keep_vec = load(vec_own, vec_all.at[member], 16)
     for step in range(1, 8):
         other = (member + step) % 8
         post.send(vec_own, vec_all.at[member], vec_sems.at[member], (other // 4, z * 4 + other % 4))
-    for copy in later:
-        copy.wait()
+    pass_diagonal(hid_all, hid_sems)
+    pass_on(down_all, dpl_sems, "x")
+    spread(proj_own, proj_all, proj_sems, 15)
+    deal(gu_own, gu_all, gup_sems, 13)
     keep_ag.wait()
     for step in range(1, devices):
         other = (seq + step) % devices
@@ -588,7 +496,6 @@
         ag_pair[tile, :TILE, :] = block[:, :HD]
         ag_pair[tile, TILE:, :] = block[:, HD:]
     k_turned[...] = kv_nat[:, :HD].T
-    first_length = docs_ref[core, 0, 0]
     up_pre[:, :, :256] = jnp.zeros((8, TILE, 256), WIDE)
     down_part = wdown.at[pl.ds(0, 384)]
     for tile in range(7, -1, -1):
@@ -613,13 +520,22 @@
         gate_pre[tile, :, :HD] = turned[:TILE]
         gate_pre[tile, :, HD:256] = turned[TILE:]
 
-    qgain = qgain_ref[pl.ds(chip * 2, 2), :]
-    kgain = kgain_ref[pl.ds(chip, 1), :]
+    pass_on(proj_all, proj_sems, "y")
+    keep_vec.wait()
+    for step in range(1, 8):
+        other = (member + step) % 8
+        arrived(spot, vec_all.at[other], vec_sems.at[other], spare)
+    vec = vec_all[0]
+    for other in range(1, 8):
+        vec = vec + vec_all[other]
+    vec_far[pl.ds(z, 1)] = vec[None]
+    for far in spot.far_z:
+        post.send(vec_far.at[z], vec_far.at[z], vec_sems.at[8 + z], along.place(far))
+
     gains = [jnp.zeros((1, HD), WIDE) for _ in range(3)]
     for part in range(8):
         rows = pl.ds(part * TILE, TILE)
-        cos = jnp.concatenate([rope_rows(cos_ref, part * 2 + piece, first_length) for piece in range(2)], axis=0)
-        sine = jnp.concatenate([rope_rows(sine_ref, part * 2 + piece, first_length) for piece in range(2)], axis=0)
+        cos, sine = rope_part(rope_ref, part, first_length)
         dots = []
         for head in range(3):
             lanes = slice(head * HD, (head + 1) * HD)
@@ -670,28 +586,38 @@
             grad = scale[:, column : column + 1] * (weighted - normal * mean[:, column : column + 1])
             grad_nat[pl.ds(part * 2, 2), :, head * HD : (head + 1) * HD] = grad.astype(LOW).reshape(2, 64, HD)
         grad_nat[pl.ds(part * 2, 2), :, 3 * HD :] = up_pre[part, :, HD:256].astype(LOW).reshape(2, 64, HD)
-    grad_recv[pl.ds(chip, 1), pl.ds(core, 1)] = grad_nat[order_ref[seq]][None, None]
-    for step in range(1, devices):
+    for step in range(devices):
         other = (seq + step) % devices
-        rows = pl.ds(step * 64, 64)
-        grad_send[rows, :] = grad_nat[order_ref[other]]
-        post.send(grad_send.at[rows], grad_recv.at[chip, core], grad_sems.at[seq], (dp, other))
-
-    load_tok.wait()
+        rows = aligned(other * 64, 64)
+        block = grad_nat[order_ref[other]]
+        grad_send[rows, :] = block
+        if step > 0:
+            post.send(grad_send.at[rows], grad_recv.at[chip, core], grad_sems.at[seq], (dp, other))
+        else:
+            grad_recv[pl.ds(chip, 1), pl.ds(core, 1)] = block[None, None]
+
     part_low = wdown.at[pl.ds(2048, 1024), pl.ds(0, 512)]
-    part_low[...] = dot_tn(wout[:1024, :], grad_nat[...].reshape(1024, 512)).astype(LOW)
+    for first in range(0, 1024, 256):
+        part = dot_tn(tok_all[:, :, first : first + 256].reshape(1024, 256), grad_send[...])
+        part_low[first : first + 256, :] = part.astype(LOW)
     post.send(part_low.at[aligned((1 - core) * 512, 512)], part_sib, sib_sem.at[0], sib_place)
 
     dealt(gu_all, gup_sems, 13)
     whole(hid_all, hid_sems, 9)
     gu_part = wout.at[pl.ds(1024, 1024), pl.ds(0, 768)]
-    gu_part[...] = dot_tn(hid_all[...].reshape(1024, 1024), gu_all[...].reshape(1024, 768)).astype(LOW)
+    for first in range(0, 1024, 256):
+        part = dot_tn(hid_all[:, :, first : first + 256].reshape(1024, 256), gu_all[...].reshape(1024, 768))
+        gu_part[first : first + 256, :] = part.astype(LOW)
     for y in range(2):
         for slot, far in enumerate((along.far_inner, along.far_outer)):
             post.send(
                 gu_part.at[aligned(y * 512 + far * 128, 128)], gu_transit.at[slot, y], gut_sems.at[slot, y],
                 along.place(along.partner), along.outer,
             )
+    arrived(spot, part_sib, sib_sem.at[0], spare)
+    part_sum = wdown.at[pl.ds(2048, 512), pl.ds(512, 512)]
+    part_sum[...] = (part_low[aligned(core * 512, 512), :].astype(WIDE) + part_sib[...].astype(WIDE)).astype(LOW)
+    post.send(part_sum.at[aligned((1 - dp) * 256, 256)], part_far, sib_sem.at[1], y_place)
     for step in range(8):
         other = (member + step) % 8
         first = (other // 4) * 512 + (other % 4) * 32
@@ -706,40 +632,32 @@
             )
     gu_land[2, pl.ds(member, 1)] = gu_part[aligned((member // 4) * 512 + z * 128 + (member % 4) * 32, 32), :][None]
 
-    arrived(spot, part_sib, sib_sem.at[0], spare)
-    part_sum = wdown.at[pl.ds(2048, 512), pl.ds(512, 512)]
-    part_sum[...] = (part_low[aligned(core * 512, 512), :].astype(WIDE) + part_sib[...].astype(WIDE)).astype(LOW)
-    own_slot = dp * chips + chip
-
-    @pl.when(core == dp)
-    def _():
-        wqkv_recv[pl.ds(own_slot, 1)] = part_sum[aligned(seq * 32, 32), :][None]
-
-    post.send(part_sum.at[aligned(seq * 32, 32)], wqkv_recv.at[own_slot], wqkv_sems.at[own_slot], (1 - dp, seq), core != dp)
-    for step in range(1, devices):
-        other = (seq + step) % devices
-        post.send(part_sum.at[aligned(other * 32, 32)], wqkv_recv.at[own_slot], wqkv_sems.at[own_slot], (core, other))
-
-    pass_on(proj_all, proj_sems, "y")
+    arrived(spot, part_far, sib_sem.at[1], spare)
+    part_end = wdown.at[pl.ds(2560, 256), pl.ds(512, 512)]
+    part_end[...] = (part_sum[aligned(dp * 256, 256), :].astype(WIDE) + part_far[...].astype(WIDE)).astype(LOW)
+    for step in range(8):
+        slot = (seq + step) % 8
+        other = dp * 8 + slot
+        rows = aligned(slot * 32, 32)
+
+        @pl.when((core == dp) & (other == seq))
+        def _():
+            wqkv_recv[pl.ds(chip, 1)] = part_end[rows, :][None]
+
+        post.send(
+            part_end.at[rows], wqkv_recv.at[chip], wqkv_sems.at[chip], (core, other),
+            (core != dp) | (other != seq),
+        )
+
     pass_diagonal(proj_all, proj_sems)
     dealt(att_all, attp_sems, 10)
     whole(proj_all, proj_sems, 15)
     turned = jnp.concatenate([att_all[other] for other in range(8)], axis=1)
+    wout_part = wdown.at[pl.ds(384, 256)]
     wout_part[...] = dot(turned, proj_all[...].reshape(1024, 1024)).astype(LOW)
     wout_land[pl.ds(z, 1)] = wout_part[aligned(z * 64, 64), :][None]
     for far in spot.far_z:
         post.send(wout_part.at[aligned(far * 64, 64)], wout_land.at[z], wout_sems.at[z], along.place(far))
-    keep_vec.wait()
-    for step in range(1, 8):
-        other = (member + step) % 8
-        arrived(spot, vec_all.at[other], vec_sems.at[other], spare)
-    vec = vec_all[0]
-    for other in range(1, 8):
-        vec = vec + vec_all[other]
-    vec_far[pl.ds(z, 1)] = vec[None]
-    for far in spot.far_z:
-        post.send(vec_far.at[z], vec_far.at[z], vec_sems.at[8 + z], along.place(far))
-
     for step in range(1, devices):
         other = (seq + step) % devices
         arrived(spot, grad_recv.at[other // 2, other % 2], grad_sems.at[other], spare)
@@ -781,15 +699,15 @@
                 arrived(spot, gain_recv.at[source], gain_sems.at[source], spare)
 
     gain_out[...] = sum(gain_recv[source] for source in range(4))
-    for source in range(16):
-        sender = (source // chips) * devices + (source % chips) * 2 + dp
+    for source in range(chips):
+        sender = (seq // 8) * devices + source * 2 + dp
 
         @pl.when(sender != me)
         def _():
             arrived(spot, wqkv_recv.at[source], wqkv_sems.at[source], spare)
 
     for piece in range(chips):
-        block = wqkv_recv[piece].astype(WIDE) + wqkv_recv[chips + piece].astype(WIDE)
+        block = wqkv_recv[piece].astype(WIDE)
         g_query[:, piece * 256 : (piece + 1) * 256] = block[:, :256]
         g_key[:, piece * 128 : (piece + 1) * 128] = block[:, 256:384]
         g_value[:, piece * 128 : (piece + 1) * 128] = block[:, 384:]
@@ -810,12 +728,13 @@
         arrived(spot, wout_land.at[far], wout_sems.at[far], spare)
     g_out[...] = sum(wout_land[far].astype(WIDE) for far in range(4))
     post.finish()
-
-
-POST_SENDS = 288
-
-
-def row_backward(*operands):
+    gather.drain()
+
+
+POST_SENDS = 256
+
+
+def whole_layer(*operands):
     length, width = 1024, 1024
     any_spec = pl.BlockSpec(memory_space=pl.ANY)
     vmem = pl.BlockSpec(memory_space=pltpu.VMEM)
@@ -823,7 +742,7 @@
     shape = jax.ShapeDtypeStruct
     dma = pltpu.SemaphoreType.DMA
     return pl.pallas_call(
-        backward_kernel,
+        layer_kernel,
         out_shape=(
             shape((128, width), LOW),
             shape((128, width), WIDE),
@@ -831,15 +750,20 @@
             shape((32, 1024), WIDE),
             shape((32, 1024), WIDE),
             shape((64, 1024), WIDE),
-            shape((8, 1024), WIDE),
+            shape((8, 256), WIDE),
             shape((8, 384), WIDE),
             shape((32, 3072), WIDE),
             shape((32, 3072), WIDE),
             shape((96, 1024), WIDE),
         ),
-        in_specs=[vmem] * 9 + [any_spec] * 13 + [smem] * 2,
+        in_specs=[vmem] * 6 + [any_spec] * 8 + [smem] * 2,
         out_specs=(vmem,) * 11,
         scratch_shapes=[
+            pltpu.VMEM((16, 64, width), LOW),
+            pltpu.VMEM((16, 8, HD), WIDE),
+            pltpu.VMEM((8, length), WIDE),
+            pltpu.VMEM((8, 2 * TILE), WIDE),
+            pltpu.VMEM((8, 2, 64, 2 * HD), LOW),
             pltpu.VMEM((2048, width), LOW),
             pltpu.VMEM((width, 3072), LOW),
             pltpu.VMEM((width, 3072), LOW),
@@ -848,31 +772,27 @@
             pltpu.VMEM((length, 2 * HD), LOW),
             pltpu.VMEM((length, 3 * HD), WIDE),
             pltpu.VMEM((length + 64, HD), WIDE),
-            pltpu.VMEM((length + 64, HD), WIDE),
-            pltpu.VMEM((128, width), WIDE),
             pltpu.VMEM((128, width), WIDE),
             pltpu.VMEM((128, width), LOW),
             pltpu.VMEM((8, 128, 384), WIDE),
             pltpu.VMEM((8, 128, 384), WIDE),
-            pltpu.VMEM((128, 3072), LOW),
             pltpu.VMEM((8, 384, 128), LOW),
             pltpu.VMEM((8, 256, 128), LOW),
             pltpu.VMEM((128, width), LOW),
             pltpu.VMEM((8, 128, 768), LOW),
             pltpu.VMEM((128, width), LOW),
             pltpu.VMEM((2, 64, 2048), LOW),
-            pltpu.VMEM((8, width), WIDE),
+            pltpu.VMEM((8, 256), WIDE),
             pltpu.VMEM((8, 128, width), LOW),
             pltpu.VMEM((8, 128, width), LOW),
             pltpu.VMEM((8, 128, width), LOW),
             pltpu.VMEM((8, 128, 768), LOW),
             pltpu.VMEM((8, 384, 128), LOW),
             pltpu.VMEM((8, 256, 128), LOW),
-            pltpu.VMEM((8, 8, width), WIDE),
-            pltpu.VMEM((4, 8, width), WIDE),
+            pltpu.VMEM((8, 8, 256), WIDE),
+            pltpu.VMEM((4, 8, 256), WIDE),
             pltpu.VMEM((3, 96, width), LOW),
             pltpu.VMEM((2, 96, width), LOW),
-            pltpu.VMEM((256, width), LOW),
             pltpu.VMEM((4, 64, width), LOW),
             pltpu.VMEM((3, 8, 32, 768), LOW),
             pltpu.VMEM((2, 2, 128, 768), LOW),
@@ -883,10 +803,15 @@
             pltpu.VMEM((16, 64, 512), LOW),
             pltpu.VMEM((8, 2, 64, 512), LOW),
             pltpu.VMEM((512, 512), LOW),
-            pltpu.VMEM((16, 32, 512), LOW),
+            pltpu.VMEM((256, 512), LOW),
+            pltpu.VMEM((8, 32, 512), LOW),
             pltpu.VMEM((8, 384), WIDE),
             pltpu.VMEM((4, 8, 384), WIDE),
             pltpu.SMEM((16,), jnp.int32),
+            dma((GATHER_SENDS,)),
+            dma((GATHER_RECVS,)),
+            dma((16,)),
+            dma((16,)),
             dma((17,)),
             dma((POST_SENDS,)),
             dma((8,)),
@@ -903,15 +828,22 @@
             dma((16,)),
             dma((8,)),
             dma((16,)),
-            dma((1,)),
+            dma((2,)),
             dma((16,)),
             dma((4,)),
         ],
         compiler_params=pltpu.CompilerParams(
-            collective_id=1, has_side_effects=True, vmem_limit_bytes=63 * 2**20
+            collective_id=0, has_side_effects=True, vmem_limit_bytes=63 * 2**20
         ),
-        name="row_backward",
+        name="whole_layer",
     )(*operands)
+
+
+def rope_constant(length):
+    frequency = np.power(np.float32(ROPE_BASE), -np.arange(0, HD, 2).astype(np.float32) / np.float32(HD)).astype(np.float32)
+    angles = (np.arange(length, dtype=np.float32)[:, None] * frequency[None, :]).astype(np.float32).astype(np.float64)
+    table = np.concatenate([np.cos(angles), np.sin(angles)], axis=1)
+    return jnp.asarray(np.concatenate([np.zeros((64, HD)), table], axis=0), WIDE)
 
 
 def finish_kernel(*refs):
@@ -923,15 +855,17 @@
     seq = lax.axis_index("seq")
     me = lax.axis_index("dp") * 16 + seq
     part = seq % 4
-    gains, vec = gain_ref[...], vec_ref[...]
+    gains = gain_ref[...]
     q_out, k_out, attn_out, mlp_out = small
     q_all = pltpu.roll(gains[:, :256], (256 - part * 64) % 256, axis=1)
     k_all = pltpu.roll(gains[:, 256:], (128 - part * 32) % 128, axis=1)
-    vec = pltpu.roll(vec, (1024 - me * 32) % 1024, axis=1)
+    turn = (256 - (me % 8) * 32) % 256
+    attn_all = pltpu.roll(jnp.broadcast_to(vec_ref[pl.ds(me // 8, 1), :], (8, 256)), turn, axis=1)
+    mlp_all = pltpu.roll(jnp.broadcast_to(vec_ref[pl.ds(4 + me // 8, 1), :], (8, 256)), turn, axis=1)
     q_out[...] = q_all[0:1, :64]
     k_out[...] = k_all[0:1, :32]
-    attn_out[...] = vec[0:1, :32]
-    mlp_out[...] = vec[1:2, :32]
+    attn_out[...] = attn_all[0:1, :32]
+    mlp_out[...] = mlp_all[0:1, :32]
 
 
 def finish(arrays, vec, gains):
@@ -1242,16 +1176,12 @@
     tokens, cotangent, w_query, w_key, w_value, w_out, q_gain, k_gain, attn_gain,
     w_gate, w_up, w_down, mlp_gain, doc_lengths, block_order,
 ):
-    cos, sine = rope_constants(1024)
+    rope = rope_constant(1024)
     q_gain_rows, k_gain_rows = q_gain.reshape(16, HD), k_gain.reshape(8, HD)
     own_tokens = tokens[:, 0]
-    att_tok, tok_nat, q_pair, kv_nat, hat, factors, lse = row_forward(
-        own_tokens, w_query, w_key, w_value, q_gain_rows, k_gain_rows, cos, sine, block_order, doc_lengths
-    )
-    layer_out, in_grad, g_query, g_key, g_value, g_out, vec, gains, g_gate, g_up, g_down = row_backward(
-        att_tok, own_tokens, cotangent[:, 0], attn_gain[None], mlp_gain[None], q_gain_rows, k_gain_rows, factors, lse,
-        tok_nat, q_pair, kv_nat, hat, cos, sine,
-        w_out, w_gate, w_up, w_down, w_query, w_key, w_value, block_order, doc_lengths,
+    layer_out, in_grad, g_query, g_key, g_value, g_out, vec, gains, g_gate, g_up, g_down = whole_layer(
+        own_tokens, cotangent[:, 0], attn_gain[None], mlp_gain[None], q_gain_rows, k_gain_rows,
+        rope, w_out, w_gate, w_up, w_down, w_query, w_key, w_value, block_order, doc_lengths,
     )
     (
         layer_out, in_grad, g_query, g_key, g_value, g_out, g_gate, g_up, g_down,

time: 209 us -> 198 us (0.947)
  the two profiles are of different devices: /device:TPU:0 before, /device:TPU:7 now
where the time goes in v4:
time: 198 us
  Pallas kernels  197 us (99%)
    pallas_call x1, Pallas kernels, whole_layer(): pl.pallas_call(layer_kernel, out_shape=(shape((128, width), LOW), shape((...  194 us

profile of v4, /device:TPU:7, one launch (start us, length us, event | category | flops | bytes accessed | tf_op | source)
XLA Modules:
  0.0 197.9 jit_solution(2633259748963727827)
XLA Ops:
  0.7 193.7 %whole_layer.1 = (bf16[128,1024]{1,0:T(8,128)(2,1)}, f32[128,1024]{1,0:T(8,128)}, f32[32,2048]{1,0:T(8,128)}, f32[32,1024]{1,0:T(8,128)}, f32[32,1024]{1,0:T(8,1...) custom-call(bf16[2,64,1024]{2,1,0:T(8,128)(2,1)} %bitcast.16, ...), custom_call_target="tpu_custom_call" | custom-call | tf_op jit(solution)/shard_map/whole_layer/pallas_call | solution.py:744
  194.4 3.3 %finish.1 = (bf16[128,1024]{1,0:T(8,128)(2,1)}, f32[128,1024]{1,0:T(8,128)}, f32[32,2048]{1,0:T(8,128)}, f32[32,1024]{1,0:T(8,128)}, f32[32,1024]{1,0:T(8,128)},...) custom-call(bf16[128,1024]{1,0:T(8,128)(2,1)} %get-tuple-element.37., ...), custom_call_target="tpu_custom_call" | custom-call | tf_op jit(solution)/shard_map/finish/pallas_call | solution.py:875

commit v5 on v4

--- a/solution.py
+++ b/solution.py
@@ -448,7 +448,6 @@
     mlp_sum = jnp.sum(cot * normal, axis=0, keepdims=True)
     for piece in range(4):
         vec_own[4 + piece : 5 + piece, :] = mlp_sum[:, piece * 256 : (piece + 1) * 256]
-    spread(down_own, down_all, dpl_sems, 12)
 
     for step in range(1, 9):
         group = (member + step) % 8
@@ -483,6 +482,7 @@
     for step in range(1, 8):
         other = (member + step) % 8
         post.send(vec_own, vec_all.at[member], vec_sems.at[member], (other // 4, z * 4 + other % 4))
+    spread(down_own, down_all, dpl_sems, 12)
     pass_diagonal(hid_all, hid_sems)
     pass_on(down_all, dpl_sems, "x")
     spread(proj_own, proj_all, proj_sems, 15)
@@ -499,7 +499,7 @@
     up_pre[:, :, :256] = jnp.zeros((8, TILE, 256), WIDE)
     down_part = wdown.at[pl.ds(0, 384)]
     for tile in range(7, -1, -1):
-        if tile == 4:
+        if tile == 1:
             pass_diagonal(down_all, dpl_sems)
             dealt(mix_all, mix_sems, 11)
             whole(down_all, dpl_sems, 12)
@@ -649,6 +649,21 @@
             (core != dp) | (other != seq),
         )
 
+    for slot, far in enumerate((along.far_inner, along.far_outer)):
+        for y in range(2):
+
+            @pl.when(along.inner)
+            def _():
+                arrived(spot, gu_transit.at[slot, y], gut_sems.at[slot, y], spare)
+                added = gu_transit[slot, y].astype(WIDE) + gu_part[aligned(y * 512 + far * 128, 128), :].astype(WIDE)
+                gu_transit[slot, y] = added.astype(LOW)
+
+            for piece in range(4):
+                post.send(
+                    gu_transit.at[slot, y, pl.ds(piece * 32, 32)], gu_land.at[1, member], gu_sems.at[1, member],
+                    (y, far * 4 + piece), along.inner,
+                )
+
     pass_diagonal(proj_all, proj_sems)
     dealt(att_all, attp_sems, 10)
     whole(proj_all, proj_sems, 15)
@@ -673,21 +688,6 @@
         grad_v.append(block[:, 384:])
     gradient = gradient + dot_nt(jnp.concatenate(grad_k, axis=1), wgate[:, 2048:])
     in_grad[...] = gradient + dot_nt(jnp.concatenate(grad_v, axis=1), wup[:, :1024])
-
-    for slot, far in enumerate((along.far_inner, along.far_outer)):
-        for y in range(2):
-
-            @pl.when(along.inner)
-            def _():
-                arrived(spot, gu_transit.at[slot, y], gut_sems.at[slot, y], spare)
-                added = gu_transit[slot, y].astype(WIDE) + gu_part[aligned(y * 512 + far * 128, 128), :].astype(WIDE)
-                gu_transit[slot, y] = added.astype(LOW)
-
-            for piece in range(4):
-                post.send(
-                    gu_transit.at[slot, y, pl.ds(piece * 32, 32)], gu_land.at[1, member], gu_sems.at[1, member],
-                    (y, far * 4 + piece), along.inner,
-                )
 
     for y in range(2):
         for micro in range(2):

time: 198 us -> 196 us (0.990)
  the two profiles are of different devices: /device:TPU:7 before, /device:TPU:0 now
where the time goes in v5:
time: 196 us
  Pallas kernels  195 us (99%)
    pallas_call x1, Pallas kernels, whole_layer(): pl.pallas_call(layer_kernel, out_shape=(shape((128, width), LOW), shape((...  192 us

profile of v5, /device:TPU:0, one launch (start us, length us, event | category | flops | bytes accessed | tf_op | source)
XLA Modules:
  0.0 196.3 jit_solution(17080999488915369989)
XLA Ops:
  0.7 192.1 %whole_layer.1 = (bf16[128,1024]{1,0:T(8,128)(2,1)}, f32[128,1024]{1,0:T(8,128)}, f32[32,2048]{1,0:T(8,128)}, f32[32,1024]{1,0:T(8,128)}, f32[32,1024]{1,0:T(8,1...) custom-call(bf16[2,64,1024]{2,1,0:T(8,128)(2,1)} %bitcast.16, ...), custom_call_target="tpu_custom_call" | custom-call | tf_op jit(solution)/shard_map/whole_layer/pallas_call | solution.py:744
  192.8 3.3 %finish.1 = (bf16[128,1024]{1,0:T(8,128)(2,1)}, f32[128,1024]{1,0:T(8,128)}, f32[32,2048]{1,0:T(8,128)}, f32[32,1024]{1,0:T(8,128)}, f32[32,1024]{1,0:T(8,128)},...) custom-call(bf16[128,1024]{1,0:T(8,128)(2,1)} %get-tuple-element.37., ...), custom_call_target="tpu_custom_call" | custom-call | tf_op jit(solution)/shard_map/finish/pallas_call | solution.py:875
